TPU v7x, 32 devices: a whole 2x2x4 slice. The times are simulated.
32 devices in a mesh: group: 2 (over x), latent: 16 (over z, y, core).
Axes of the slice: x: 2, y: 2, z: 4, core: 2. Of those that a mesh axis runs over, the one named last changes fastest.
Arguments:
- rows_in: bfloat16 [64, 3584], P(('group', 'latent')), parts along dimension 0, may hold values from -6 to 6
- active_ids: int32 [64, 128], P('group'), parts along dimension 0, may hold values from 0 to 2047, all different within a row
- encoder_weight: bfloat16 [7168, 2048], P('group', 'latent'), parts along dimension 0, may hold values from -0.09375 to 0.09375
- encoder_bias: float32 [4096], P(('group', 'latent')), parts along dimension 0, may hold values from -3 to 3
- threshold: float32 [4096], P(('group', 'latent')), parts along dimension 0, may hold values from 0.25 to 2
- decoder_weight: bfloat16 [4096, 3584], P(('group', 'latent')), parts along dimension 0, may hold values from -0.5 to 0.5
- decoder_bias: float32 [7168], P('group'), parts along dimension 0, may hold values from -3 to 3
Outputs:
- grad_encoder: bfloat16 [7168, 2048], P('group', 'latent'), parts along dimension 0
- grad_encoder_bias: float32 [4096], P(('group', 'latent')), parts along dimension 0
- grad_threshold: float32 [4096], P(('group', 'latent')), parts along dimension 0
- grad_decoder: bfloat16 [4096, 3584], P(('group', 'latent')), parts along dimension 0
- grad_decoder_bias: float32 [7168], P('group'), parts along dimension 0
There are 2 independent parts, one for each index of `group`. A program takes and returns all parts, laid end to end along the dimension named above; each array names one. Nothing has to cross between parts.
Inputs may be any that keep to these rules, and one draw needn't show every extreme that they name: `active_ids`: each row names 128 different latents; every latent is named by some row.
All inputs are finite; a program needn't handle non-finite values.
Results may differ from a plain program's by a relative error of at most 0.0069.
Values may be sent and summed in bfloat16 or wider, within the bound.
No kernel may reach another device: no remote copies, remote signals or barrier semaphores. Data moves between devices by JAX's collectives and lax.ppermute only.
A program may use at most 64 MiB of HBM per device.

v0:
```python
import math

import jax
import jax.numpy as jnp
from jax import lax
from jax.sharding import PartitionSpec as P

EPSILON = 0.5
SPARSITY = 0.5


def on_device(
    rows_in, active_ids, encoder_weight, encoder_bias, threshold, decoder_weight, decoder_bias
):
    local_width = encoder_weight.shape[1]
    offset = lax.axis_index("latent") * local_width
    gathered = lax.all_gather(rows_in, "latent", axis=0, tiled=True)
    total_rows = gathered.shape[0]
    centered = (gathered.astype(jnp.float32) - decoder_bias).astype(jnp.bfloat16)
    preact = jnp.dot(centered, encoder_weight, preferred_element_type=jnp.float32) + encoder_bias
    local_index = active_ids - offset
    local_index = jnp.where(
        (local_index >= 0) & (local_index < local_width), local_index, local_width
    )
    row_index = jnp.broadcast_to(jnp.arange(total_rows, dtype=jnp.int32)[:, None], active_ids.shape)
    gating = (
        jnp.zeros((total_rows, local_width), jnp.float32)
        .at[row_index, local_index]
        .set(1.0, mode="drop")
    )
    latent_codes = (preact * gating).astype(jnp.bfloat16)
    partial_sum = jnp.dot(latent_codes, decoder_weight, preferred_element_type=jnp.float32)
    rebuilt = lax.psum(partial_sum, "latent") + decoder_bias
    errors = (rebuilt - gathered.astype(jnp.float32)).astype(jnp.bfloat16)
    code_grad = lax.dot_general(
        errors, decoder_weight, (((1,), (1,)), ((), ())), preferred_element_type=jnp.float32
    )
    distance = (preact - threshold) / EPSILON
    kernel = jnp.exp(-0.5 * distance * distance) / (EPSILON * math.sqrt(2.0 * math.pi))
    grad_threshold = jnp.sum(-threshold * code_grad * kernel - SPARSITY * kernel, axis=0)
    preact_grad = code_grad * gating
    grad_encoder_bias = jnp.sum(preact_grad, axis=0)
    preact_low = preact_grad.astype(jnp.bfloat16)
    grad_encoder = lax.dot_general(
        centered, preact_low, (((0,), (0,)), ((), ())), preferred_element_type=jnp.float32
    ).astype(jnp.bfloat16)
    grad_decoder = lax.dot_general(
        latent_codes, errors, (((0,), (0,)), ((), ())), preferred_element_type=jnp.float32
    ).astype(jnp.bfloat16)
    encoder_part = jnp.dot(
        encoder_weight,
        grad_encoder_bias,
        preferred_element_type=jnp.float32,
        precision=lax.Precision.HIGHEST,
    )
    encoder_total = lax.psum(encoder_part, "latent")
    grad_decoder_bias = jnp.sum(errors, axis=0, dtype=jnp.float32) - encoder_total
    return (grad_encoder, grad_encoder_bias, grad_threshold, grad_decoder, grad_decoder_bias)


def solution(mesh):
    placed = (
        P(("group", "latent"), None),
        P("group", None),
        P("group", "latent"),
        P(("group", "latent")),
        P(("group", "latent")),
        P(("group", "latent"), None),
        P("group"),
    )
    return jax.shard_map(
        on_device,
        mesh=mesh,
        in_specs=placed,
        out_specs=(
            P("group", "latent"),
            P(("group", "latent")),
            P(("group", "latent")),
            P(("group", "latent"), None),
            P("group"),
        ),
        check_vma=False,
    )
```

profile of v0, /device:TPU:0, one launch (start us, length us, event | category | flops | bytes accessed | tf_op | source)
XLA Modules:
  0.0 210.7 jit_solution(14200854081797732922)
XLA Ops:
  7.2 0.0 copy-start
  7.2 0.0 copy-start.2
  7.2 0.0 copy-start.1
  7.2 0.0 copy-start.4
  7.2 0.0 all-reduce.2.cloned.1.call-start
  7.3 0.8 fusion
  8.1 0.7 and_reduce_fusion
  8.8 0.7 multiply_reduce_fusion
  9.6 23.9 %all-gather = bf16[16,2,3584]{2,1,0:T(2,128)(2,1)S(1)} all-gather(bf16[1,2,3584]{2,1,0:T(2,128)(2,1)} %bitcast.27), channel_id=1, replica_groups=mesh['group'=2,'latent'=16] {'latent'}, dimensions={0}, use_global_device_ids=true | all-gather | bytes 243712 | tf_op jit(solution)/shard_map/all_gather | solution.py:17
  33.5 0.1 reshape.38
  33.6 15.5 %scatter_custom_fusion = f32[4096]{0:T(1024)S(1)} fusion(s32[4096]{0:T(1024)S(1)} %select_bitcast_fusion, f32[4096]{0:T(1024)S(1)} %broadcast.49, f32[]{:T(128)} %constant.9.clone.1), kind=kCustom, calls=%fused_computation.18 | custom fusion | bytes 16388
  49.1 0.0 copy-done.2
  49.2 0.0 copy-done.1
  49.2 0.0 copy-done.4
  49.2 0.3 fusion.1
  49.4 0.0 copy-done
  49.5 0.0 copy-start.5
  49.5 1.0 fusion.7
  50.5 0.0 all-reduce.2.cloned.1.call-update
  50.5 0.0 copy-done.5
  50.5 87.3 %all-reduce.2.cloned.1.call-done = f32[32,3584]{1,0:T(8,128)} async-done(((f32[32,3584]{1,0:T(8,128)}), f32[32,3584]{1,0:T(8,128)}) %all-reduce.2.cloned.1.call-update) | async-done | bytes 458768 | tf_op jit(solution)/shard_map/psum | solution.py:33
  137.8 1.1 convert_reduce_fusion
  138.9 1.3 convolution_convert_fusion
  140.3 0.9 subtract_reduce_fusion
  141.2 0.0 copy-start.3
  141.2 0.8 convolution_reduce_fusion
  142.1 59.8 %psum.15 = f32[3584]{0:T(1024)S(1)} all-reduce(f32[3584]{0:T(1024)S(1)} %convolution_reduce_fusion), channel_id=1, replica_groups=mesh['group'=2,'latent'=16] {'latent'}, use_global_device_ids=true, to_apply=%region_5.6 | all-reduce | flops 3584 | bytes 28672 | tf_op jit(solution)/shard_map/psum | solution.py:56
  201.9 1.4 convolution_convert_fusion.1
  203.3 0.0 copy-done.3
  203.3 0.6 sub.39
  (4 shorter events, 0.0 us)
Async XLA Ops:
  7.2 42.3 %copy-start = (bf16[128,3584]{1,0:T(8,128)(2,1)S(1)}, bf16[128,3584]{1,0:T(8,128)(2,1)}, u32[]{:S(2)}) copy-start(bf16[128,3584]{1,0:T(8,128)(2,1)} %param.12) | copy-start | bytes 2752516
  7.2 42.0 %copy-start.2 = (f32[3584]{0:T(1024)S(1)}, f32[3584]{0:T(1024)}, u32[]{:S(2)}) copy-start(f32[3584]{0:T(1024)} %param.13) | copy-start | bytes 43012
  7.2 42.0 %copy-start.1 = (bf16[3584,128]{1,0:T(8,128)(2,1)S(1)}, bf16[3584,128]{1,0:T(8,128)(2,1)}, u32[]{:S(2)}) copy-start(bf16[3584,128]{1,0:T(8,128)(2,1)} %param.9) | copy-start | bytes 2752516
  7.2 42.0 %copy-start.4 = (f32[128]{0:T(128)S(1)}, f32[128]{0:T(128)}, u32[]{:S(2)}) copy-start(f32[128]{0:T(128)} %param.10) | copy-start | bytes 1540
  7.2 130.6 %all-reduce.2.cloned.1.call-start = ((), (), s32[]{:S(2)}) async-start(), calls=%async_computation | async-start | bytes 917504 | tf_op jit(solution)/shard_map/psum | solution.py:33
  49.5 1.1 copy-start.5
  141.2 62.0 %copy-start.3 = (f32[128]{0:T(128)}, f32[128]{0:T(128)S(1)}, u32[]{:S(2)}) copy-start(f32[128]{0:T(128)S(1)} %get-tuple-element.6) | copy-start | bytes 1540
Sparse Core Ops, SparseCore 0:
  50.6 87.1 all-reduce.1
where the time goes:
time: 211 us
  waiting for transfers between devices  87.3 us (41%)
  blocking collectives  83.8 us (40%)
  local copies, waits for them, and re-layouts  15.6 us (7%)
  between operations  14.2 us (7%)
  matrix products  5.75 us (3%)
  other arithmetic  4.03 us (2%)
    psum x1, waiting for transfers between devices, on_device(): rebuilt = lax.psum(partial_sum, 'latent') + decoder_bias  87.3 us
    psum x1, blocking collectives, on_device(): encoder_total = lax.psum(encoder_part, 'latent')  59.8 us
    all_gather x1, blocking collectives, on_device(): gathered = lax.all_gather(rows_in, 'latent', axis=0, tiled=True)  23.9 us
    unnamed x14, local copies, waits for them, and re-layouts  15.6 us
  transfers between devices with their start and end apart: 1, of which 1 were waited for; matrix products, arithmetic and copies ran while one was open for 0% of the time, Pallas kernels for 0%

commit v1 on v0

v1 whole, which is shorter than its diff:
```python
import math

import jax
import jax.numpy as jnp
from jax import lax
from jax.sharding import PartitionSpec as P

EPSILON = 0.5
SPARSITY = 0.5
F32 = jnp.float32
BF16 = jnp.bfloat16


def opened(ids, offset, width):
    latent = offset + lax.broadcasted_iota(jnp.int32, (1, 1, width), 2)
    return jnp.any(ids[:, :, None] == latent, axis=1)


def on_device(
    count, rows_in, active_ids, encoder_weight, encoder_bias, threshold, decoder_weight, decoder_bias
):
    width = encoder_weight.shape[1]
    me = lax.axis_index("latent")
    core = me & 1

    def swap(array, bit):
        return lax.ppermute(array, "latent", [(i, i ^ bit) for i in range(count)])

    hops = []
    bit = 2
    while bit < count:
        hops.append(bit)
        bit *= 2

    encoder_other = swap(encoder_weight, 1)
    decoder_other = swap(decoder_weight, 1)
    bias_other = swap(encoder_bias, 1)

    per_device, depth = rows_in.shape
    block = rows_in[None]
    for bit in hops:
        other = swap(block, bit)
        low = jnp.concatenate([block, other], axis=0)
        high = jnp.concatenate([other, block], axis=0)
        block = jnp.where((me & bit) == 0, low, high)
    half_rows = block.shape[0] * per_device
    rows = block.reshape(half_rows, depth)

    ids = active_ids.reshape(half_rows // per_device, 2, per_device, active_ids.shape[1])
    ids_mine = lax.dynamic_index_in_dim(ids, core, 1, keepdims=False).reshape(half_rows, -1)
    ids_other = lax.dynamic_index_in_dim(ids, 1 - core, 1, keepdims=False).reshape(half_rows, -1)

    def center(part):
        return (part.astype(F32) - decoder_bias).astype(BF16)

    def dot(a, b):
        return jnp.dot(a, b, preferred_element_type=F32)

    def dot_last(a, b):
        return lax.dot_general(a, b, (((1,), (1,)), ((), ())), preferred_element_type=F32)

    def dot_rows(a, b):
        return lax.dot_general(a, b, (((0,), (0,)), ((), ())), preferred_element_type=F32)

    centered = center(rows)
    gate_mine = opened(ids_mine, me * width, width)
    gate_other = opened(ids_mine, (me ^ 1) * width, width)
    preact_mine = dot(centered, encoder_weight) + encoder_bias
    preact_other = dot(centered, encoder_other) + bias_other
    codes_mine = jnp.where(gate_mine, preact_mine, 0.0).astype(BF16)
    codes_other = jnp.where(gate_other, preact_other, 0.0).astype(BF16)
    total = dot(codes_mine, decoder_weight) + dot(codes_other, decoder_other)
    for bit in hops:
        low = lax.optimization_barrier(total.astype(BF16))
        total = low.astype(F32) + swap(low, bit).astype(F32)
    errors = lax.optimization_barrier((total + decoder_bias - rows.astype(F32)).astype(BF16))

    grad_mine = jnp.sum(jnp.where(gate_mine, dot_last(errors, decoder_weight), 0.0), axis=0)
    grad_other = jnp.sum(jnp.where(gate_other, dot_last(errors, decoder_other), 0.0), axis=0)

    def product(weight, vector):
        upper = vector.astype(BF16)
        lower = (vector - upper.astype(F32)).astype(BF16)
        both = jnp.stack([upper, lower])
        return dot_last(both, weight)

    part = product(encoder_weight, grad_mine) + product(encoder_other, grad_other)
    part = part[0] + part[1]
    for bit in hops:
        part = part + swap(part, bit)
    part = jnp.sum(errors, axis=0, dtype=F32) - part
    grad_decoder_bias = part + swap(part, 1)

    rows_other = swap(rows, 1)
    errors_other = swap(errors, 1)
    centered_other = center(rows_other)
    gate_rest = opened(ids_other, me * width, width)
    preact_rest = dot(centered_other, encoder_weight) + encoder_bias
    preact = jnp.concatenate([preact_mine, preact_rest])
    gate = jnp.concatenate([gate_mine, gate_rest])
    every_error = jnp.concatenate([errors, errors_other])
    every_centered = jnp.concatenate([centered, centered_other])
    codes = jnp.where(gate, preact, 0.0).astype(BF16)
    code_grad = dot_last(every_error, decoder_weight)
    distance = (preact - threshold) / EPSILON
    kernel = jnp.exp(-0.5 * distance * distance) / (EPSILON * math.sqrt(2.0 * math.pi))
    grad_threshold = jnp.sum(-threshold * code_grad * kernel - SPARSITY * kernel, axis=0)
    preact_grad = jnp.where(gate, code_grad, 0.0)
    grad_encoder_bias = jnp.sum(preact_grad, axis=0)
    grad_encoder = dot_rows(every_centered, preact_grad.astype(BF16)).astype(BF16)
    grad_decoder = dot_rows(codes, every_error).astype(BF16)
    return (grad_encoder, grad_encoder_bias, grad_threshold, grad_decoder, grad_decoder_bias)


def solution(mesh):
    count = mesh.shape["latent"]

    def body(*args):
        return on_device(count, *args)

    placed = (
        P(("group", "latent"), None),
        P("group", None),
        P("group", "latent"),
        P(("group", "latent")),
        P(("group", "latent")),
        P(("group", "latent"), None),
        P("group"),
    )
    return jax.shard_map(
        body,
        mesh=mesh,
        in_specs=placed,
        out_specs=(
            P("group", "latent"),
            P(("group", "latent")),
            P(("group", "latent")),
            P(("group", "latent"), None),
            P("group"),
        ),
        check_vma=False,
    )
```

time: 211 us -> 57.4 us (0.27)
  blocking collectives: 83.8 us -> 0 us
  waiting for transfers between devices: 87.3 us -> 19 us
  starting transfers between devices: 0.04 us -> 24.2 us
  local copies, waits for them, and re-layouts: 15.6 us -> 0.79 us
  between operations: 14.2 us -> 0.82 us
  matrix products: 5.75 us -> 8.52 us
    psum x1 -> x0, waiting for transfers between devices: 87.3 us -> none  [on_device(): rebuilt = lax.psum(partial_sum, 'latent') + decoder_bias]
    psum x1 -> x0, blocking collectives: 59.8 us -> none  [on_device(): encoder_total = lax.psum(encoder_part, 'latent')]
    ppermute x0 -> x15, starting transfers between devices: none -> 24.2 us  [swap(): return lax.ppermute(array, 'latent', [(i, i ^ bit) for i in range(count)])]
    all_gather x1 -> x0, blocking collectives: 23.9 us -> none  [on_device(): gathered = lax.all_gather(rows_in, 'latent', axis=0, tiled=True)]
    ppermute x0 -> x15, waiting for transfers between devices: none -> 19 us  [swap(): return lax.ppermute(array, 'latent', [(i, i ^ bit) for i in range(count)])]
    unnamed x14 -> x10, local copies, waits for them, and re-layouts: 15.6 us -> 0.03 us
    dot_general x6 -> x11, matrix products: 5.75 us -> 8.52 us  [the longest x5 3.47 us: dot_last(): lax.dot_general(a, b, (((1,), (1,)), ((), ())), preferred_element_type=F32)]
  transfers between devices with their start and end apart: 1 -> 15, of which waited for: 1 -> 10; matrix products, arithmetic and copies ran while one was open for 0% -> 8% of each run, Pallas kernels for 0% -> 0%
where the time goes in v1:
time: 57.4 us; the launch traced here: 57 us
  starting transfers between devices  24.2 us (42%)
  waiting for transfers between devices  19 us (33%)
  matrix products  8.52 us (15%)
  other arithmetic  3.6 us (6%)
  between operations  0.82 us (1%)
  local copies, waits for them, and re-layouts  0.79 us (1%)
    ppermute x15, starting transfers between devices, swap(): return lax.ppermute(array, 'latent', [(i, i ^ bit) for i in range(count)])  24.2 us
    ppermute x15, waiting for transfers between devices, swap(): return lax.ppermute(array, 'latent', [(i, i ^ bit) for i in range(count)])  19 us
    dot_general x5, matrix products, dot_last(): lax.dot_general(a, b, (((1,), (1,)), ((), ())), preferred_element_type=F32)  3.47 us
    dot_general x2, matrix products, dot_rows(): lax.dot_general(a, b, (((0,), (0,)), ((), ())), preferred_element_type=F32)  2.72 us
    dot_general x4, matrix products, dot(): return jnp.dot(a, b, preferred_element_type=F32)  2.32 us
    select_n x3, other arithmetic, on_device(): block = jnp.where(me & bit == 0, low, high)  1.23 us
  transfers between devices with their start and end apart: 15, of which 10 were waited for; matrix products, arithmetic and copies ran while one was open for 8% of the time, Pallas kernels for 0%

profile of v1, /device:TPU:0, one launch (start us, length us, event | category | flops | bytes accessed | tf_op | source)
XLA Modules:
  0.0 57.0 jit_solution(8809553837859086923)
XLA Ops:
  0.7 3.0 %collective-permute-start = (bf16[1,2,3584]{2,1,0:T(2,128)(2,1)}, bf16[1,2,3584]{2,1,0:T(2,128)(2,1)S(1)}, u32[]{:S(2)}, u32[]{:S(2)}) collective-permute-start(bf16[1,2,3584]{2,1,0:T(2,128)(2,1)} %bitcast.36), channel_id=1, source_target_pairs={{0,2},{1,3},{2,0},{3,1},{4,6},{5,7},{6,4},{7,5},{8,10},{9,11},{10,... | collective-permute-start | bytes 43016 | tf_op jit(solution)/shard_map/ppermute | solution.py:27
  3.7 0.5 collective-permute-start.6
  4.2 0.0 collective-permute-start.5
  4.2 0.7 %constant_dynamic-slice_fusion = (s32[8,1,2,128]{3,2,1,0:T(2,128)S(1)}, s32[8,1,2,128]{3,2,1,0:T(2,128)S(1)}) fusion(s32[8,2,2,128]{3,2,1,0:T(2,128)} %bitcast.35, s32[]{:T(128)S(6)} %select_n.63, s32[]{:T(128)S(6)} %select_n.62), kind=kLoop, calls=%fused_computation.64 | loop fusion | bytes 32776 | tf_op jit(solution)/shard_map/jit(dynamic_index_in_dim)/dynamic_slice | solution.py:51
  4.9 0.7 %collective-permute-done = bf16[1,2,3584]{2,1,0:T(2,128)(2,1)S(1)} collective-permute-done((bf16[1,2,3584]{2,1,0:T(2,128)(2,1)}, bf16[1,2,3584]{2,1,0:T(2,128)(2,1)S(1)}, u32[]{:S(2)}, u32[]{:S(2)}) %collective-permute-start) | collective-permute-done | bytes 14368 | tf_op jit(solution)/shard_map/ppermute | solution.py:27
  5.6 0.8 %broadcast_select_fusion.2 = bf16[2,2,3584]{2,1,0:T(2,128)(2,1)S(1)} fusion(pred[]{:T(512)S(6)} %eq.50, bf16[1,2,3584]{2,1,0:T(2,128)(2,1)S(1)} %collective-permute-done, bf16[1,2,3584]{2,1,0:T(2,128)(2,1)} %bitcast.37), kind=kLoop, calls=%fused_computation.32 | loop fusion | flops 43008 | bytes 57345 | tf_op jit(solution)/shard_map/jit(_where)/select_n | solution.py:45
  6.4 2.1 %collective-permute-start.1 = (bf16[2,2,3584]{2,1,0:T(2,128)(2,1)S(1)}, bf16[2,2,3584]{2,1,0:T(2,128)(2,1)S(1)}, u32[]{:S(2)}, u32[]{:S(2)}) collective-permute-start(bf16[2,2,3584]{2,1,0:T(2,128)(2,1)S(1)} %broadcast_select_fusion.2), channel_id=1, source_target_pairs={{0,4},{1,5},{2,6},{3,7},{4,0},{5,1},{6,2},{7,3},{8,12},{9,13},{10,... | collective-permute-start | bytes 86024 | tf_op jit(solution)/shard_map/ppermute | solution.py:27
  8.6 1.8 %collective-permute-done.1 = bf16[2,2,3584]{2,1,0:T(2,128)(2,1)S(1)} collective-permute-done((bf16[2,2,3584]{2,1,0:T(2,128)(2,1)S(1)}, bf16[2,2,3584]{2,1,0:T(2,128)(2,1)S(1)}, u32[]{:S(2)}, u32[]{:S(2)}) %collective-permute-start.1) | collective-permute-done | bytes 28704 | tf_op jit(solution)/shard_map/ppermute | solution.py:27
  10.4 0.1 broadcast_select_fusion.1
  10.6 0.0 copy-start
  10.6 3.1 %collective-permute-start.2 = (bf16[4,2,3584]{2,1,0:T(2,128)(2,1)S(1)}, bf16[4,2,3584]{2,1,0:T(2,128)(2,1)S(1)}, u32[]{:S(2)}, u32[]{:S(2)}) collective-permute-start(bf16[4,2,3584]{2,1,0:T(2,128)(2,1)S(1)} %broadcast_select_fusion.1), channel_id=1, source_target_pairs={{0,8},{1,9},{2,10},{3,11},{4,12},{5,13},{6,14},{7,15},{8,0},{9,1},... | collective-permute-start | bytes 172040 | tf_op jit(solution)/shard_map/ppermute | solution.py:27
  13.7 0.7 %compare_reduce_fusion = (pred[16,128]{1,0:T(8,128)(4,1)S(1)}, pred[16,128]{1,0:T(8,128)(4,1)S(1)}, pred[16,128]{1,0:T(8,128)(4,1)S(1)}) fusion(s32[128]{0:T(128)S(1)} %iota_add_fusion, s32[16,128]{1,0:T(8,128)S(1)} %bitcast.34, s32[128]{0:T(128)S(1)} %iota_add_fusion.1, s32[16,128]{1,0:T(8,128)S(1)} %bitcast.33), kind=kLoop, calls=%fused_computation.14 | loop fusion | flops 1566720 | bytes 23552 | tf_op jit(solution)/shard_map/reduce_or | solution.py:16
  14.4 1.4 %collective-permute-done.2 = bf16[4,2,3584]{2,1,0:T(2,128)(2,1)S(1)} collective-permute-done((bf16[4,2,3584]{2,1,0:T(2,128)(2,1)S(1)}, bf16[4,2,3584]{2,1,0:T(2,128)(2,1)S(1)}, u32[]{:S(2)}, u32[]{:S(2)}) %collective-permute-start.2) | collective-permute-done | bytes 57376 | tf_op jit(solution)/shard_map/ppermute | solution.py:27
  15.8 0.3 broadcast_select_fusion
  16.1 0.7 %fusion.5 = bf16[16,3584]{1,0:T(8,128)(2,1)S(1)} fusion(bf16[16,3584]{1,0:T(8,128)(2,1)S(1)} %select_n.61, f32[3584]{0:T(1024)} %param.13), kind=kLoop, calls=%fused_computation.19 | loop fusion | flops 172032 | bytes 243712 | tf_op jit(solution)/shard_map/convert_element_type | solution.py:54
  16.9 0.2 convolution_add_fusion.4
  17.1 0.2 fusion.14
  17.4 0.0 collective-permute-done.6
  17.4 0.0 copy-start.2
  17.4 1.6 %fusion = bf16[16,3584]{1,0:T(8,128)(2,1)S(1)} fusion(f32[16,3584]{1,0:T(8,128)S(1)} %fusion.14, bf16[128,3584]{1,0:T(8,128)(2,1)S(1)} %collective-permute-done.6, pred[16,128]{1,0:T(8,128)(4,1)S(1)} %get-tuple-element.7, bf16[16,3584]{1,0:T(8,128)(2,1)S(1)} %fusion.5, bf16[3584,128]{1,0:T(8,128)(2,1)} %collective-permute-done.4, ...), kind=kOutput, calls=%fused_computation.3 | convolution fusion | flops 29480960 | bytes 2296320 | tf_op jit(solution)/shard_map/dot_general | solution.py:57
  19.0 1.9 %collective-permute-start.7 = (bf16[16,3584]{1,0:T(8,128)(2,1)S(1)}, bf16[16,3584]{1,0:T(8,128)(2,1)S(1)}, u32[]{:S(2)}, u32[]{:S(2)}) collective-permute-start(bf16[16,3584]{1,0:T(8,128)(2,1)S(1)} %fusion), channel_id=1, source_target_pairs={{0,2},{1,3},{2,0},{3,1},{4,6},{5,7},{6,4},{7,5},{8,10},{9,11},{10,... | collective-permute-start | bytes 344072 | tf_op jit(solution)/shard_map/ppermute | solution.py:27
  21.0 2.9 %collective-permute-done.7 = bf16[16,3584]{1,0:T(8,128)(2,1)S(1)} collective-permute-done((bf16[16,3584]{1,0:T(8,128)(2,1)S(1)}, bf16[16,3584]{1,0:T(8,128)(2,1)S(1)}, u32[]{:S(2)}, u32[]{:S(2)}) %collective-permute-start.7) | collective-permute-done | bytes 114720 | tf_op jit(solution)/shard_map/ppermute | solution.py:27
  23.9 2.0 %collective-permute-start.8 = (bf16[16,3584]{1,0:T(8,128)(2,1)S(1)}, bf16[16,3584]{1,0:T(8,128)(2,1)S(1)}, u32[]{:S(2)}, u32[]{:S(2)}) collective-permute-start(bf16[16,3584]{1,0:T(8,128)(2,1)S(1)} %add_convert_fusion.1), channel_id=1, source_target_pairs={{0,4},{1,5},{2,6},{3,7},{4,0},{5,1},{6,2},{7,3},{8,12},{9,13},{10,... | collective-permute-start | bytes 344072 | tf_op jit(solution)/shard_map/ppermute | solution.py:27
  25.9 0.0 collective-permute-start.3
  25.9 2.9 %collective-permute-done.8 = bf16[16,3584]{1,0:T(8,128)(2,1)S(1)} collective-permute-done((bf16[16,3584]{1,0:T(8,128)(2,1)S(1)}, bf16[16,3584]{1,0:T(8,128)(2,1)S(1)}, u32[]{:S(2)}, u32[]{:S(2)}) %collective-permute-start.8) | collective-permute-done | bytes 114720 | tf_op jit(solution)/shard_map/ppermute | solution.py:27
  28.8 4.3 %collective-permute-start.9 = (bf16[16,3584]{1,0:T(8,128)(2,1)S(1)}, bf16[16,3584]{1,0:T(8,128)(2,1)S(1)}, u32[]{:S(2)}, u32[]{:S(2)}) collective-permute-start(bf16[16,3584]{1,0:T(8,128)(2,1)S(1)} %add_convert_fusion), channel_id=1, source_target_pairs={{0,8},{1,9},{2,10},{3,11},{4,12},{5,13},{6,14},{7,15},{8,0},{9,1},... | collective-permute-start | bytes 344072 | tf_op jit(solution)/shard_map/ppermute | solution.py:27
  33.1 0.0 collective-permute-done.3
  33.1 2.8 %collective-permute-done.9 = bf16[16,3584]{1,0:T(8,128)(2,1)S(1)} collective-permute-done((bf16[16,3584]{1,0:T(8,128)(2,1)S(1)}, bf16[16,3584]{1,0:T(8,128)(2,1)S(1)}, u32[]{:S(2)}, u32[]{:S(2)}) %collective-permute-start.9) | collective-permute-done | bytes 114720 | tf_op jit(solution)/shard_map/ppermute | solution.py:27
  35.9 0.1 fusion.6
  35.9 0.3 fusion.3
  36.3 0.3 fusion.4
  36.7 0.0 copy-start.4
  36.7 0.3 fusion.18
  37.0 1.5 %convolution_add_fusion.1 = f32[2,3584]{1,0:T(2,128)S(1)} fusion(f32[2,3584]{1,0:T(2,128)S(1)} %fusion.18, bf16[3584,128]{1,0:T(8,128)(2,1)} %collective-permute-done.4, bf16[1,128]{1,0:T(2,128)(2,1)S(1)} %fusion.25, bf16[1,128]{1,0:T(2,128)(2,1)S(1)} %bitcast_convert_fusion), kind=kOutput, calls=%fused_computation.4 | convolution fusion | flops 1843200 | bytes 975360 | tf_op jit(solution)/shard_map/dot_general | solution.py:60
  38.6 0.1 fusion.11
  38.6 1.6 %collective-permute-start.11 = (f32[3584]{0:T(1024)S(1)}, f32[3584]{0:T(1024)S(1)}, u32[]{:S(2)}, u32[]{:S(2)}) collective-permute-start(f32[3584]{0:T(1024)S(1)} %fusion.11), channel_id=1, source_target_pairs={{0,2},{1,3},{2,0},{3,1},{4,6},{5,7},{6,4},{7,5},{8,10},{9,11},{10,... | collective-permute-start | bytes 43016 | tf_op jit(solution)/shard_map/ppermute | solution.py:27
  40.2 2.2 %collective-permute-done.11 = f32[3584]{0:T(1024)S(1)} collective-permute-done((f32[3584]{0:T(1024)S(1)}, f32[3584]{0:T(1024)S(1)}, u32[]{:S(2)}, u32[]{:S(2)}) %collective-permute-start.11) | collective-permute-done | bytes 14368 | tf_op jit(solution)/shard_map/ppermute | solution.py:27
  42.5 2.2 %collective-permute-start.12 = (f32[3584]{0:T(1024)S(1)}, f32[3584]{0:T(1024)S(1)}, u32[]{:S(2)}, u32[]{:S(2)}) collective-permute-start(f32[3584]{0:T(1024)S(1)} %add.112), channel_id=1, source_target_pairs={{0,4},{1,5},{2,6},{3,7},{4,0},{5,1},{6,2},{7,3},{8,12},{9,13},{10,... | collective-permute-start | bytes 43016 | tf_op jit(solution)/shard_map/ppermute | solution.py:27
  44.7 1.7 %collective-permute-done.12 = f32[3584]{0:T(1024)S(1)} collective-permute-done((f32[3584]{0:T(1024)S(1)}, f32[3584]{0:T(1024)S(1)}, u32[]{:S(2)}, u32[]{:S(2)}) %collective-permute-start.12) | collective-permute-done | bytes 14368 | tf_op jit(solution)/shard_map/ppermute | solution.py:27
  46.4 3.4 %collective-permute-start.13 = (f32[3584]{0:T(1024)S(1)}, f32[3584]{0:T(1024)S(1)}, u32[]{:S(2)}, u32[]{:S(2)}) collective-permute-start(f32[3584]{0:T(1024)S(1)} %add.113), channel_id=1, source_target_pairs={{0,8},{1,9},{2,10},{3,11},{4,12},{5,13},{6,14},{7,15},{8,0},{9,1},... | collective-permute-start | bytes 43016 | tf_op jit(solution)/shard_map/ppermute | solution.py:27
  49.8 0.1 collective-permute-start.10
  49.9 1.6 %collective-permute-done.13 = f32[3584]{0:T(1024)S(1)} collective-permute-done((f32[3584]{0:T(1024)S(1)}, f32[3584]{0:T(1024)S(1)}, u32[]{:S(2)}, u32[]{:S(2)}) %collective-permute-start.13) | collective-permute-done | bytes 14368 | tf_op jit(solution)/shard_map/ppermute | solution.py:27
  51.5 0.2 convolution_add_fusion.2
  51.7 0.9 %collective-permute-done.14 = f32[3584]{0:T(1024)S(1)} collective-permute-done((f32[3584]{0:T(1024)S(1)}, f32[3584]{0:T(1024)S(1)}, u32[]{:S(2)}, u32[]{:S(2)}) %collective-permute-start.14) | collective-permute-done | bytes 14368 | tf_op jit(solution)/shard_map/ppermute | solution.py:27
  52.7 0.6 %add.115 = f32[3584]{0:T(1024)} add(f32[3584]{0:T(1024)S(1)} %add_subtract_fusion, f32[3584]{0:T(1024)S(1)} %collective-permute-done.14) | non-fusion elementwise | flops 3584 | bytes 43008 | tf_op jit(solution)/shard_map/add | solution.py:92
  53.3 0.9 %subtract_reduce_fusion = (f32[128]{0:T(128)}, f32[128]{0:T(128)}, bf16[32,128]{1,0:T(8,128)(2,1)S(1)}) fusion(f32[16,128]{1,0:T(8,128)S(1)} %convolution_add_fusion.2, f32[16,128]{1,0:T(8,128)S(1)} %convolution_add_fusion.4, f32[128]{0:T(128)S(1)} %copy-done.4, f32[128]{0:T(128)S(1)} %neg.3, pred[16,128]{1,0:T(8,128)(4,1)S(1)} %get-tuple-element.9, ...), kind=kOutput, calls=%fused_computation.36 | convolution fusion | flops 29880064 | bytes 1177600 | tf_op jit(solution)/shard_map/dot_general | solution.py:60
  54.2 1.4 %convolution_convert_fusion.1 = bf16[3584,128]{1,0:T(8,128)(2,1)} fusion(bf16[16,3584]{1,0:T(8,128)(2,1)S(1)} %get-tuple-element.11, bf16[16,3584]{1,0:T(8,128)(2,1)S(1)} %fusion.5, bf16[32,128]{1,0:T(8,128)(2,1)S(1)} %get-tuple-element.14, pred[16,128]{1,0:T(8,128)(4,1)S(1)} %get-tuple-element.9, pred[16,128]{1,0:T(8,128)(4,1)S(1)} %get-tuple-element.8), kind=kOutput, calls=%fused_computation.1 | convolution fusion | flops 30285824 | bytes 1159168 | tf_op jit(solution)/shard_map/dot_general | solution.py:63
  55.6 1.3 %convolution_convert_fusion = bf16[128,3584]{1,0:T(8,128)(2,1)} fusion(bf16[16,3584]{1,0:T(8,128)(2,1)S(1)} %collective-permute-done.10, bf16[16,3584]{1,0:T(8,128)(2,1)S(1)} %get-tuple-element.10, f32[16,128]{1,0:T(8,128)S(1)} %convolution_add_fusion.2, f32[16,128]{1,0:T(8,128)S(1)} %convolution_add_fusion.4, pred[16,128]{1,0:T(8,128)(4,1)S(1)} %get-tuple-element.9, ...), kind=kOutput, calls=%fused_computation | convolution fusion | flops 30302208 | bytes 1167360 | tf_op jit(solution)/shard_map/dot_general | solution.py:63
  (26 shorter events, 0.3 us)
Async XLA Ops:
  0.6 16.3 %copy-start.1 = (bf16[3584,128]{1,0:T(8,128)(2,1)S(1)}, bf16[3584,128]{1,0:T(8,128)(2,1)}, u32[]{:S(2)}) copy-start(bf16[3584,128]{1,0:T(8,128)(2,1)} %param.9) | copy-start | bytes 2752516
  0.6 16.3 %copy-start.3 = (f32[128]{0:T(128)S(1)}, f32[128]{0:T(128)}, u32[]{:S(2)}) copy-start(f32[128]{0:T(128)} %param.10) | copy-start | bytes 1540
  0.7 4.9 %collective-permute-start = (bf16[1,2,3584]{2,1,0:T(2,128)(2,1)}, bf16[1,2,3584]{2,1,0:T(2,128)(2,1)S(1)}, u32[]{:S(2)}, u32[]{:S(2)}) collective-permute-start(bf16[1,2,3584]{2,1,0:T(2,128)(2,1)} %bitcast.36), channel_id=1, source_target_pairs={{0,2},{1,3},{2,0},{3,1},{4,6},{5,7},{6,4},{7,5},{8,10},{9,11},{10,... | collective-permute-start | bytes 43016 | tf_op jit(solution)/shard_map/ppermute | solution.py:27
  3.7 13.7 %collective-permute-start.4 = (bf16[3584,128]{1,0:T(8,128)(2,1)}, bf16[3584,128]{1,0:T(8,128)(2,1)}, u32[]{:S(2)}, u32[]{:S(2)}) collective-permute-start(bf16[3584,128]{1,0:T(8,128)(2,1)} %param.9), channel_id=1, source_target_pairs={{0,1},{1,0},{2,3},{3,2},{4,5},{5,4},{6,7},{7,6},{8,9},{9,8},{10,11... | collective-permute-start | bytes 2752520 | tf_op jit(solution)/shard_map/ppermute | solution.py:27
  3.7 13.7 %collective-permute-start.6 = (bf16[128,3584]{1,0:T(8,128)(2,1)}, bf16[128,3584]{1,0:T(8,128)(2,1)S(1)}, u32[]{:S(2)}, u32[]{:S(2)}) collective-permute-start(bf16[128,3584]{1,0:T(8,128)(2,1)} %param.12), channel_id=1, source_target_pairs={{0,1},{1,0},{2,3},{3,2},{4,5},{5,4},{6,7},{7,6},{8,9},{9,8},{10,11... | collective-permute-start | bytes 2752520 | tf_op jit(solution)/shard_map/ppermute | solution.py:27
  4.2 13.2 %collective-permute-start.5 = (f32[128]{0:T(128)}, f32[128]{0:T(128)S(1)}, u32[]{:S(2)}, u32[]{:S(2)}) collective-permute-start(f32[128]{0:T(128)} %param.10), channel_id=1, source_target_pairs={{0,1},{1,0},{2,3},{3,2},{4,5},{5,4},{6,7},{7,6},{8,9},{9,8},{10,11... | collective-permute-start | bytes 1544 | tf_op jit(solution)/shard_map/ppermute | solution.py:27
  6.4 4.0 %collective-permute-start.1 = (bf16[2,2,3584]{2,1,0:T(2,128)(2,1)S(1)}, bf16[2,2,3584]{2,1,0:T(2,128)(2,1)S(1)}, u32[]{:S(2)}, u32[]{:S(2)}) collective-permute-start(bf16[2,2,3584]{2,1,0:T(2,128)(2,1)S(1)} %broadcast_select_fusion.2), channel_id=1, source_target_pairs={{0,4},{1,5},{2,6},{3,7},{4,0},{5,1},{6,2},{7,3},{8,12},{9,13},{10,... | collective-permute-start | bytes 86024 | tf_op jit(solution)/shard_map/ppermute | solution.py:27
  10.6 6.6 %copy-start = (bf16[128,3584]{1,0:T(8,128)(2,1)S(1)}, bf16[128,3584]{1,0:T(8,128)(2,1)}, u32[]{:S(2)}) copy-start(bf16[128,3584]{1,0:T(8,128)(2,1)} %param.12) | copy-start | bytes 2752516
  10.6 5.3 %collective-permute-start.2 = (bf16[4,2,3584]{2,1,0:T(2,128)(2,1)S(1)}, bf16[4,2,3584]{2,1,0:T(2,128)(2,1)S(1)}, u32[]{:S(2)}, u32[]{:S(2)}) collective-permute-start(bf16[4,2,3584]{2,1,0:T(2,128)(2,1)S(1)} %broadcast_select_fusion.1), channel_id=1, source_target_pairs={{0,8},{1,9},{2,10},{3,11},{4,12},{5,13},{6,14},{7,15},{8,0},{9,1},... | collective-permute-start | bytes 172040 | tf_op jit(solution)/shard_map/ppermute | solution.py:27
  17.4 18.5 %copy-start.2 = (f32[3584]{0:T(1024)S(1)}, f32[3584]{0:T(1024)}, u32[]{:S(2)}) copy-start(f32[3584]{0:T(1024)} %param.13) | copy-start | bytes 43012
  19.0 4.8 %collective-permute-start.7 = (bf16[16,3584]{1,0:T(8,128)(2,1)S(1)}, bf16[16,3584]{1,0:T(8,128)(2,1)S(1)}, u32[]{:S(2)}, u32[]{:S(2)}) collective-permute-start(bf16[16,3584]{1,0:T(8,128)(2,1)S(1)} %fusion), channel_id=1, source_target_pairs={{0,2},{1,3},{2,0},{3,1},{4,6},{5,7},{6,4},{7,5},{8,10},{9,11},{10,... | collective-permute-start | bytes 344072 | tf_op jit(solution)/shard_map/ppermute | solution.py:27
  23.9 4.9 %collective-permute-start.8 = (bf16[16,3584]{1,0:T(8,128)(2,1)S(1)}, bf16[16,3584]{1,0:T(8,128)(2,1)S(1)}, u32[]{:S(2)}, u32[]{:S(2)}) collective-permute-start(bf16[16,3584]{1,0:T(8,128)(2,1)S(1)} %add_convert_fusion.1), channel_id=1, source_target_pairs={{0,4},{1,5},{2,6},{3,7},{4,0},{5,1},{6,2},{7,3},{8,12},{9,13},{10,... | collective-permute-start | bytes 344072 | tf_op jit(solution)/shard_map/ppermute | solution.py:27
  25.9 7.2 %collective-permute-start.3 = (bf16[16,3584]{1,0:T(8,128)(2,1)S(1)}, bf16[16,3584]{1,0:T(8,128)(2,1)S(1)}, u32[]{:S(2)}, u32[]{:S(2)}) collective-permute-start(bf16[16,3584]{1,0:T(8,128)(2,1)S(1)} %select_n.61), channel_id=1, source_target_pairs={{0,1},{1,0},{2,3},{3,2},{4,5},{5,4},{6,7},{7,6},{8,9},{9,8},{10,11... | collective-permute-start | bytes 344072 | tf_op jit(solution)/shard_map/ppermute | solution.py:27
  28.8 7.0 %collective-permute-start.9 = (bf16[16,3584]{1,0:T(8,128)(2,1)S(1)}, bf16[16,3584]{1,0:T(8,128)(2,1)S(1)}, u32[]{:S(2)}, u32[]{:S(2)}) collective-permute-start(bf16[16,3584]{1,0:T(8,128)(2,1)S(1)} %add_convert_fusion), channel_id=1, source_target_pairs={{0,8},{1,9},{2,10},{3,11},{4,12},{5,13},{6,14},{7,15},{8,0},{9,1},... | collective-permute-start | bytes 344072 | tf_op jit(solution)/shard_map/ppermute | solution.py:27
  36.7 8.0 %copy-start.4 = (f32[128]{0:T(128)S(1)}, f32[128]{0:T(128)}, u32[]{:S(2)}) copy-start(f32[128]{0:T(128)} %param.11) | copy-start | bytes 1540
  38.6 3.8 %collective-permute-start.11 = (f32[3584]{0:T(1024)S(1)}, f32[3584]{0:T(1024)S(1)}, u32[]{:S(2)}, u32[]{:S(2)}) collective-permute-start(f32[3584]{0:T(1024)S(1)} %fusion.11), channel_id=1, source_target_pairs={{0,2},{1,3},{2,0},{3,1},{4,6},{5,7},{6,4},{7,5},{8,10},{9,11},{10,... | collective-permute-start | bytes 43016 | tf_op jit(solution)/shard_map/ppermute | solution.py:27
  42.5 3.9 %collective-permute-start.12 = (f32[3584]{0:T(1024)S(1)}, f32[3584]{0:T(1024)S(1)}, u32[]{:S(2)}, u32[]{:S(2)}) collective-permute-start(f32[3584]{0:T(1024)S(1)} %add.112), channel_id=1, source_target_pairs={{0,4},{1,5},{2,6},{3,7},{4,0},{5,1},{6,2},{7,3},{8,12},{9,13},{10,... | collective-permute-start | bytes 43016 | tf_op jit(solution)/shard_map/ppermute | solution.py:27
  46.4 5.1 %collective-permute-start.13 = (f32[3584]{0:T(1024)S(1)}, f32[3584]{0:T(1024)S(1)}, u32[]{:S(2)}, u32[]{:S(2)}) collective-permute-start(f32[3584]{0:T(1024)S(1)} %add.113), channel_id=1, source_target_pairs={{0,8},{1,9},{2,10},{3,11},{4,12},{5,13},{6,14},{7,15},{8,0},{9,1},... | collective-permute-start | bytes 43016 | tf_op jit(solution)/shard_map/ppermute | solution.py:27
  49.8 3.5 %collective-permute-start.10 = (bf16[16,3584]{1,0:T(8,128)(2,1)S(1)}, bf16[16,3584]{1,0:T(8,128)(2,1)S(1)}, u32[]{:S(2)}, u32[]{:S(2)}) collective-permute-start(bf16[16,3584]{1,0:T(8,128)(2,1)S(1)} %get-tuple-element.10), channel_id=1, source_target_pairs={{0,1},{1,0},{2,3},{3,2},{4,5},{5,4},{6,7},{7,6},{8,9},{9,8},{10,11... | collective-permute-start | bytes 344072 | tf_op jit(solution)/shard_map/ppermute | solution.py:27
  51.5 1.2 %collective-permute-start.14 = (f32[3584]{0:T(1024)S(1)}, f32[3584]{0:T(1024)S(1)}, u32[]{:S(2)}, u32[]{:S(2)}) collective-permute-start(f32[3584]{0:T(1024)S(1)} %add_subtract_fusion), channel_id=1, source_target_pairs={{0,1},{1,0},{2,3},{3,2},{4,5},{5,4},{6,7},{7,6},{8,9},{9,8},{10,11... | collective-permute-start | bytes 43016 | tf_op jit(solution)/shard_map/ppermute | solution.py:27

commit v2 on v1

--- a/solution.py
+++ b/solution.py
@@ -70,6 +70,15 @@
     codes_mine = jnp.where(gate_mine, preact_mine, 0.0).astype(BF16)
     codes_other = jnp.where(gate_other, preact_other, 0.0).astype(BF16)
     total = dot(codes_mine, decoder_weight) + dot(codes_other, decoder_other)
+    rows_other = swap(rows, 1)
+    centered_other = center(rows_other)
+    gate_rest = opened(ids_other, me * width, width)
+    preact_rest = dot(centered_other, encoder_weight) + encoder_bias
+    preact = jnp.concatenate([preact_mine, preact_rest])
+    gate = jnp.concatenate([gate_mine, gate_rest])
+    every_centered = jnp.concatenate([centered, centered_other])
+    codes = jnp.where(gate, preact, 0.0).astype(BF16)
+
     for bit in hops:
         low = lax.optimization_barrier(total.astype(BF16))
         total = low.astype(F32) + swap(low, bit).astype(F32)
@@ -86,29 +95,35 @@
 
     part = product(encoder_weight, grad_mine) + product(encoder_other, grad_other)
     part = part[0] + part[1]
-    for bit in hops:
+    errors_other = swap(errors, 1)
+
+    every_error = jnp.concatenate([errors, errors_other])
+
+    def small_outputs():
+        code_grad = dot_last(every_error, decoder_weight)
+        distance = (preact - threshold) / EPSILON
+        kernel = jnp.exp(-0.5 * distance * distance) / (EPSILON * math.sqrt(2.0 * math.pi))
+        grad_threshold = jnp.sum(-threshold * code_grad * kernel - SPARSITY * kernel, axis=0)
+        preact_grad = jnp.where(gate, code_grad, 0.0)
+        return grad_threshold, jnp.sum(preact_grad, axis=0), preact_grad.astype(BF16)
+
+    def decoder_output():
+        return dot_rows(codes, every_error).astype(BF16)
+
+    def encoder_output():
+        return dot_rows(every_centered, small[2]).astype(BF16)
+
+    part = part + swap(part, hops[0])
+    small, part = lax.optimization_barrier((small_outputs(), part))
+    part = part + swap(part, hops[1])
+    grad_decoder, part = lax.optimization_barrier((decoder_output(), part))
+    part = part + swap(part, hops[2])
+    grad_encoder, part = lax.optimization_barrier((encoder_output(), part))
+    for bit in hops[3:]:
         part = part + swap(part, bit)
     part = jnp.sum(errors, axis=0, dtype=F32) - part
     grad_decoder_bias = part + swap(part, 1)
-
-    rows_other = swap(rows, 1)
-    errors_other = swap(errors, 1)
-    centered_other = center(rows_other)
-    gate_rest = opened(ids_other, me * width, width)
-    preact_rest = dot(centered_other, encoder_weight) + encoder_bias
-    preact = jnp.concatenate([preact_mine, preact_rest])
-    gate = jnp.concatenate([gate_mine, gate_rest])
-    every_error = jnp.concatenate([errors, errors_other])
-    every_centered = jnp.concatenate([centered, centered_other])
-    codes = jnp.where(gate, preact, 0.0).astype(BF16)
-    code_grad = dot_last(every_error, decoder_weight)
-    distance = (preact - threshold) / EPSILON
-    kernel = jnp.exp(-0.5 * distance * distance) / (EPSILON * math.sqrt(2.0 * math.pi))
-    grad_threshold = jnp.sum(-threshold * code_grad * kernel - SPARSITY * kernel, axis=0)
-    preact_grad = jnp.where(gate, code_grad, 0.0)
-    grad_encoder_bias = jnp.sum(preact_grad, axis=0)
-    grad_encoder = dot_rows(every_centered, preact_grad.astype(BF16)).astype(BF16)
-    grad_decoder = dot_rows(codes, every_error).astype(BF16)
+    grad_threshold, grad_encoder_bias, _ = small
     return (grad_encoder, grad_encoder_bias, grad_threshold, grad_decoder, grad_decoder_bias)
 
 

time: 57.4 us -> 54.8 us (0.955)
  waiting for transfers between devices: 19 us -> 16.4 us
    ppermute x15, waiting for transfers between devices: 19 us -> 16.4 us  [swap(): return lax.ppermute(array, 'latent', [(i, i ^ bit) for i in range(count)])]
  transfers between devices with their start and end apart: 15 -> 15, of which waited for: 10 -> 10; matrix products, arithmetic and copies ran while one was open for 8% -> 16% of each run, Pallas kernels for 0% -> 0%
where the time goes in v2:
time: 54.8 us; the launch traced here: 54.4 us
  starting transfers between devices  24.3 us (44%)
  waiting for transfers between devices  16.4 us (30%)
  matrix products  8.52 us (16%)
  other arithmetic  3.62 us (7%)
  between operations  0.83 us (2%)
  local copies, waits for them, and re-layouts  0.79 us (1%)
    ppermute x15, starting transfers between devices, swap(): return lax.ppermute(array, 'latent', [(i, i ^ bit) for i in range(count)])  24.3 us
    ppermute x15, waiting for transfers between devices, swap(): return lax.ppermute(array, 'latent', [(i, i ^ bit) for i in range(count)])  16.4 us
    dot_general x5, matrix products, dot_last(): lax.dot_general(a, b, (((1,), (1,)), ((), ())), preferred_element_type=F32)  3.47 us
    dot_general x2, matrix products, dot_rows(): lax.dot_general(a, b, (((0,), (0,)), ((), ())), preferred_element_type=F32)  2.73 us
    dot_general x4, matrix products, dot(): return jnp.dot(a, b, preferred_element_type=F32)  2.32 us
    select_n x3, other arithmetic, on_device(): block = jnp.where(me & bit == 0, low, high)  1.23 us
  transfers between devices with their start and end apart: 15, of which 10 were waited for; matrix products, arithmetic and copies ran while one was open for 16% of the time, Pallas kernels for 0%

profile of v2, /device:TPU:0, one launch (start us, length us, event | category | flops | bytes accessed | tf_op | source)
XLA Modules:
  0.0 54.4 jit_solution(2026790514846963709)
XLA Ops:
  0.7 3.0 %collective-permute-start = (bf16[1,2,3584]{2,1,0:T(2,128)(2,1)}, bf16[1,2,3584]{2,1,0:T(2,128)(2,1)S(1)}, u32[]{:S(2)}, u32[]{:S(2)}) collective-permute-start(bf16[1,2,3584]{2,1,0:T(2,128)(2,1)} %bitcast.37), channel_id=1, source_target_pairs={{0,2},{1,3},{2,0},{3,1},{4,6},{5,7},{6,4},{7,5},{8,10},{9,11},{10,... | collective-permute-start | bytes 43016 | tf_op jit(solution)/shard_map/ppermute | solution.py:27
  3.7 0.5 collective-permute-start.6
  4.2 0.0 collective-permute-start.5
  4.2 0.7 %constant_dynamic-slice_fusion = (s32[8,1,2,128]{3,2,1,0:T(2,128)S(1)}, s32[8,1,2,128]{3,2,1,0:T(2,128)S(1)}) fusion(s32[8,2,2,128]{3,2,1,0:T(2,128)} %bitcast.36, s32[]{:T(128)S(6)} %select_n.65, s32[]{:T(128)S(6)} %select_n.62), kind=kLoop, calls=%fused_computation.62 | loop fusion | bytes 32776 | tf_op jit(solution)/shard_map/jit(dynamic_index_in_dim)/dynamic_slice | solution.py:51
  4.9 0.7 %collective-permute-done = bf16[1,2,3584]{2,1,0:T(2,128)(2,1)S(1)} collective-permute-done((bf16[1,2,3584]{2,1,0:T(2,128)(2,1)}, bf16[1,2,3584]{2,1,0:T(2,128)(2,1)S(1)}, u32[]{:S(2)}, u32[]{:S(2)}) %collective-permute-start) | collective-permute-done | bytes 14368 | tf_op jit(solution)/shard_map/ppermute | solution.py:27
  5.6 0.8 %broadcast_select_fusion.2 = bf16[2,2,3584]{2,1,0:T(2,128)(2,1)S(1)} fusion(pred[]{:T(512)S(6)} %eq.50, bf16[1,2,3584]{2,1,0:T(2,128)(2,1)S(1)} %collective-permute-done, bf16[1,2,3584]{2,1,0:T(2,128)(2,1)} %bitcast.38), kind=kLoop, calls=%fused_computation.32 | loop fusion | flops 43008 | bytes 57345 | tf_op jit(solution)/shard_map/jit(_where)/select_n | solution.py:45
  6.4 2.1 %collective-permute-start.1 = (bf16[2,2,3584]{2,1,0:T(2,128)(2,1)S(1)}, bf16[2,2,3584]{2,1,0:T(2,128)(2,1)S(1)}, u32[]{:S(2)}, u32[]{:S(2)}) collective-permute-start(bf16[2,2,3584]{2,1,0:T(2,128)(2,1)S(1)} %broadcast_select_fusion.2), channel_id=1, source_target_pairs={{0,4},{1,5},{2,6},{3,7},{4,0},{5,1},{6,2},{7,3},{8,12},{9,13},{10,... | collective-permute-start | bytes 86024 | tf_op jit(solution)/shard_map/ppermute | solution.py:27
  8.6 1.8 %collective-permute-done.1 = bf16[2,2,3584]{2,1,0:T(2,128)(2,1)S(1)} collective-permute-done((bf16[2,2,3584]{2,1,0:T(2,128)(2,1)S(1)}, bf16[2,2,3584]{2,1,0:T(2,128)(2,1)S(1)}, u32[]{:S(2)}, u32[]{:S(2)}) %collective-permute-start.1) | collective-permute-done | bytes 28704 | tf_op jit(solution)/shard_map/ppermute | solution.py:27
  10.4 0.1 broadcast_select_fusion.1
  10.6 0.0 copy-start
  10.6 3.1 %collective-permute-start.2 = (bf16[4,2,3584]{2,1,0:T(2,128)(2,1)S(1)}, bf16[4,2,3584]{2,1,0:T(2,128)(2,1)S(1)}, u32[]{:S(2)}, u32[]{:S(2)}) collective-permute-start(bf16[4,2,3584]{2,1,0:T(2,128)(2,1)S(1)} %broadcast_select_fusion.1), channel_id=1, source_target_pairs={{0,8},{1,9},{2,10},{3,11},{4,12},{5,13},{6,14},{7,15},{8,0},{9,1},... | collective-permute-start | bytes 172040 | tf_op jit(solution)/shard_map/ppermute | solution.py:27
  13.7 0.7 %compare_reduce_fusion.1 = (pred[16,128]{1,0:T(8,128)(4,1)S(1)}, pred[16,128]{1,0:T(8,128)(4,1)S(1)}, pred[16,128]{1,0:T(8,128)(4,1)S(1)}) fusion(s32[128]{0:T(128)S(1)} %iota_add_fusion, s32[16,128]{1,0:T(8,128)S(1)} %bitcast.35, s32[128]{0:T(128)S(1)} %iota_add_fusion.1, s32[16,128]{1,0:T(8,128)S(1)} %bitcast.34), kind=kLoop, calls=%fused_computation.15 | loop fusion | flops 1566720 | bytes 23552 | tf_op jit(solution)/shard_map/reduce_or | solution.py:16
  14.4 1.4 %collective-permute-done.2 = bf16[4,2,3584]{2,1,0:T(2,128)(2,1)S(1)} collective-permute-done((bf16[4,2,3584]{2,1,0:T(2,128)(2,1)S(1)}, bf16[4,2,3584]{2,1,0:T(2,128)(2,1)S(1)}, u32[]{:S(2)}, u32[]{:S(2)}) %collective-permute-start.2) | collective-permute-done | bytes 57376 | tf_op jit(solution)/shard_map/ppermute | solution.py:27
  15.8 0.3 broadcast_select_fusion
  16.1 0.7 %fusion.5 = bf16[16,3584]{1,0:T(8,128)(2,1)S(1)} fusion(bf16[16,3584]{1,0:T(8,128)(2,1)S(1)} %select_n.61, f32[3584]{0:T(1024)} %param.13), kind=kLoop, calls=%fused_computation.19 | loop fusion | flops 172032 | bytes 243712 | tf_op jit(solution)/shard_map/convert_element_type | solution.py:54
  16.9 0.2 convolution_add_fusion.4
  17.1 0.2 fusion.13
  17.4 0.0 collective-permute-done.6
  17.4 0.0 copy-start.4
  17.4 0.0 copy-start.2
  17.4 1.6 %fusion = bf16[16,3584]{1,0:T(8,128)(2,1)S(1)} fusion(f32[16,3584]{1,0:T(8,128)S(1)} %fusion.13, bf16[128,3584]{1,0:T(8,128)(2,1)S(1)} %collective-permute-done.6, pred[16,128]{1,0:T(8,128)(4,1)S(1)} %get-tuple-element.23, bf16[16,3584]{1,0:T(8,128)(2,1)S(1)} %fusion.5, bf16[3584,128]{1,0:T(8,128)(2,1)} %collective-permute-done.4, ...), kind=kOutput, calls=%fused_computation.3 | convolution fusion | flops 29480960 | bytes 2296320 | tf_op jit(solution)/shard_map/dot_general | solution.py:57
  19.1 1.9 %collective-permute-start.7 = (bf16[16,3584]{1,0:T(8,128)(2,1)S(1)}, bf16[16,3584]{1,0:T(8,128)(2,1)S(1)}, u32[]{:S(2)}, u32[]{:S(2)}) collective-permute-start(bf16[16,3584]{1,0:T(8,128)(2,1)S(1)} %fusion), channel_id=1, source_target_pairs={{0,2},{1,3},{2,0},{3,1},{4,6},{5,7},{6,4},{7,5},{8,10},{9,11},{10,... | collective-permute-start | bytes 344072 | tf_op jit(solution)/shard_map/ppermute | solution.py:27
  21.0 2.9 %collective-permute-done.7 = bf16[16,3584]{1,0:T(8,128)(2,1)S(1)} collective-permute-done((bf16[16,3584]{1,0:T(8,128)(2,1)S(1)}, bf16[16,3584]{1,0:T(8,128)(2,1)S(1)}, u32[]{:S(2)}, u32[]{:S(2)}) %collective-permute-start.7) | collective-permute-done | bytes 114720 | tf_op jit(solution)/shard_map/ppermute | solution.py:27
  23.9 2.0 %collective-permute-start.8 = (bf16[16,3584]{1,0:T(8,128)(2,1)S(1)}, bf16[16,3584]{1,0:T(8,128)(2,1)S(1)}, u32[]{:S(2)}, u32[]{:S(2)}) collective-permute-start(bf16[16,3584]{1,0:T(8,128)(2,1)S(1)} %add_convert_fusion.1), channel_id=1, source_target_pairs={{0,4},{1,5},{2,6},{3,7},{4,0},{5,1},{6,2},{7,3},{8,12},{9,13},{10,... | collective-permute-start | bytes 344072 | tf_op jit(solution)/shard_map/ppermute | solution.py:27
  25.9 2.9 %collective-permute-done.8 = bf16[16,3584]{1,0:T(8,128)(2,1)S(1)} collective-permute-done((bf16[16,3584]{1,0:T(8,128)(2,1)S(1)}, bf16[16,3584]{1,0:T(8,128)(2,1)S(1)}, u32[]{:S(2)}, u32[]{:S(2)}) %collective-permute-start.8) | collective-permute-done | bytes 114720 | tf_op jit(solution)/shard_map/ppermute | solution.py:27
  28.8 4.3 %collective-permute-start.9 = (bf16[16,3584]{1,0:T(8,128)(2,1)S(1)}, bf16[16,3584]{1,0:T(8,128)(2,1)S(1)}, u32[]{:S(2)}, u32[]{:S(2)}) collective-permute-start(bf16[16,3584]{1,0:T(8,128)(2,1)S(1)} %add_convert_fusion), channel_id=1, source_target_pairs={{0,8},{1,9},{2,10},{3,11},{4,12},{5,13},{6,14},{7,15},{8,0},{9,1},... | collective-permute-start | bytes 344072 | tf_op jit(solution)/shard_map/ppermute | solution.py:27
  33.1 2.8 %collective-permute-done.9 = bf16[16,3584]{1,0:T(8,128)(2,1)S(1)} collective-permute-done((bf16[16,3584]{1,0:T(8,128)(2,1)S(1)}, bf16[16,3584]{1,0:T(8,128)(2,1)S(1)}, u32[]{:S(2)}, u32[]{:S(2)}) %collective-permute-start.9) | collective-permute-done | bytes 114720 | tf_op jit(solution)/shard_map/ppermute | solution.py:27
  35.9 0.1 subtract_convert_fusion
  36.0 0.3 fusion.4
  36.3 0.3 fusion.3
  36.7 0.1 collective-permute-start.10
  36.8 0.3 fusion.17
  37.1 1.5 %convolution_add_fusion.1 = f32[2,3584]{1,0:T(2,128)S(1)} fusion(f32[2,3584]{1,0:T(2,128)S(1)} %fusion.17, bf16[3584,128]{1,0:T(8,128)(2,1)} %collective-permute-done.4, bf16[1,128]{1,0:T(2,128)(2,1)S(1)} %fusion.24, bf16[1,128]{1,0:T(2,128)(2,1)S(1)} %bitcast_convert_fusion), kind=kOutput, calls=%fused_computation.4 | convolution fusion | flops 1843200 | bytes 975360 | tf_op jit(solution)/shard_map/dot_general | solution.py:60
  38.7 0.1 fusion.11
  38.7 1.6 %collective-permute-start.11 = (f32[3584]{0:T(1024)S(1)}, f32[3584]{0:T(1024)S(1)}, u32[]{:S(2)}, u32[]{:S(2)}) collective-permute-start(f32[3584]{0:T(1024)S(1)} %fusion.11), channel_id=1, source_target_pairs={{0,2},{1,3},{2,0},{3,1},{4,6},{5,7},{6,4},{7,5},{8,10},{9,11},{10,... | collective-permute-start | bytes 43016 | tf_op jit(solution)/shard_map/ppermute | solution.py:27
  40.3 0.2 convolution_add_fusion.2
  40.5 0.1 convert_reduce_fusion
  40.6 1.9 %collective-permute-done.11 = f32[3584]{0:T(1024)S(1)} collective-permute-done((f32[3584]{0:T(1024)S(1)}, f32[3584]{0:T(1024)S(1)}, u32[]{:S(2)}, u32[]{:S(2)}) %collective-permute-start.11) | collective-permute-done | bytes 14368 | tf_op jit(solution)/shard_map/ppermute | solution.py:27
  42.5 0.9 %select_reduce_fusion = (f32[128]{0:T(128)}, f32[128]{0:T(128)}, bf16[32,128]{1,0:T(8,128)(2,1)S(1)}) fusion(pred[16,128]{1,0:T(8,128)(4,1)S(1)} %get-tuple-element.25, pred[16,128]{1,0:T(8,128)(4,1)S(1)} %get-tuple-element.24, f32[128]{0:T(128)S(1)} %copy-done.4, f32[16,128]{1,0:T(8,128)S(1)} %convolution_add_fusion.2, ...), kind=kOutput, calls=%fused_computation.40 | convolution fusion | flops 29880064 | bytes 1177600 | tf_op jit(solution)/shard_map/dot_general | solution.py:60
  43.5 2.2 %collective-permute-start.12 = (f32[3584]{0:T(1024)S(1)}, f32[3584]{0:T(1024)S(1)}, u32[]{:S(2)}, u32[]{:S(2)}) collective-permute-start(f32[3584]{0:T(1024)S(1)} %add.112), channel_id=1, source_target_pairs={{0,4},{1,5},{2,6},{3,7},{4,0},{5,1},{6,2},{7,3},{8,12},{9,13},{10,... | collective-permute-start | bytes 43016 | tf_op jit(solution)/shard_map/ppermute | solution.py:27
  45.7 1.3 %convolution_convert_fusion = bf16[128,3584]{1,0:T(8,128)(2,1)} fusion(bf16[16,3584]{1,0:T(8,128)(2,1)S(1)} %collective-permute-done.10, bf16[16,3584]{1,0:T(8,128)(2,1)S(1)} %get-tuple-element.27, f32[16,128]{1,0:T(8,128)S(1)} %convolution_add_fusion.2, f32[16,128]{1,0:T(8,128)S(1)} %convolution_add_fusion.4, pred[16,128]{1,0:T(8,128)(4,1)S(1)} %get-tuple-element.25, ...), kind=kOutput, calls=%fused_computation | convolution fusion | flops 30302208 | bytes 1167360 | tf_op jit(solution)/shard_map/dot_general | solution.py:63
  47.1 0.4 collective-permute-done.12
  47.4 3.4 %collective-permute-start.13 = (f32[3584]{0:T(1024)S(1)}, f32[3584]{0:T(1024)S(1)}, u32[]{:S(2)}, u32[]{:S(2)}) collective-permute-start(f32[3584]{0:T(1024)S(1)} %add.113), channel_id=1, source_target_pairs={{0,8},{1,9},{2,10},{3,11},{4,12},{5,13},{6,14},{7,15},{8,0},{9,1},... | collective-permute-start | bytes 43016 | tf_op jit(solution)/shard_map/ppermute | solution.py:27
  50.8 1.4 %convolution_convert_fusion.1 = bf16[3584,128]{1,0:T(8,128)(2,1)} fusion(bf16[32,128]{1,0:T(8,128)(2,1)S(1)} %select_convert_fusion.1, bf16[16,3584]{1,0:T(8,128)(2,1)S(1)} %get-tuple-element.26, bf16[16,3584]{1,0:T(8,128)(2,1)S(1)} %fusion.5), kind=kOutput, calls=%fused_computation.1 | convolution fusion | flops 30277632 | bytes 1155072 | tf_op jit(solution)/shard_map/dot_general | solution.py:63
  52.2 0.3 collective-permute-done.13
  52.5 0.1 collective-permute-start.14
  52.6 1.2 %collective-permute-done.14 = f32[3584]{0:T(1024)S(1)} collective-permute-done((f32[3584]{0:T(1024)S(1)}, f32[3584]{0:T(1024)S(1)}, u32[]{:S(2)}, u32[]{:S(2)}) %collective-permute-start.14) | collective-permute-done | bytes 14368 | tf_op jit(solution)/shard_map/ppermute | solution.py:27
  53.8 0.6 %add.115 = f32[3584]{0:T(1024)} add(f32[3584]{0:T(1024)S(1)} %sub.64, f32[3584]{0:T(1024)S(1)} %collective-permute-done.14) | non-fusion elementwise | flops 3584 | bytes 43008 | tf_op jit(solution)/shard_map/add | solution.py:125
  (28 shorter events, 0.2 us)
Async XLA Ops:
  0.6 16.3 %copy-start.1 = (bf16[3584,128]{1,0:T(8,128)(2,1)S(1)}, bf16[3584,128]{1,0:T(8,128)(2,1)}, u32[]{:S(2)}) copy-start(bf16[3584,128]{1,0:T(8,128)(2,1)} %param.9) | copy-start | bytes 2752516
  0.6 16.3 %copy-start.3 = (f32[128]{0:T(128)S(1)}, f32[128]{0:T(128)}, u32[]{:S(2)}) copy-start(f32[128]{0:T(128)} %param.10) | copy-start | bytes 1540
  0.7 4.9 %collective-permute-start = (bf16[1,2,3584]{2,1,0:T(2,128)(2,1)}, bf16[1,2,3584]{2,1,0:T(2,128)(2,1)S(1)}, u32[]{:S(2)}, u32[]{:S(2)}) collective-permute-start(bf16[1,2,3584]{2,1,0:T(2,128)(2,1)} %bitcast.37), channel_id=1, source_target_pairs={{0,2},{1,3},{2,0},{3,1},{4,6},{5,7},{6,4},{7,5},{8,10},{9,11},{10,... | collective-permute-start | bytes 43016 | tf_op jit(solution)/shard_map/ppermute | solution.py:27
  3.7 13.7 %collective-permute-start.4 = (bf16[3584,128]{1,0:T(8,128)(2,1)}, bf16[3584,128]{1,0:T(8,128)(2,1)}, u32[]{:S(2)}, u32[]{:S(2)}) collective-permute-start(bf16[3584,128]{1,0:T(8,128)(2,1)} %param.9), channel_id=1, source_target_pairs={{0,1},{1,0},{2,3},{3,2},{4,5},{5,4},{6,7},{7,6},{8,9},{9,8},{10,11... | collective-permute-start | bytes 2752520 | tf_op jit(solution)/shard_map/ppermute | solution.py:27
  3.7 13.7 %collective-permute-start.6 = (bf16[128,3584]{1,0:T(8,128)(2,1)}, bf16[128,3584]{1,0:T(8,128)(2,1)S(1)}, u32[]{:S(2)}, u32[]{:S(2)}) collective-permute-start(bf16[128,3584]{1,0:T(8,128)(2,1)} %param.12), channel_id=1, source_target_pairs={{0,1},{1,0},{2,3},{3,2},{4,5},{5,4},{6,7},{7,6},{8,9},{9,8},{10,11... | collective-permute-start | bytes 2752520 | tf_op jit(solution)/shard_map/ppermute | solution.py:27
  4.2 13.2 %collective-permute-start.5 = (f32[128]{0:T(128)}, f32[128]{0:T(128)S(1)}, u32[]{:S(2)}, u32[]{:S(2)}) collective-permute-start(f32[128]{0:T(128)} %param.10), channel_id=1, source_target_pairs={{0,1},{1,0},{2,3},{3,2},{4,5},{5,4},{6,7},{7,6},{8,9},{9,8},{10,11... | collective-permute-start | bytes 1544 | tf_op jit(solution)/shard_map/ppermute | solution.py:27
  6.4 4.0 %collective-permute-start.1 = (bf16[2,2,3584]{2,1,0:T(2,128)(2,1)S(1)}, bf16[2,2,3584]{2,1,0:T(2,128)(2,1)S(1)}, u32[]{:S(2)}, u32[]{:S(2)}) collective-permute-start(bf16[2,2,3584]{2,1,0:T(2,128)(2,1)S(1)} %broadcast_select_fusion.2), channel_id=1, source_target_pairs={{0,4},{1,5},{2,6},{3,7},{4,0},{5,1},{6,2},{7,3},{8,12},{9,13},{10,... | collective-permute-start | bytes 86024 | tf_op jit(solution)/shard_map/ppermute | solution.py:27
  10.6 6.6 %copy-start = (bf16[128,3584]{1,0:T(8,128)(2,1)S(1)}, bf16[128,3584]{1,0:T(8,128)(2,1)}, u32[]{:S(2)}) copy-start(bf16[128,3584]{1,0:T(8,128)(2,1)} %param.12) | copy-start | bytes 2752516
  10.6 5.3 %collective-permute-start.2 = (bf16[4,2,3584]{2,1,0:T(2,128)(2,1)S(1)}, bf16[4,2,3584]{2,1,0:T(2,128)(2,1)S(1)}, u32[]{:S(2)}, u32[]{:S(2)}) collective-permute-start(bf16[4,2,3584]{2,1,0:T(2,128)(2,1)S(1)} %broadcast_select_fusion.1), channel_id=1, source_target_pairs={{0,8},{1,9},{2,10},{3,11},{4,12},{5,13},{6,14},{7,15},{8,0},{9,1},... | collective-permute-start | bytes 172040 | tf_op jit(solution)/shard_map/ppermute | solution.py:27
  17.4 15.7 %copy-start.4 = (f32[128]{0:T(128)S(1)}, f32[128]{0:T(128)}, u32[]{:S(2)}) copy-start(f32[128]{0:T(128)} %param.11) | copy-start | bytes 1540
  17.4 18.5 %copy-start.2 = (f32[3584]{0:T(1024)S(1)}, f32[3584]{0:T(1024)}, u32[]{:S(2)}) copy-start(f32[3584]{0:T(1024)} %param.13) | copy-start | bytes 43012
  19.1 4.8 %collective-permute-start.7 = (bf16[16,3584]{1,0:T(8,128)(2,1)S(1)}, bf16[16,3584]{1,0:T(8,128)(2,1)S(1)}, u32[]{:S(2)}, u32[]{:S(2)}) collective-permute-start(bf16[16,3584]{1,0:T(8,128)(2,1)S(1)} %fusion), channel_id=1, source_target_pairs={{0,2},{1,3},{2,0},{3,1},{4,6},{5,7},{6,4},{7,5},{8,10},{9,11},{10,... | collective-permute-start | bytes 344072 | tf_op jit(solution)/shard_map/ppermute | solution.py:27
  23.9 4.9 %collective-permute-start.8 = (bf16[16,3584]{1,0:T(8,128)(2,1)S(1)}, bf16[16,3584]{1,0:T(8,128)(2,1)S(1)}, u32[]{:S(2)}, u32[]{:S(2)}) collective-permute-start(bf16[16,3584]{1,0:T(8,128)(2,1)S(1)} %add_convert_fusion.1), channel_id=1, source_target_pairs={{0,4},{1,5},{2,6},{3,7},{4,0},{5,1},{6,2},{7,3},{8,12},{9,13},{10,... | collective-permute-start | bytes 344072 | tf_op jit(solution)/shard_map/ppermute | solution.py:27
  25.9 7.2 %collective-permute-start.3 = (bf16[16,3584]{1,0:T(8,128)(2,1)S(1)}, bf16[16,3584]{1,0:T(8,128)(2,1)S(1)}, u32[]{:S(2)}, u32[]{:S(2)}) collective-permute-start(bf16[16,3584]{1,0:T(8,128)(2,1)S(1)} %select_n.61), channel_id=1, source_target_pairs={{0,1},{1,0},{2,3},{3,2},{4,5},{5,4},{6,7},{7,6},{8,9},{9,8},{10,11... | collective-permute-start | bytes 344072 | tf_op jit(solution)/shard_map/ppermute | solution.py:27
  28.8 7.0 %collective-permute-start.9 = (bf16[16,3584]{1,0:T(8,128)(2,1)S(1)}, bf16[16,3584]{1,0:T(8,128)(2,1)S(1)}, u32[]{:S(2)}, u32[]{:S(2)}) collective-permute-start(bf16[16,3584]{1,0:T(8,128)(2,1)S(1)} %add_convert_fusion), channel_id=1, source_target_pairs={{0,8},{1,9},{2,10},{3,11},{4,12},{5,13},{6,14},{7,15},{8,0},{9,1},... | collective-permute-start | bytes 344072 | tf_op jit(solution)/shard_map/ppermute | solution.py:27
  36.7 5.8 %collective-permute-start.10 = (bf16[16,3584]{1,0:T(8,128)(2,1)S(1)}, bf16[16,3584]{1,0:T(8,128)(2,1)S(1)}, u32[]{:S(2)}, u32[]{:S(2)}) collective-permute-start(bf16[16,3584]{1,0:T(8,128)(2,1)S(1)} %get-tuple-element.27), channel_id=1, source_target_pairs={{0,1},{1,0},{2,3},{3,2},{4,5},{5,4},{6,7},{7,6},{8,9},{9,8},{10,11... | collective-permute-start | bytes 344072 | tf_op jit(solution)/shard_map/ppermute | solution.py:27
  38.7 3.8 %collective-permute-start.11 = (f32[3584]{0:T(1024)S(1)}, f32[3584]{0:T(1024)S(1)}, u32[]{:S(2)}, u32[]{:S(2)}) collective-permute-start(f32[3584]{0:T(1024)S(1)} %fusion.11), channel_id=1, source_target_pairs={{0,2},{1,3},{2,0},{3,1},{4,6},{5,7},{6,4},{7,5},{8,10},{9,11},{10,... | collective-permute-start | bytes 43016 | tf_op jit(solution)/shard_map/ppermute | solution.py:27
  43.5 3.9 %collective-permute-start.12 = (f32[3584]{0:T(1024)S(1)}, f32[3584]{0:T(1024)S(1)}, u32[]{:S(2)}, u32[]{:S(2)}) collective-permute-start(f32[3584]{0:T(1024)S(1)} %add.112), channel_id=1, source_target_pairs={{0,4},{1,5},{2,6},{3,7},{4,0},{5,1},{6,2},{7,3},{8,12},{9,13},{10,... | collective-permute-start | bytes 43016 | tf_op jit(solution)/shard_map/ppermute | solution.py:27
  47.4 5.1 %collective-permute-start.13 = (f32[3584]{0:T(1024)S(1)}, f32[3584]{0:T(1024)S(1)}, u32[]{:S(2)}, u32[]{:S(2)}) collective-permute-start(f32[3584]{0:T(1024)S(1)} %add.113), channel_id=1, source_target_pairs={{0,8},{1,9},{2,10},{3,11},{4,12},{5,13},{6,14},{7,15},{8,0},{9,1},... | collective-permute-start | bytes 43016 | tf_op jit(solution)/shard_map/ppermute | solution.py:27
  52.5 1.2 %collective-permute-start.14 = (f32[3584]{0:T(1024)S(1)}, f32[3584]{0:T(1024)S(1)}, u32[]{:S(2)}, u32[]{:S(2)}) collective-permute-start(f32[3584]{0:T(1024)S(1)} %sub.64), channel_id=1, source_target_pairs={{0,1},{1,0},{2,3},{3,2},{4,5},{5,4},{6,7},{7,6},{8,9},{9,8},{10,11... | collective-permute-start | bytes 43016 | tf_op jit(solution)/shard_map/ppermute | solution.py:27

commit v3 on v2

v3 whole, which is shorter than its diff:
```python
import math

import jax
import jax.numpy as jnp
from jax import lax
from jax.experimental import pallas as pl
from jax.experimental.pallas import tpu as pltpu
from jax.sharding import PartitionSpec as P

EPSILON = 0.5
SPARSITY = 0.5
F32 = jnp.float32
BF16 = jnp.bfloat16
LIMIT = 12 * 1024 * 1024


def opened(ids, offset, width):
    latent = offset + lax.broadcasted_iota(jnp.int32, (1, 1, width), 2)
    return jnp.any(ids[:, :, None] == latent, axis=1)


def dot(a, b):
    return jnp.dot(a, b, preferred_element_type=F32)


def dot_last(a, b):
    return lax.dot_general(a, b, (((1,), (1,)), ((), ())), preferred_element_type=F32)


def dot_rows(a, b):
    return lax.dot_general(a, b, (((0,), (0,)), ((), ())), preferred_element_type=F32)


def forward_kernel(
    block, received, first, decoder_bias, gates, encoder, encoder_other, bias, bias_other, decoder,
    decoder_other, rows, centered, preact, partial
):
    width = encoder.shape[1]
    lead = first[0:1, 0:1] > 0.0
    here, there = block[...].astype(F32), received[...].astype(F32)
    every = jnp.concatenate([jnp.where(lead, here, there), jnp.where(lead, there, here)], axis=0)
    rows[...] = every.astype(BF16)
    shifted = (every - decoder_bias[...]).astype(BF16)
    centered[...] = shifted
    mine = dot(shifted, encoder[...]) + bias[...]
    other = dot(shifted, encoder_other[...]) + bias_other[...]
    preact[...] = mine
    codes = (mine * gates[:, :width]).astype(BF16)
    codes_other = (other * gates[:, width:]).astype(BF16)
    partial[...] = (dot(codes, decoder[...]) + dot(codes_other, decoder_other[...])).astype(BF16)


def backward_kernel(
    low, received, rows, decoder_bias, gates, encoder, encoder_other, decoder, decoder_other,
    errors, error_sum, part
):
    width = encoder.shape[1]
    total = low[...].astype(F32) + received[...].astype(F32)
    found = (total + decoder_bias[...] - rows[...].astype(F32)).astype(BF16)
    errors[...] = found
    error_sum[...] = jnp.sum(found.astype(F32), axis=0, keepdims=True)

    def product(gate, decoder_block, encoder_block):
        grad = jnp.sum(dot_last(found, decoder_block[...]) * gate, axis=0, keepdims=True)
        upper = grad.astype(BF16).astype(F32)
        row = lax.broadcasted_iota(jnp.int32, (8, width), 0)
        both = jnp.where(row == 0, upper, jnp.where(row == 1, grad - upper, 0.0))
        return dot_last(both.astype(BF16), encoder_block[...])

    both = product(gates[:, :width], decoder, encoder)
    both += product(gates[:, width:], decoder_other, encoder_other)
    part[...] = jnp.sum(both, axis=0, keepdims=True)


def stage_kernel(*refs):
    half = (len(refs) - 1) // 2
    copies = [
        pltpu.make_async_copy(
            source, target if len(source.shape) > 1 else target.at[0], refs[-1].at[i]
        )
        for i, (source, target) in enumerate(zip(refs[:half], refs[half:-1]))
    ]
    for copy in copies:
        copy.start()
    for copy in copies:
        copy.wait()


def stage(*arrays):
    shapes = [array.shape if array.ndim > 1 else (1,) + array.shape for array in arrays]
    return pl.pallas_call(
        stage_kernel,
        in_specs=[pl.BlockSpec(memory_space=pltpu.HBM)] * len(arrays),
        out_specs=[pl.BlockSpec(memory_space=pltpu.VMEM)] * len(arrays),
        out_shape=[pltpu.VMEM(shape, array.dtype) for shape, array in zip(shapes, arrays)],
        scratch_shapes=[pltpu.SemaphoreType.DMA((len(arrays),))],
        compiler_params=pltpu.CompilerParams(vmem_limit_bytes=LIMIT),
    )(*[pltpu.with_memory_space_constraint(array, pltpu.HBM) for array in arrays])


def near(kernel, arrays, outs):
    whole = pl.BlockSpec(memory_space=pltpu.VMEM)
    return pl.pallas_call(
        kernel,
        in_specs=[whole] * len(arrays),
        out_specs=[whole] * len(outs),
        out_shape=[pltpu.VMEM(shape, dtype) for shape, dtype in outs],
        compiler_params=pltpu.CompilerParams(vmem_limit_bytes=LIMIT),
    )(*[pltpu.with_memory_space_constraint(array, pltpu.VMEM) for array in arrays])


def on_device(
    count, rows_in, active_ids, encoder_weight, encoder_bias, threshold, decoder_weight, decoder_bias
):
    width = encoder_weight.shape[1]
    me = lax.axis_index("latent")
    core = me & 1

    def swap(array, bit):
        return lax.ppermute(array, "latent", [(i, i ^ bit) for i in range(count)])

    hops = []
    bit = 2
    while bit < count:
        hops.append(bit)
        bit *= 2

    encoder_other = swap(encoder_weight, 1)
    decoder_other = swap(decoder_weight, 1)
    bias_other = swap(encoder_bias[None], 1)

    per_device, depth = rows_in.shape
    block, bias_row = stage(rows_in, decoder_bias)
    for bit in hops[:-1]:
        other = swap(rows_in if bit == hops[0] else block, bit)
        low = jnp.concatenate([block, other], axis=0)
        high = jnp.concatenate([other, block], axis=0)
        block = jnp.where((me & bit) == 0, low, high)
    weights = (encoder_weight, decoder_weight, encoder_bias)
    block, weights = lax.optimization_barrier((block, weights))
    received = swap(block, hops[-1])
    encoder_near, decoder_near, encoder_row = stage(*weights)
    first = jnp.full((1, width), jnp.where((me & hops[-1]) == 0, 1.0, 0.0), F32)
    half_rows = 2 * block.shape[0]

    ids = active_ids.reshape(half_rows // per_device, 2, per_device, active_ids.shape[1])
    ids_mine = lax.dynamic_index_in_dim(ids, core, 1, keepdims=False).reshape(half_rows, -1)
    ids_other = lax.dynamic_index_in_dim(ids, 1 - core, 1, keepdims=False).reshape(half_rows, -1)

    def center(part):
        return (part.astype(F32) - bias_row).astype(BF16)

    gate_mine = opened(ids_mine, me * width, width)
    gates = jnp.concatenate([gate_mine, opened(ids_mine, (me ^ 1) * width, width)], axis=1)
    gates = gates.astype(F32)
    rows, centered, preact_mine, partial = near(
        forward_kernel,
        (block, received, first, bias_row, gates, encoder_near, encoder_other, encoder_row, bias_other,
         decoder_near, decoder_other),
        (
            ((half_rows, depth), BF16),
            ((half_rows, depth), BF16),
            ((half_rows, width), F32),
            ((half_rows, depth), BF16),
        ),
    )

    rows_other = swap(rows, 1)
    centered_other = center(rows_other)
    gate_rest = opened(ids_other, me * width, width)
    preact_rest = dot(centered_other, encoder_near) + encoder_row
    preact = jnp.concatenate([preact_mine, preact_rest])
    gate = jnp.concatenate([gate_mine, gate_rest])
    every_centered = jnp.concatenate([centered, centered_other])
    codes = jnp.where(gate, preact, 0.0).astype(BF16)

    for bit in hops[:-1]:
        partial = partial + swap(partial, bit)
        partial = lax.optimization_barrier(partial)
    partial, weights = lax.optimization_barrier((partial, (encoder_weight, decoder_weight)))
    received = swap(partial, hops[-1])
    encoder_near, decoder_near = stage(*weights)
    errors, error_sum, part = near(
        backward_kernel,
        (partial, received, rows, bias_row, gates, encoder_near, encoder_other, decoder_near,
         decoder_other),
        (((half_rows, depth), BF16), ((1, depth), F32), ((1, depth), F32)),
    )
    errors_other = swap(errors, 1)

    every_error = jnp.concatenate([errors, errors_other])

    def small_outputs():
        code_grad = dot_last(every_error, decoder_near)
        distance = (preact - threshold) / EPSILON
        kernel = jnp.exp(-0.5 * distance * distance) / (EPSILON * math.sqrt(2.0 * math.pi))
        grad_threshold = jnp.sum(-threshold * code_grad * kernel - SPARSITY * kernel, axis=0)
        preact_grad = jnp.where(gate, code_grad, 0.0)
        return grad_threshold, jnp.sum(preact_grad, axis=0), preact_grad.astype(BF16)

    def decoder_output():
        return dot_rows(codes, every_error).astype(BF16)

    def encoder_output():
        return dot_rows(every_centered, small[2]).astype(BF16)

    part = part + swap(part, hops[0])
    small, part = lax.optimization_barrier((small_outputs(), part))
    part = part + swap(part, hops[1])
    grad_decoder, part = lax.optimization_barrier((decoder_output(), part))
    part = part + swap(part, hops[2])
    grad_encoder, part = lax.optimization_barrier((encoder_output(), part))
    for bit in hops[3:]:
        part = part + swap(part, bit)
    part = error_sum - part
    grad_decoder_bias = (part + swap(part, 1)).reshape(depth)
    grad_threshold, grad_encoder_bias, _ = small
    return (grad_encoder, grad_encoder_bias, grad_threshold, grad_decoder, grad_decoder_bias)


def solution(mesh):
    count = mesh.shape["latent"]

    def body(*args):
        return on_device(count, *args)

    placed = (
        P(("group", "latent"), None),
        P("group", None),
        P("group", "latent"),
        P(("group", "latent")),
        P(("group", "latent")),
        P(("group", "latent"), None),
        P("group"),
    )
    return jax.shard_map(
        body,
        mesh=mesh,
        in_specs=placed,
        out_specs=(
            P("group", "latent"),
            P(("group", "latent")),
            P(("group", "latent")),
            P(("group", "latent"), None),
            P("group"),
        ),
        check_vma=False,
    )
```

time: 54.8 us -> 50.2 us (0.916)
  Pallas kernels: 0 us -> 5.61 us
  matrix products: 8.52 us -> 3.88 us
  starting transfers between devices: 24.3 us -> 20.2 us
  other arithmetic: 3.62 us -> 1.68 us
    pallas_call x0 -> x5, Pallas kernels: none -> 5.61 us  [the longest x3 3.71 us: stage(): pl.pallas_call(stage_kernel, in_specs=[pl.BlockSpec(memory_space=pltpu.HB...]
    ppermute x15, starting transfers between devices: 24.3 us -> 20.2 us  [swap(): return lax.ppermute(array, 'latent', [(i, i ^ bit) for i in range(count)])]
    dot_general x5 -> x1, matrix products: 3.47 us -> 0.93 us  [dot_last(): lax.dot_general(a, b, (((1,), (1,)), ((), ())), preferred_element_type=F32)]
    dot_general x4 -> x1, matrix products: 2.32 us -> 0.23 us  [dot(): return jnp.dot(a, b, preferred_element_type=F32)]
    select_n x3 -> x2, other arithmetic: 1.23 us -> 0.12 us  [on_device(): block = jnp.where(me & bit == 0, low, high)]
    convert_element_type x8 -> x2, other arithmetic: 0.93 us -> 0.03 us  [the longest x1 0.02 us: center(): return (part.astype(F32) - bias_row).astype(BF16)]
  transfers between devices with their start and end apart: 15 -> 15, of which waited for: 10 -> 9; matrix products, arithmetic and copies ran while one was open for 16% -> 9% of each run, Pallas kernels for 0% -> 7%
where the time goes in v3:
time: 50.2 us; the launch traced here: 49.9 us
  starting transfers between devices  20.2 us (40%)
  waiting for transfers between devices  16.9 us (34%)
  Pallas kernels  5.61 us (11%)
  matrix products  3.88 us (8%)
  other arithmetic  1.68 us (3%)
  between operations  0.79 us (2%)
  local copies, waits for them, and re-layouts  0.74 us (1%)
    ppermute x15, starting transfers between devices, swap(): return lax.ppermute(array, 'latent', [(i, i ^ bit) for i in range(count)])  20.2 us
    ppermute x15, waiting for transfers between devices, swap(): return lax.ppermute(array, 'latent', [(i, i ^ bit) for i in range(count)])  16.9 us
    pallas_call x3, Pallas kernels, stage(): pl.pallas_call(stage_kernel, in_specs=[pl.BlockSpec(memory_space=pltpu.HB...  3.71 us
    dot_general x2, matrix products, dot_rows(): lax.dot_general(a, b, (((0,), (0,)), ((), ())), preferred_element_type=F32)  2.73 us
    pallas_call x2, Pallas kernels, near(): pl.pallas_call(kernel, in_specs=[whole] * len(arrays), out_specs=[whole]...  1.9 us
  transfers between devices with their start and end apart: 15, of which 9 were waited for; matrix products, arithmetic and copies ran while one was open for 9% of the time, Pallas kernels for 7%

profile of v3, /device:TPU:0, one launch (start us, length us, event | category | flops | bytes accessed | tf_op | source)
XLA Modules:
  0.0 49.9 jit_solution(2416657966909230828)
XLA Ops:
  0.6 0.5 %collective-permute-start.4 = (f32[1,128]{1,0:T(1,128)}, f32[1,128]{1,0:T(1,128)S(1)}, u32[]{:S(2)}, u32[]{:S(2)}) collective-permute-start(f32[1,128]{1,0:T(1,128)} %bitcast.15), channel_id=1, source_target_pairs={{0,1},{1,0},{2,3},{3,2},{4,5},{5,4},{6,7},{7,6},{8,9},{9,8},{10,11... | collective-permute-start | bytes 1544 | tf_op jit(solution)/shard_map/ppermute | solution.py:120
  1.1 2.6 %collective-permute-start = (bf16[2,3584]{1,0:T(2,128)(2,1)}, bf16[2,3584]{1,0:T(2,128)(2,1)S(1)}, u32[]{:S(2)}, u32[]{:S(2)}) collective-permute-start(bf16[2,3584]{1,0:T(2,128)(2,1)} %refs_0_.1), channel_id=1, source_target_pairs={{0,2},{1,3},{2,0},{3,1},{4,6},{5,7},{6,4},{7,5},{8,10},{9,11},{10,... | collective-permute-start | bytes 43016 | tf_op jit(solution)/shard_map/ppermute | solution.py:120
  3.7 0.2 collective-permute-start.3
  3.9 0.3 collective-permute-start.5
  4.3 0.7 %constant_dynamic-slice_fusion = (s32[8,1,2,128]{3,2,1,0:T(2,128)S(1)}, s32[8,1,2,128]{3,2,1,0:T(2,128)S(1)}) fusion(s32[8,2,2,128]{3,2,1,0:T(2,128)} %bitcast.14, s32[]{:T(128)S(6)} %select_n.40, s32[]{:T(128)S(6)} %select_n.39), kind=kLoop, calls=%fused_computation.25 | loop fusion | bytes 32776 | tf_op jit(solution)/shard_map/jit(dynamic_index_in_dim)/dynamic_slice | solution.py:148
  5.0 0.7 %shard_map.110 = (bf16[2,3584]{1,0:T(2,128)(2,1)S(1)}, f32[1,3584]{1,0:T(1,128)S(1)}) custom-call(bf16[2,3584]{1,0:T(2,128)(2,1)} %refs_0_.1, f32[3584]{0:T(1024)} %refs_1_.1), custom_call_target="tpu_custom_call" | custom-call | tf_op jit(solution)/shard_map/pallas_call | solution.py:91
  5.7 0.0 collective-permute-done
  5.7 0.1 maximum_select_fusion.1
  5.8 2.0 %collective-permute-start.1 = (bf16[4,3584]{1,0:T(4,128)(2,1)S(1)}, bf16[4,3584]{1,0:T(4,128)(2,1)S(1)}, u32[]{:S(2)}, u32[]{:S(2)}) collective-permute-start(bf16[4,3584]{1,0:T(4,128)(2,1)S(1)} %maximum_select_fusion.1), channel_id=1, source_target_pairs={{0,4},{1,5},{2,6},{3,7},{4,0},{5,1},{6,2},{7,3},{8,12},{9,13},{10,... | collective-permute-start | bytes 86024 | tf_op jit(solution)/shard_map/ppermute | solution.py:120
  7.9 0.7 %compare_reduce_fusion.2 = (pred[16,128]{1,0:T(8,128)(4,1)S(1)}, pred[16,128]{1,0:T(8,128)(4,1)S(1)}, pred[16,128]{1,0:T(8,128)(4,1)S(1)}) fusion(s32[128]{0:T(128)S(1)} %iota_add_fusion.1, s32[16,128]{1,0:T(8,128)S(1)} %bitcast.13, s32[128]{0:T(128)S(1)} %iota_add_fusion, s32[16,128]{1,0:T(8,128)S(1)} %bitcast.12), kind=kLoop, calls=%fused_computation.5 | loop fusion | flops 1566720 | bytes 23552 | tf_op jit(solution)/shard_map/reduce_or | solution.py:19
  8.6 1.2 %collective-permute-done.1 = bf16[4,3584]{1,0:T(4,128)(2,1)S(1)} collective-permute-done((bf16[4,3584]{1,0:T(4,128)(2,1)S(1)}, bf16[4,3584]{1,0:T(4,128)(2,1)S(1)}, u32[]{:S(2)}, u32[]{:S(2)}) %collective-permute-start.1) | collective-permute-done | bytes 28704 | tf_op jit(solution)/shard_map/ppermute | solution.py:120
  9.7 0.1 maximum_select_fusion.block
  9.8 3.1 %collective-permute-start.2 = (bf16[8,3584]{1,0:T(8,128)(2,1)S(1)}, bf16[8,3584]{1,0:T(8,128)(2,1)S(1)}, u32[]{:S(2)}, u32[]{:S(2)}) collective-permute-start(bf16[8,3584]{1,0:T(8,128)(2,1)S(1)} %maximum_select_fusion.block), channel_id=1, source_target_pairs={{0,8},{1,9},{2,10},{3,11},{4,12},{5,13},{6,14},{7,15},{8,0},{9,1},... | collective-permute-start | bytes 172040 | tf_op jit(solution)/shard_map/ppermute | solution.py:120
  12.9 1.5 %shard_map.111 = (bf16[3584,128]{1,0:T(8,128)(2,1)S(1)}, bf16[128,3584]{1,0:T(8,128)(2,1)S(1)}, f32[1,128]{1,0:T(1,128)S(1)}) custom-call(bf16[3584,128]{1,0:T(8,128)(2,1)} %refs_0_.3, bf16[128,3584]{1,0:T(8,128)(2,1)} %refs_1_.3, f32[128]{0:T(128)} %refs_2_), custom_call_target="tpu_custom_call" | custom-call | tf_op jit(solution)/shard_map/pallas_call | solution.py:91
  14.4 0.0 collective-permute-done.4.bias_other
  14.4 0.7 %collective-permute-done.2.received = bf16[8,3584]{1,0:T(8,128)(2,1)S(1)} collective-permute-done((bf16[8,3584]{1,0:T(8,128)(2,1)S(1)}, bf16[8,3584]{1,0:T(8,128)(2,1)S(1)}, u32[]{:S(2)}, u32[]{:S(2)}) %collective-permute-start.2) | collective-permute-done | bytes 57376 | tf_op jit(solution)/shard_map/ppermute | solution.py:120
  15.0 0.0 collective-permute-done.3.encoder_other
  15.0 0.0 collective-permute-done.5.decoder_other
  15.0 0.0 copy-start
  15.0 0.7 %shard_map.112 = (bf16[16,3584]{1,0:T(8,128)(2,1)S(1)}, bf16[16,3584]{1,0:T(8,128)(2,1)S(1)}, f32[16,128]{1,0:T(8,128)S(1)}, bf16[16,3584]{1,0:T(8,128)(2,1)S(1)}) custom-call(bf16[8,3584]{1,0:T(8,128)(2,1)S(1)} %maximum_select_fusion.block, bf16[8,3584]{1,0:T(8,128)(2,1)S(1)} %collective-permute-done.2.received, f32[1,128]{1,0:T(1,128)S(1)} %broadcast_in_dim.13.first, ...), custom_call_target="tpu_custom_call" | custom-call | tf_op jit(solution)/shard_map/pallas_call | solution.py:103
  15.8 1.9 %collective-permute-start.7 = (bf16[16,3584]{1,0:T(8,128)(2,1)S(1)}, bf16[16,3584]{1,0:T(8,128)(2,1)S(1)}, u32[]{:S(2)}, u32[]{:S(2)}) collective-permute-start(bf16[16,3584]{1,0:T(8,128)(2,1)S(1)} %get-tuple-element.45), channel_id=1, source_target_pairs={{0,2},{1,3},{2,0},{3,1},{4,6},{5,7},{6,4},{7,5},{8,10},{9,11},{10,... | collective-permute-start | bytes 344072 | tf_op jit(solution)/shard_map/ppermute | solution.py:120
  17.7 0.0 collective-permute-start.6
  17.7 0.0 copy-done
  17.7 2.9 %collective-permute-done.7 = bf16[16,3584]{1,0:T(8,128)(2,1)S(1)} collective-permute-done((bf16[16,3584]{1,0:T(8,128)(2,1)S(1)}, bf16[16,3584]{1,0:T(8,128)(2,1)S(1)}, u32[]{:S(2)}, u32[]{:S(2)}) %collective-permute-start.7) | collective-permute-done | bytes 114720 | tf_op jit(solution)/shard_map/ppermute | solution.py:120
  20.7 2.0 %collective-permute-start.8 = (bf16[16,3584]{1,0:T(8,128)(2,1)S(1)}, bf16[16,3584]{1,0:T(8,128)(2,1)S(1)}, u32[]{:S(2)}, u32[]{:S(2)}) collective-permute-start(bf16[16,3584]{1,0:T(8,128)(2,1)S(1)} %add.65), channel_id=1, source_target_pairs={{0,4},{1,5},{2,6},{3,7},{4,0},{5,1},{6,2},{7,3},{8,12},{9,13},{10,... | collective-permute-start | bytes 344072 | tf_op jit(solution)/shard_map/ppermute | solution.py:120
  22.6 0.0 collective-permute-done.6
  22.7 2.9 %collective-permute-done.8 = bf16[16,3584]{1,0:T(8,128)(2,1)S(1)} collective-permute-done((bf16[16,3584]{1,0:T(8,128)(2,1)S(1)}, bf16[16,3584]{1,0:T(8,128)(2,1)S(1)}, u32[]{:S(2)}, u32[]{:S(2)}) %collective-permute-start.8) | collective-permute-done | bytes 114720 | tf_op jit(solution)/shard_map/ppermute | solution.py:120
  25.6 4.0 %collective-permute-start.9 = (bf16[16,3584]{1,0:T(8,128)(2,1)S(1)}, bf16[16,3584]{1,0:T(8,128)(2,1)S(1)}, u32[]{:S(2)}, u32[]{:S(2)}) collective-permute-start(bf16[16,3584]{1,0:T(8,128)(2,1)S(1)} %add.66.low), channel_id=1, source_target_pairs={{0,8},{1,9},{2,10},{3,11},{4,12},{5,13},{6,14},{7,15},{8,0},{9,1},... | collective-permute-start | bytes 344072 | tf_op jit(solution)/shard_map/ppermute | solution.py:120
  29.6 0.2 convolution_add_fusion
  29.8 1.5 %shard_map.113 = (bf16[3584,128]{1,0:T(8,128)(2,1)S(1)}, bf16[128,3584]{1,0:T(8,128)(2,1)S(1)}) custom-call(bf16[3584,128]{1,0:T(8,128)(2,1)} %refs_0_.3, bf16[128,3584]{1,0:T(8,128)(2,1)} %refs_1_.3), custom_call_target="tpu_custom_call" | custom-call | tf_op jit(solution)/shard_map/pallas_call | solution.py:91
  31.3 2.3 %collective-permute-done.9.received = bf16[16,3584]{1,0:T(8,128)(2,1)S(1)} collective-permute-done((bf16[16,3584]{1,0:T(8,128)(2,1)S(1)}, bf16[16,3584]{1,0:T(8,128)(2,1)S(1)}, u32[]{:S(2)}, u32[]{:S(2)}) %collective-permute-start.9) | collective-permute-done | bytes 114720 | tf_op jit(solution)/shard_map/ppermute | solution.py:120
  33.6 1.2 %shard_map.114 = (bf16[16,3584]{1,0:T(8,128)(2,1)S(1)}, f32[1,3584]{1,0:T(1,128)S(1)}, f32[1,3584]{1,0:T(1,128)S(1)}) custom-call(bf16[16,3584]{1,0:T(8,128)(2,1)S(1)} %add.66.low, bf16[16,3584]{1,0:T(8,128)(2,1)S(1)} %collective-permute-done.9.received, bf16[16,3584]{1,0:T(8,128)(2,1)S(1)} %get-tuple-element.44.rows, ...), custom_call_target="tpu_custom_call" | custom-call | tf_op jit(solution)/shard_map/pallas_call | solution.py:103
  34.7 0.9 %collective-permute-start.11 = (f32[1,3584]{1,0:T(1,128)S(1)}, f32[1,3584]{1,0:T(1,128)S(1)}, u32[]{:S(2)}, u32[]{:S(2)}) collective-permute-start(f32[1,3584]{1,0:T(1,128)S(1)} %get-tuple-element.53), channel_id=1, source_target_pairs={{0,2},{1,3},{2,0},{3,1},{4,6},{5,7},{6,4},{7,5},{8,10},{9,11},{10,... | collective-permute-start | bytes 43016 | tf_op jit(solution)/shard_map/ppermute | solution.py:120
  35.6 0.0 collective-permute-start.10
  35.6 2.9 %collective-permute-done.11 = f32[1,3584]{1,0:T(1,128)S(1)} collective-permute-done((f32[1,3584]{1,0:T(1,128)S(1)}, f32[1,3584]{1,0:T(1,128)S(1)}, u32[]{:S(2)}, u32[]{:S(2)}) %collective-permute-start.11) | collective-permute-done | bytes 14368 | tf_op jit(solution)/shard_map/ppermute | solution.py:120
  38.5 0.0 collective-permute-done.10
  38.6 0.9 %select_reduce_fusion = (f32[128]{0:T(128)}, f32[128]{0:T(128)}, bf16[32,128]{1,0:T(8,128)(2,1)S(1)}) fusion(pred[16,128]{1,0:T(8,128)(4,1)S(1)} %get-tuple-element.67, pred[16,128]{1,0:T(8,128)(4,1)S(1)} %get-tuple-element.65, f32[128]{0:T(128)S(1)} %copy-done, f32[16,128]{1,0:T(8,128)S(1)} %convolution_add_fusion, f32[16,128]{1,0:T(8,128)S(1)} %get-tuple-element.52, ...), kind=kOutput, calls=%fused_computation.19 | convolution fusion | flops 29421312 | bytes 1177600 | tf_op jit(solution)/shard_map/dot_general | solution.py:27
  39.5 0.6 %collective-permute-start.12 = (f32[1,3584]{1,0:T(1,128)S(1)}, f32[1,3584]{1,0:T(1,128)S(1)}, u32[]{:S(2)}, u32[]{:S(2)}) collective-permute-start(f32[1,3584]{1,0:T(1,128)S(1)} %add.71), channel_id=1, source_target_pairs={{0,4},{1,5},{2,6},{3,7},{4,0},{5,1},{6,2},{7,3},{8,12},{9,13},{10,... | collective-permute-start | bytes 43016 | tf_op jit(solution)/shard_map/ppermute | solution.py:120
  40.1 1.3 %convolution_convert_fusion = bf16[128,3584]{1,0:T(8,128)(2,1)} fusion(bf16[32,3584]{1,0:T(8,128)(2,1)S(1)} %constant_dynamic-update-slice_fusion, f32[16,128]{1,0:T(8,128)S(1)} %convolution_add_fusion, f32[16,128]{1,0:T(8,128)S(1)} %get-tuple-element.52, pred[16,128]{1,0:T(8,128)(4,1)S(1)} %get-tuple-element.67, pred[16,128]{1,0:T(8,128)(4,1)S(1)} %get-tuple-element.65), kind=kOutput, calls=%fused_computation | convolution fusion | flops 29843456 | bytes 1167360 | tf_op jit(solution)/shard_map/dot_general | solution.py:31
  41.5 1.8 %collective-permute-done.12 = f32[1,3584]{1,0:T(1,128)S(1)} collective-permute-done((f32[1,3584]{1,0:T(1,128)S(1)}, f32[1,3584]{1,0:T(1,128)S(1)}, u32[]{:S(2)}, u32[]{:S(2)}) %collective-permute-start.12) | collective-permute-done | bytes 14368 | tf_op jit(solution)/shard_map/ppermute | solution.py:120
  43.2 2.0 %collective-permute-start.13 = (f32[1,3584]{1,0:T(1,128)S(1)}, f32[1,3584]{1,0:T(1,128)S(1)}, u32[]{:S(2)}, u32[]{:S(2)}) collective-permute-start(f32[1,3584]{1,0:T(1,128)S(1)} %add.72), channel_id=1, source_target_pairs={{0,8},{1,9},{2,10},{3,11},{4,12},{5,13},{6,14},{7,15},{8,0},{9,1},... | collective-permute-start | bytes 43016 | tf_op jit(solution)/shard_map/ppermute | solution.py:120
  45.3 1.4 %convolution_convert_fusion.1 = bf16[3584,128]{1,0:T(8,128)(2,1)} fusion(bf16[32,128]{1,0:T(8,128)(2,1)S(1)} %select_convert_fusion.1, bf16[16,3584]{1,0:T(8,128)(2,1)S(1)} %subtract_convert_fusion, bf16[16,3584]{1,0:T(8,128)(2,1)S(1)} %get-tuple-element.43), kind=kOutput, calls=%fused_computation.1 | convolution fusion | flops 30277632 | bytes 1155072 | tf_op jit(solution)/shard_map/dot_general | solution.py:31
  46.7 1.3 %collective-permute-done.13 = f32[1,3584]{1,0:T(1,128)S(1)} collective-permute-done((f32[1,3584]{1,0:T(1,128)S(1)}, f32[1,3584]{1,0:T(1,128)S(1)}, u32[]{:S(2)}, u32[]{:S(2)}) %collective-permute-start.13) | collective-permute-done | bytes 14368 | tf_op jit(solution)/shard_map/ppermute | solution.py:120
  48.0 0.1 collective-permute-start.14
  48.0 1.2 %collective-permute-done.14 = f32[1,3584]{1,0:T(1,128)S(1)} collective-permute-done((f32[1,3584]{1,0:T(1,128)S(1)}, f32[1,3584]{1,0:T(1,128)S(1)}, u32[]{:S(2)}, u32[]{:S(2)}) %collective-permute-start.14) | collective-permute-done | bytes 14368 | tf_op jit(solution)/shard_map/ppermute | solution.py:120
  49.2 0.6 %add_reduce_fusion = f32[3584]{0:T(1024)} fusion(f32[1,3584]{1,0:T(1,128)S(1)} %sub.34, f32[1,3584]{1,0:T(1,128)S(1)} %collective-permute-done.14), kind=kLoop, calls=%fused_computation.17 | loop fusion | flops 3584 | bytes 43008 | tf_op jit(solution)/shard_map/add | solution.py:216
  (16 shorter events, 0.2 us)
Async XLA Ops:
  0.6 13.7 %collective-permute-start.4 = (f32[1,128]{1,0:T(1,128)}, f32[1,128]{1,0:T(1,128)S(1)}, u32[]{:S(2)}, u32[]{:S(2)}) collective-permute-start(f32[1,128]{1,0:T(1,128)} %bitcast.15), channel_id=1, source_target_pairs={{0,1},{1,0},{2,3},{3,2},{4,5},{5,4},{6,7},{7,6},{8,9},{9,8},{10,11... | collective-permute-start | bytes 1544 | tf_op jit(solution)/shard_map/ppermute | solution.py:120
  1.1 4.6 %collective-permute-start = (bf16[2,3584]{1,0:T(2,128)(2,1)}, bf16[2,3584]{1,0:T(2,128)(2,1)S(1)}, u32[]{:S(2)}, u32[]{:S(2)}) collective-permute-start(bf16[2,3584]{1,0:T(2,128)(2,1)} %refs_0_.1), channel_id=1, source_target_pairs={{0,2},{1,3},{2,0},{3,1},{4,6},{5,7},{6,4},{7,5},{8,10},{9,11},{10,... | collective-permute-start | bytes 43016 | tf_op jit(solution)/shard_map/ppermute | solution.py:120
  3.7 11.3 %collective-permute-start.3 = (bf16[3584,128]{1,0:T(8,128)(2,1)}, bf16[3584,128]{1,0:T(8,128)(2,1)S(1)}, u32[]{:S(2)}, u32[]{:S(2)}) collective-permute-start(bf16[3584,128]{1,0:T(8,128)(2,1)} %refs_0_.3), channel_id=1, source_target_pairs={{0,1},{1,0},{2,3},{3,2},{4,5},{5,4},{6,7},{7,6},{8,9},{9,8},{10,11... | collective-permute-start | bytes 2752520 | tf_op jit(solution)/shard_map/ppermute | solution.py:120
  3.9 11.1 %collective-permute-start.5 = (bf16[128,3584]{1,0:T(8,128)(2,1)}, bf16[128,3584]{1,0:T(8,128)(2,1)S(1)}, u32[]{:S(2)}, u32[]{:S(2)}) collective-permute-start(bf16[128,3584]{1,0:T(8,128)(2,1)} %refs_1_.3), channel_id=1, source_target_pairs={{0,1},{1,0},{2,3},{3,2},{4,5},{5,4},{6,7},{7,6},{8,9},{9,8},{10,11... | collective-permute-start | bytes 2752520 | tf_op jit(solution)/shard_map/ppermute | solution.py:120
  5.8 3.9 %collective-permute-start.1 = (bf16[4,3584]{1,0:T(4,128)(2,1)S(1)}, bf16[4,3584]{1,0:T(4,128)(2,1)S(1)}, u32[]{:S(2)}, u32[]{:S(2)}) collective-permute-start(bf16[4,3584]{1,0:T(4,128)(2,1)S(1)} %maximum_select_fusion.1), channel_id=1, source_target_pairs={{0,4},{1,5},{2,6},{3,7},{4,0},{5,1},{6,2},{7,3},{8,12},{9,13},{10,... | collective-permute-start | bytes 86024 | tf_op jit(solution)/shard_map/ppermute | solution.py:120
  9.8 5.2 %collective-permute-start.2 = (bf16[8,3584]{1,0:T(8,128)(2,1)S(1)}, bf16[8,3584]{1,0:T(8,128)(2,1)S(1)}, u32[]{:S(2)}, u32[]{:S(2)}) collective-permute-start(bf16[8,3584]{1,0:T(8,128)(2,1)S(1)} %maximum_select_fusion.block), channel_id=1, source_target_pairs={{0,8},{1,9},{2,10},{3,11},{4,12},{5,13},{6,14},{7,15},{8,0},{9,1},... | collective-permute-start | bytes 172040 | tf_op jit(solution)/shard_map/ppermute | solution.py:120
  15.0 2.7 %copy-start = (f32[128]{0:T(128)S(1)}, f32[128]{0:T(128)}, u32[]{:S(2)}) copy-start(f32[128]{0:T(128)} %param.11) | copy-start | bytes 1540
  15.8 4.8 %collective-permute-start.7 = (bf16[16,3584]{1,0:T(8,128)(2,1)S(1)}, bf16[16,3584]{1,0:T(8,128)(2,1)S(1)}, u32[]{:S(2)}, u32[]{:S(2)}) collective-permute-start(bf16[16,3584]{1,0:T(8,128)(2,1)S(1)} %get-tuple-element.45), channel_id=1, source_target_pairs={{0,2},{1,3},{2,0},{3,1},{4,6},{5,7},{6,4},{7,5},{8,10},{9,11},{10,... | collective-permute-start | bytes 344072 | tf_op jit(solution)/shard_map/ppermute | solution.py:120
  17.7 5.0 %collective-permute-start.6 = (bf16[16,3584]{1,0:T(8,128)(2,1)S(1)}, bf16[16,3584]{1,0:T(8,128)(2,1)S(1)}, u32[]{:S(2)}, u32[]{:S(2)}) collective-permute-start(bf16[16,3584]{1,0:T(8,128)(2,1)S(1)} %get-tuple-element.44.rows), channel_id=1, source_target_pairs={{0,1},{1,0},{2,3},{3,2},{4,5},{5,4},{6,7},{7,6},{8,9},{9,8},{10,11... | collective-permute-start | bytes 344072 | tf_op jit(solution)/shard_map/ppermute | solution.py:120
  20.7 4.9 %collective-permute-start.8 = (bf16[16,3584]{1,0:T(8,128)(2,1)S(1)}, bf16[16,3584]{1,0:T(8,128)(2,1)S(1)}, u32[]{:S(2)}, u32[]{:S(2)}) collective-permute-start(bf16[16,3584]{1,0:T(8,128)(2,1)S(1)} %add.65), channel_id=1, source_target_pairs={{0,4},{1,5},{2,6},{3,7},{4,0},{5,1},{6,2},{7,3},{8,12},{9,13},{10,... | collective-permute-start | bytes 344072 | tf_op jit(solution)/shard_map/ppermute | solution.py:120
  25.6 8.0 %collective-permute-start.9 = (bf16[16,3584]{1,0:T(8,128)(2,1)S(1)}, bf16[16,3584]{1,0:T(8,128)(2,1)S(1)}, u32[]{:S(2)}, u32[]{:S(2)}) collective-permute-start(bf16[16,3584]{1,0:T(8,128)(2,1)S(1)} %add.66.low), channel_id=1, source_target_pairs={{0,8},{1,9},{2,10},{3,11},{4,12},{5,13},{6,14},{7,15},{8,0},{9,1},... | collective-permute-start | bytes 344072 | tf_op jit(solution)/shard_map/ppermute | solution.py:120
  34.7 3.8 %collective-permute-start.11 = (f32[1,3584]{1,0:T(1,128)S(1)}, f32[1,3584]{1,0:T(1,128)S(1)}, u32[]{:S(2)}, u32[]{:S(2)}) collective-permute-start(f32[1,3584]{1,0:T(1,128)S(1)} %get-tuple-element.53), channel_id=1, source_target_pairs={{0,2},{1,3},{2,0},{3,1},{4,6},{5,7},{6,4},{7,5},{8,10},{9,11},{10,... | collective-permute-start | bytes 43016 | tf_op jit(solution)/shard_map/ppermute | solution.py:120
  35.6 2.9 %collective-permute-start.10 = (bf16[16,3584]{1,0:T(8,128)(2,1)S(1)}, bf16[16,3584]{1,0:T(8,128)(2,1)S(1)}, u32[]{:S(2)}, u32[]{:S(2)}) collective-permute-start(bf16[16,3584]{1,0:T(8,128)(2,1)S(1)} %get-tuple-element.51), channel_id=1, source_target_pairs={{0,1},{1,0},{2,3},{3,2},{4,5},{5,4},{6,7},{7,6},{8,9},{9,8},{10,11... | collective-permute-start | bytes 344072 | tf_op jit(solution)/shard_map/ppermute | solution.py:120
  39.5 3.7 %collective-permute-start.12 = (f32[1,3584]{1,0:T(1,128)S(1)}, f32[1,3584]{1,0:T(1,128)S(1)}, u32[]{:S(2)}, u32[]{:S(2)}) collective-permute-start(f32[1,3584]{1,0:T(1,128)S(1)} %add.71), channel_id=1, source_target_pairs={{0,4},{1,5},{2,6},{3,7},{4,0},{5,1},{6,2},{7,3},{8,12},{9,13},{10,... | collective-permute-start | bytes 43016 | tf_op jit(solution)/shard_map/ppermute | solution.py:120
  43.2 4.7 %collective-permute-start.13 = (f32[1,3584]{1,0:T(1,128)S(1)}, f32[1,3584]{1,0:T(1,128)S(1)}, u32[]{:S(2)}, u32[]{:S(2)}) collective-permute-start(f32[1,3584]{1,0:T(1,128)S(1)} %add.72), channel_id=1, source_target_pairs={{0,8},{1,9},{2,10},{3,11},{4,12},{5,13},{6,14},{7,15},{8,0},{9,1},... | collective-permute-start | bytes 43016 | tf_op jit(solution)/shard_map/ppermute | solution.py:120
  48.0 1.2 %collective-permute-start.14 = (f32[1,3584]{1,0:T(1,128)S(1)}, f32[1,3584]{1,0:T(1,128)S(1)}, u32[]{:S(2)}, u32[]{:S(2)}) collective-permute-start(f32[1,3584]{1,0:T(1,128)S(1)} %sub.34), channel_id=1, source_target_pairs={{0,1},{1,0},{2,3},{3,2},{4,5},{5,4},{6,7},{7,6},{8,9},{9,8},{10,11... | collective-permute-start | bytes 43016 | tf_op jit(solution)/shard_map/ppermute | solution.py:120

commit v4 on v3

v4 whole, which is shorter than its diff:
```python
import math

import jax
import jax.numpy as jnp
from jax import lax
from jax.experimental import pallas as pl
from jax.experimental.pallas import tpu as pltpu
from jax.sharding import PartitionSpec as P

EPSILON = 0.5
SPARSITY = 0.5
F32 = jnp.float32
BF16 = jnp.bfloat16
LIMIT = 12 * 1024 * 1024


def opened(ids, offset, width):
    latent = offset + lax.broadcasted_iota(jnp.int32, (1, 1, width), 2)
    return jnp.any(ids[:, :, None] == latent, axis=1)


def dot(a, b):
    return jnp.dot(a, b, preferred_element_type=F32)


def dot_last(a, b):
    return lax.dot_general(a, b, (((1,), (1,)), ((), ())), preferred_element_type=F32)


def dot_rows(a, b):
    return lax.dot_general(a, b, (((0,), (0,)), ((), ())), preferred_element_type=F32)


def forward_kernel(
    rows, decoder_bias, gates, encoder, encoder_other, bias, bias_other, decoder, decoder_other,
    preact, partial
):
    width = encoder.shape[1]
    centered = (rows[...].astype(F32) - decoder_bias[...]).astype(BF16)
    mine = dot(centered, encoder[...]) + bias[...]
    other = dot(centered, encoder_other[...]) + bias_other[...]
    preact[...] = mine
    codes = (mine * gates[:, :width]).astype(BF16)
    codes_other = (other * gates[:, width:]).astype(BF16)
    partial[...] = (dot(codes, decoder[...]) + dot(codes_other, decoder_other[...])).astype(BF16)


def backward_kernel(
    low, low_received, rows, gates, high, high_received, rows_far, gates_far, decoder_bias,
    encoder, encoder_other, decoder, decoder_other, errors, sums
):
    width = encoder.shape[1]

    def error(total, received, block):
        total = total[...].astype(F32) + received[...].astype(F32)
        return (total + decoder_bias[...] - block[...].astype(F32)).astype(BF16).astype(F32)

    near_part = error(low, low_received, rows)
    far_part = error(high, high_received, rows_far)
    sums[0:1, :] = jnp.sum(near_part, axis=0, keepdims=True) + jnp.sum(
        far_part, axis=0, keepdims=True
    )
    found = jnp.concatenate([near_part, far_part], axis=0).astype(BF16)
    errors[...] = found
    gate = jnp.concatenate([gates[...], gates_far[...]], axis=0)

    def product(gate, decoder_block, encoder_block):
        grad = jnp.sum(dot_last(found, decoder_block[...]) * gate, axis=0, keepdims=True)
        upper = grad.astype(BF16).astype(F32)
        row = lax.broadcasted_iota(jnp.int32, (8, width), 0)
        both = jnp.where(row == 0, upper, jnp.where(row == 1, grad - upper, 0.0))
        return dot_last(both.astype(BF16), encoder_block[...])

    both = product(gate[:, :width], decoder, encoder)
    both += product(gate[:, width:], decoder_other, encoder_other)
    sums[1:2, :] = jnp.sum(both, axis=0, keepdims=True)


def size(array):
    return array.size * array.dtype.itemsize


def cost(moved):
    return pl.CostEstimate(flops=0, bytes_accessed=moved, transcendentals=0)


def stage_kernel(*refs):
    half = (len(refs) - 1) // 2
    copies = [
        pltpu.make_async_copy(
            source, target if len(source.shape) > 1 else target.at[0], refs[-1].at[i]
        )
        for i, (source, target) in enumerate(zip(refs[:half], refs[half:-1]))
    ]
    for copy in copies:
        copy.start()
    for copy in copies:
        copy.wait()


def stage(*arrays):
    shapes = [array.shape if array.ndim > 1 else (1,) + array.shape for array in arrays]
    return pl.pallas_call(
        stage_kernel,
        in_specs=[pl.BlockSpec(memory_space=pltpu.HBM)] * len(arrays),
        out_specs=[pl.BlockSpec(memory_space=pltpu.VMEM)] * len(arrays),
        out_shape=[pltpu.VMEM(shape, array.dtype) for shape, array in zip(shapes, arrays)],
        scratch_shapes=[pltpu.SemaphoreType.DMA((len(arrays),))],
        cost_estimate=cost(2 * sum(size(array) for array in arrays)),
        compiler_params=pltpu.CompilerParams(vmem_limit_bytes=LIMIT),
    )(*[pltpu.with_memory_space_constraint(array, pltpu.HBM) for array in arrays])


def near(kernel, arrays, outs):
    whole = pl.BlockSpec(memory_space=pltpu.VMEM)
    return pl.pallas_call(
        kernel,
        in_specs=[whole] * len(arrays),
        out_specs=[whole] * len(outs),
        out_shape=[pltpu.VMEM(shape, dtype) for shape, dtype in outs],
        cost_estimate=cost(sum(size(array) for array in arrays)),
        compiler_params=pltpu.CompilerParams(vmem_limit_bytes=LIMIT),
    )(*[pltpu.with_memory_space_constraint(array, pltpu.VMEM) for array in arrays])


def after(first, array):
    return lax.optimization_barrier((first, array))[1]


def on_device(
    count, rows_in, active_ids, encoder_weight, encoder_bias, threshold, decoder_weight, decoder_bias
):
    width = encoder_weight.shape[1]
    me = lax.axis_index("latent")
    core = me & 1

    def swap(array, bit):
        return lax.ppermute(array, "latent", [(i, i ^ bit) for i in range(count)])

    hops = []
    bit = 2
    while bit < count:
        hops.append(bit)
        bit *= 2

    encoder_other = swap(encoder_weight, 1)
    decoder_other = swap(decoder_weight, 1)
    bias_other = swap(encoder_bias[None], 1)

    per_device, depth = rows_in.shape
    block, bias_row = stage(rows_in, decoder_bias)
    for bit in hops[:-1]:
        if bit == hops[-2]:
            weights = (encoder_weight, decoder_weight, encoder_bias)
            block, weights = lax.optimization_barrier((block, weights))
        other = swap(rows_in if bit == hops[0] else block, bit)
        low = jnp.concatenate([block, other], axis=0)
        high = jnp.concatenate([other, block], axis=0)
        block = jnp.where((me & bit) == 0, low, high)
    encoder_near, decoder_near, encoder_row = stage(*weights)
    block, encoder_near, decoder_near, encoder_row = lax.optimization_barrier(
        (block, encoder_near, decoder_near, encoder_row)
    )
    rows = block
    rows_far = swap(block, hops[-1])
    half_rows = rows.shape[0]

    ids = active_ids.reshape(2, half_rows // per_device, 2, per_device, active_ids.shape[1])
    side = jnp.where((me & hops[-1]) == 0, 0, 1)

    def listed(half, part):
        one = lax.dynamic_index_in_dim(ids, half, 0, keepdims=False)
        one = lax.dynamic_index_in_dim(one, part, 1, keepdims=False)
        return one.reshape(half_rows, -1)

    def center(part):
        return (part.astype(F32) - bias_row).astype(BF16)

    lists = jnp.concatenate([listed(side, core), listed(1 - side, core)])
    lists_other = jnp.concatenate([listed(side, 1 - core), listed(1 - side, 1 - core)])
    gate_mine = opened(lists, me * width, width)
    gates = jnp.concatenate([gate_mine, opened(lists, (me ^ 1) * width, width)], axis=1)
    gates = gates.astype(F32)
    gates, gates_far = gates[:half_rows], gates[half_rows:]

    def forward(part, gate):
        return near(
            forward_kernel,
            (part, bias_row, gate, encoder_near, encoder_other, encoder_row, bias_other,
             decoder_near, decoder_other),
            (((half_rows, width), F32), ((half_rows, depth), BF16)),
        )

    preact_near, low = forward(rows, gates)
    preact_far, high = forward(after(low, rows_far), gates_far)
    every_row = jnp.concatenate([rows, after(high, rows_far)])
    for bit in hops[:-1]:
        low, high_received = lax.optimization_barrier(low + swap(low, bit)), swap(high, bit)
        high = lax.optimization_barrier(high + after(low, high_received))
    high_received = swap(low, hops[-1])
    high, weights = lax.optimization_barrier((high, (encoder_weight, decoder_weight)))
    low_received = swap(high, hops[-1])
    encoder_near, decoder_near = stage(*weights)

    rows_other = swap(every_row, 1)
    centered_other = center(rows_other)
    gate_rest = opened(lists_other, me * width, width)
    preact_rest = dot(centered_other, encoder_weight) + encoder_bias
    preact = jnp.concatenate([preact_near, preact_far, preact_rest])
    gate = jnp.concatenate([gate_mine, gate_rest])
    every_centered = jnp.concatenate([center(every_row), centered_other])
    codes = jnp.where(gate, preact, 0.0).astype(BF16)

    errors, sums = near(
        backward_kernel,
        (low, low_received, rows, gates, high, high_received, rows_far, gates_far, bias_row,
         encoder_near, encoder_other, decoder_near, decoder_other),
        (((2 * half_rows, depth), BF16), ((2, depth), F32)),
    )
    errors_other = swap(errors, 1)
    sums = sums + swap(sums, 1)
    errors_other, sums = lax.optimization_barrier((errors_other, sums))
    part = sums[1:]

    every_error = jnp.concatenate([errors, errors_other])

    def small_outputs():
        code_grad = dot_last(every_error, decoder_near)
        distance = (preact - threshold) / EPSILON
        kernel = jnp.exp(-0.5 * distance * distance) / (EPSILON * math.sqrt(2.0 * math.pi))
        grad_threshold = jnp.sum(-threshold * code_grad * kernel - SPARSITY * kernel, axis=0)
        preact_grad = jnp.where(gate, code_grad, 0.0)
        return grad_threshold, jnp.sum(preact_grad, axis=0), preact_grad.astype(BF16)

    def decoder_output():
        return dot_rows(codes, every_error).astype(BF16)

    def encoder_output():
        return dot_rows(every_centered, small[2]).astype(BF16)

    part = part + swap(part, hops[0])
    small, part = lax.optimization_barrier((small_outputs(), part))
    part = part + swap(part, hops[1])
    grad_decoder, part = lax.optimization_barrier((decoder_output(), part))
    for bit in hops[2:]:
        part = part + swap(part, bit)
    grad_decoder_bias = (sums[:1] - part).reshape(depth)
    grad_encoder = encoder_output()
    grad_threshold, grad_encoder_bias, _ = small
    return (grad_encoder, grad_encoder_bias, grad_threshold, grad_decoder, grad_decoder_bias)


def solution(mesh):
    count = mesh.shape["latent"]

    def body(*args):
        return on_device(count, *args)

    placed = (
        P(("group", "latent"), None),
        P("group", None),
        P("group", "latent"),
        P(("group", "latent")),
        P(("group", "latent")),
        P(("group", "latent"), None),
        P("group"),
    )
    return jax.shard_map(
        body,
        mesh=mesh,
        in_specs=placed,
        out_specs=(
            P("group", "latent"),
            P(("group", "latent")),
            P(("group", "latent")),
            P(("group", "latent"), None),
            P("group"),
        ),
        check_vma=False,
    )
```

time: 50.2 us -> 47 us (0.936)
  waiting for transfers between devices: 16.9 us -> 10.3 us
  starting transfers between devices: 20.2 us -> 22.9 us
  Pallas kernels: 5.61 us -> 6.23 us
    ppermute x15 -> x18, waiting for transfers between devices: 16.9 us -> 10.3 us  [swap(): return lax.ppermute(array, 'latent', [(i, i ^ bit) for i in range(count)])]
    ppermute x15 -> x18, starting transfers between devices: 20.2 us -> 22.9 us  [swap(): return lax.ppermute(array, 'latent', [(i, i ^ bit) for i in range(count)])]
    add x4 -> x5, other arithmetic: 0.72 us -> 0.08 us  [the longest x2 0.03 us: on_device(): high = lax.optimization_barrier(high + after(low, high_received))]
    sub x1, other arithmetic: 0.02 us -> 0.65 us  [on_device(): grad_decoder_bias = (sums[:1] - part).reshape(depth)]
    pallas_call x2 -> x3, Pallas kernels: 1.9 us -> 2.51 us  [near(): pl.pallas_call(kernel, in_specs=[whole] * len(arrays), out_specs=[whole]...]
  transfers between devices with their start and end apart: 15 -> 18, of which waited for: 9 -> 11; matrix products, arithmetic and copies ran while one was open for 9% -> 12% of each run, Pallas kernels for 7% -> 11%
where the time goes in v4:
time: 47 us; the launch traced here: 46.7 us
  starting transfers between devices  22.9 us (49%)
  waiting for transfers between devices  10.3 us (22%)
  Pallas kernels  6.23 us (13%)
  matrix products  3.89 us (8%)
  other arithmetic  1.7 us (4%)
  between operations  0.83 us (2%)
  local copies, waits for them, and re-layouts  0.8 us (2%)
    ppermute x18, starting transfers between devices, swap(): return lax.ppermute(array, 'latent', [(i, i ^ bit) for i in range(count)])  22.9 us
    ppermute x18, waiting for transfers between devices, swap(): return lax.ppermute(array, 'latent', [(i, i ^ bit) for i in range(count)])  10.3 us
    pallas_call x3, Pallas kernels, stage(): pl.pallas_call(stage_kernel, in_specs=[pl.BlockSpec(memory_space=pltpu.HB...  3.72 us
    dot_general x2, matrix products, dot_rows(): lax.dot_general(a, b, (((0,), (0,)), ((), ())), preferred_element_type=F32)  2.73 us
    pallas_call x3, Pallas kernels, near(): pl.pallas_call(kernel, in_specs=[whole] * len(arrays), out_specs=[whole]...  2.51 us
  transfers between devices with their start and end apart: 18, of which 11 were waited for; matrix products, arithmetic and copies ran while one was open for 12% of the time, Pallas kernels for 11%

profile of v4, /device:TPU:0, one launch (start us, length us, event | category | flops | bytes accessed | tf_op | source)
XLA Modules:
  0.0 46.7 jit_solution(249105807687056302)
XLA Ops:
  0.6 3.0 %collective-permute-start = (bf16[2,3584]{1,0:T(2,128)(2,1)}, bf16[2,3584]{1,0:T(2,128)(2,1)S(1)}, u32[]{:S(2)}, u32[]{:S(2)}) collective-permute-start(bf16[2,3584]{1,0:T(2,128)(2,1)} %refs_0_.1), channel_id=1, source_target_pairs={{0,2},{1,3},{2,0},{3,1},{4,6},{5,7},{6,4},{7,5},{8,10},{9,11},{10,... | collective-permute-start | bytes 43016 | tf_op jit(solution)/shard_map/ppermute | solution.py:138
  3.7 0.0 collective-permute-start.2
  3.7 0.5 %collective-permute-start.4 = (bf16[128,3584]{1,0:T(8,128)(2,1)}, bf16[128,3584]{1,0:T(8,128)(2,1)S(1)}, u32[]{:S(2)}, u32[]{:S(2)}) collective-permute-start(bf16[128,3584]{1,0:T(8,128)(2,1)} %refs_1_.3), channel_id=1, source_target_pairs={{0,1},{1,0},{2,3},{3,2},{4,5},{5,4},{6,7},{7,6},{8,9},{9,8},{10,11... | collective-permute-start | bytes 2752520 | tf_op jit(solution)/shard_map/ppermute | solution.py:138
  4.2 0.0 collective-permute-start.3
  4.2 0.7 %constant_dynamic-slice_fusion.1 = (s32[1,4,1,2,128]{4,3,2,1,0:T(2,128)S(1)}, s32[1,4,1,2,128]{4,3,2,1,0:T(2,128)S(1)}, s32[1,4,1,2,128]{4,3,2,1,0:T(2,128)S(1)}, s32[1,4,1,2,128]{4,3,2,1,0:T(2,128)S(1)}) fusion(s32[2,4,2,2,128]{4,3,2,1,0:T(2,128)} %bitcast.12, s32[]{:T(128)S(6)} %select_n.56, s32[]{:T(128)S(6)} %select_n.62, s32[]{:T(128)S(6)} %select_n.60, ...), kind=kLoop, calls=%fused_computation.29 | loop fusion | bytes 32784 | tf_op jit(solution)/shard_map/jit(dynamic_index_in_dim)/dynamic_slice | solution.py:173
  4.9 0.7 %compare_reduce_fusion.2 = (pred[16,128]{1,0:T(8,128)(4,1)S(1)}, pred[16,128]{1,0:T(8,128)(4,1)S(1)}, pred[16,128]{1,0:T(8,128)(4,1)S(1)}) fusion(s32[128]{0:T(128)S(1)} %get-tuple-element.94, s32[16,128]{1,0:T(8,128)S(1)} %get-tuple-element.91, s32[128]{0:T(128)S(1)} %get-tuple-element.93, s32[16,128]{1,0:T(8,128)S(1)} %get-tuple-element.92), kind=kLoop, calls=%fused_computation.5 | loop fusion | flops 1566720 | bytes 23552 | tf_op jit(solution)/shard_map/reduce_or | solution.py:19
  5.7 0.8 %shard_map.110 = (bf16[2,3584]{1,0:T(2,128)(2,1)S(1)}, f32[1,3584]{1,0:T(1,128)S(1)}) custom-call(bf16[2,3584]{1,0:T(2,128)(2,1)} %refs_0_.1, f32[3584]{0:T(1024)} %refs_1_.1), custom_call_target="tpu_custom_call" | custom-call | bytes 57344 | tf_op jit(solution)/shard_map/pallas_call | solution.py:103
  6.4 0.0 collective-permute-done
  6.4 0.1 maximum_select_fusion.1
  6.5 1.6 %collective-permute-start.1 = (bf16[4,3584]{1,0:T(4,128)(2,1)S(1)}, bf16[4,3584]{1,0:T(4,128)(2,1)S(1)}, u32[]{:S(2)}, u32[]{:S(2)}) collective-permute-start(bf16[4,3584]{1,0:T(4,128)(2,1)S(1)} %maximum_select_fusion.1), channel_id=1, source_target_pairs={{0,4},{1,5},{2,6},{3,7},{4,0},{5,1},{6,2},{7,3},{8,12},{9,13},{10,... | collective-permute-start | bytes 86024 | tf_op jit(solution)/shard_map/ppermute | solution.py:138
  8.1 1.5 %shard_map.111 = (bf16[3584,128]{1,0:T(8,128)(2,1)S(1)}, bf16[128,3584]{1,0:T(8,128)(2,1)S(1)}, f32[1,128]{1,0:T(1,128)S(1)}) custom-call(bf16[3584,128]{1,0:T(8,128)(2,1)} %refs_0_.3, bf16[128,3584]{1,0:T(8,128)(2,1)} %refs_1_.3, f32[128]{0:T(128)} %refs_2_), custom_call_target="tpu_custom_call" | custom-call | bytes 3671040 | tf_op jit(solution)/shard_map/pallas_call | solution.py:103
  9.6 0.8 %collective-permute-done.1 = bf16[4,3584]{1,0:T(4,128)(2,1)S(1)} collective-permute-done((bf16[4,3584]{1,0:T(4,128)(2,1)S(1)}, bf16[4,3584]{1,0:T(4,128)(2,1)S(1)}, u32[]{:S(2)}, u32[]{:S(2)}) %collective-permute-start.1) | collective-permute-done | bytes 28704 | tf_op jit(solution)/shard_map/ppermute | solution.py:138
  10.4 0.1 maximum_select_fusion.rows
  10.5 2.7 %collective-permute-start.5 = (bf16[8,3584]{1,0:T(8,128)(2,1)S(1)}, bf16[8,3584]{1,0:T(8,128)(2,1)S(1)}, u32[]{:S(2)}, u32[]{:S(2)}) collective-permute-start(bf16[8,3584]{1,0:T(8,128)(2,1)S(1)} %maximum_select_fusion.rows), channel_id=1, source_target_pairs={{0,8},{1,9},{2,10},{3,11},{4,12},{5,13},{6,14},{7,15},{8,0},{9,1},... | collective-permute-start | bytes 172040 | tf_op jit(solution)/shard_map/ppermute | solution.py:138
  13.2 0.0 collective-permute-done.2.encoder_other
  13.2 0.0 collective-permute-done.4.decoder_other
  13.2 0.7 %shard_map.112 = (f32[8,128]{1,0:T(8,128)S(1)}, bf16[8,3584]{1,0:T(8,128)(2,1)S(1)}) custom-call(bf16[8,3584]{1,0:T(8,128)(2,1)S(1)} %maximum_select_fusion.rows, f32[1,3584]{1,0:T(1,128)S(1)} %get-tuple-element.50.decoder_bias, f32[8,256]{1,0:T(8,128)S(1)} %get-tuple-element.85.gates, bf16[3584,128]{1,0:T(8,128)(2,1)S(1)} %get-tuple-element.51.encoder, ...), custom_call_target="tpu_custom_call" | custom-call | bytes 3750912 | tf_op jit(solution)/shard_map/pallas_call | solution.py:116
  13.9 1.2 %collective-permute-start.7 = (bf16[8,3584]{1,0:T(8,128)(2,1)S(1)}, bf16[8,3584]{1,0:T(8,128)(2,1)S(1)}, u32[]{:S(2)}, u32[]{:S(2)}) collective-permute-start(bf16[8,3584]{1,0:T(8,128)(2,1)S(1)} %get-tuple-element.54), channel_id=1, source_target_pairs={{0,2},{1,3},{2,0},{3,1},{4,6},{5,7},{6,4},{7,5},{8,10},{9,11},{10,... | collective-permute-start | bytes 172040 | tf_op jit(solution)/shard_map/ppermute | solution.py:138
  15.1 0.6 %collective-permute-done.5.rows.rows_far = bf16[8,3584]{1,0:T(8,128)(2,1)S(1)} collective-permute-done((bf16[8,3584]{1,0:T(8,128)(2,1)S(1)}, bf16[8,3584]{1,0:T(8,128)(2,1)S(1)}, u32[]{:S(2)}, u32[]{:S(2)}) %collective-permute-start.5) | collective-permute-done | bytes 57376 | tf_op jit(solution)/shard_map/ppermute | solution.py:138
  15.7 0.7 %shard_map.113 = (f32[8,128]{1,0:T(8,128)S(1)}, bf16[8,3584]{1,0:T(8,128)(2,1)S(1)}) custom-call(bf16[8,3584]{1,0:T(8,128)(2,1)S(1)} %collective-permute-done.5.rows.rows_far, f32[1,3584]{1,0:T(1,128)S(1)} %get-tuple-element.50.decoder_bias, f32[8,256]{1,0:T(8,128)S(1)} %get-tuple-element.84.gates.gates_far, ...), custom_call_target="tpu_custom_call" | custom-call | bytes 3750912 | tf_op jit(solution)/shard_map/pallas_call | solution.py:116
  16.3 1.2 %collective-permute-start.9 = (bf16[8,3584]{1,0:T(8,128)(2,1)S(1)}, bf16[8,3584]{1,0:T(8,128)(2,1)S(1)}, u32[]{:S(2)}, u32[]{:S(2)}) collective-permute-start(bf16[8,3584]{1,0:T(8,128)(2,1)S(1)} %get-tuple-element.56), channel_id=1, source_target_pairs={{0,2},{1,3},{2,0},{3,1},{4,6},{5,7},{6,4},{7,5},{8,10},{9,11},{10,... | collective-permute-start | bytes 172040 | tf_op jit(solution)/shard_map/ppermute | solution.py:138
  17.5 0.0 collective-permute-start.6
  17.6 1.0 %collective-permute-done.7 = bf16[8,3584]{1,0:T(8,128)(2,1)S(1)} collective-permute-done((bf16[8,3584]{1,0:T(8,128)(2,1)S(1)}, bf16[8,3584]{1,0:T(8,128)(2,1)S(1)}, u32[]{:S(2)}, u32[]{:S(2)}) %collective-permute-start.7) | collective-permute-done | bytes 57376 | tf_op jit(solution)/shard_map/ppermute | solution.py:138
  18.5 1.6 %collective-permute-start.8 = (bf16[8,3584]{1,0:T(8,128)(2,1)S(1)}, bf16[8,3584]{1,0:T(8,128)(2,1)S(1)}, u32[]{:S(2)}, u32[]{:S(2)}) collective-permute-start(bf16[8,3584]{1,0:T(8,128)(2,1)S(1)} %add.100), channel_id=1, source_target_pairs={{0,4},{1,5},{2,6},{3,7},{4,0},{5,1},{6,2},{7,3},{8,12},{9,13},{10,... | collective-permute-start | bytes 172040 | tf_op jit(solution)/shard_map/ppermute | solution.py:138
  20.2 0.4 collective-permute-done.9
  20.6 1.6 %collective-permute-start.10 = (bf16[8,3584]{1,0:T(8,128)(2,1)S(1)}, bf16[8,3584]{1,0:T(8,128)(2,1)S(1)}, u32[]{:S(2)}, u32[]{:S(2)}) collective-permute-start(bf16[8,3584]{1,0:T(8,128)(2,1)S(1)} %add.102), channel_id=1, source_target_pairs={{0,4},{1,5},{2,6},{3,7},{4,0},{5,1},{6,2},{7,3},{8,12},{9,13},{10,... | collective-permute-start | bytes 172040 | tf_op jit(solution)/shard_map/ppermute | solution.py:138
  22.3 1.1 %collective-permute-done.8 = bf16[8,3584]{1,0:T(8,128)(2,1)S(1)} collective-permute-done((bf16[8,3584]{1,0:T(8,128)(2,1)S(1)}, bf16[8,3584]{1,0:T(8,128)(2,1)S(1)}, u32[]{:S(2)}, u32[]{:S(2)}) %collective-permute-start.8) | collective-permute-done | bytes 57376 | tf_op jit(solution)/shard_map/ppermute | solution.py:138
  23.4 2.1 %collective-permute-start.12 = (bf16[8,3584]{1,0:T(8,128)(2,1)S(1)}, bf16[8,3584]{1,0:T(8,128)(2,1)S(1)}, u32[]{:S(2)}, u32[]{:S(2)}) collective-permute-start(bf16[8,3584]{1,0:T(8,128)(2,1)S(1)} %add.101.low), channel_id=1, source_target_pairs={{0,8},{1,9},{2,10},{3,11},{4,12},{5,13},{6,14},{7,15},{8,0},{9,1},... | collective-permute-start | bytes 172040 | tf_op jit(solution)/shard_map/ppermute | solution.py:138
  25.5 0.0 collective-permute-done.10
  25.5 2.3 %collective-permute-start.11 = (bf16[8,3584]{1,0:T(8,128)(2,1)S(1)}, bf16[8,3584]{1,0:T(8,128)(2,1)S(1)}, u32[]{:S(2)}, u32[]{:S(2)}) collective-permute-start(bf16[8,3584]{1,0:T(8,128)(2,1)S(1)} %add.103.high), channel_id=1, source_target_pairs={{0,8},{1,9},{2,10},{3,11},{4,12},{5,13},{6,14},{7,15},{8,0},{9,1},... | collective-permute-start | bytes 172040 | tf_op jit(solution)/shard_map/ppermute | solution.py:138
  27.9 0.2 convolution_add_fusion
  28.1 1.5 %shard_map.114 = (bf16[3584,128]{1,0:T(8,128)(2,1)S(1)}, bf16[128,3584]{1,0:T(8,128)(2,1)S(1)}) custom-call(bf16[3584,128]{1,0:T(8,128)(2,1)} %refs_0_.3, bf16[128,3584]{1,0:T(8,128)(2,1)} %refs_1_.3), custom_call_target="tpu_custom_call" | custom-call | bytes 3670016 | tf_op jit(solution)/shard_map/pallas_call | solution.py:103
  29.6 1.4 %collective-permute-done.11.low_received = bf16[8,3584]{1,0:T(8,128)(2,1)S(1)} collective-permute-done((bf16[8,3584]{1,0:T(8,128)(2,1)S(1)}, bf16[8,3584]{1,0:T(8,128)(2,1)S(1)}, u32[]{:S(2)}, u32[]{:S(2)}) %collective-permute-start.11) | collective-permute-done | bytes 57376 | tf_op jit(solution)/shard_map/ppermute | solution.py:138
  31.0 1.2 %shard_map.115 = (bf16[16,3584]{1,0:T(8,128)(2,1)S(1)}, f32[2,3584]{1,0:T(2,128)S(1)}) custom-call(bf16[8,3584]{1,0:T(8,128)(2,1)S(1)} %add.101.low, bf16[8,3584]{1,0:T(8,128)(2,1)S(1)} %collective-permute-done.11.low_received, bf16[8,3584]{1,0:T(8,128)(2,1)S(1)} %maximum_select_fusion.rows, f32[8,256]{1,0:T(8,128)S(1)} %get-tuple-element.85.gates, ...), custom_call_target="tpu_custom_call" | custom-call | bytes 4044800 | tf_op jit(solution)/shard_map/pallas_call | solution.py:116
  32.1 0.1 collective-permute-start.14
  32.2 0.5 %collective-permute-start.13 = (bf16[16,3584]{1,0:T(8,128)(2,1)S(1)}, bf16[16,3584]{1,0:T(8,128)(2,1)S(1)}, u32[]{:S(2)}, u32[]{:S(2)}) collective-permute-start(bf16[16,3584]{1,0:T(8,128)(2,1)S(1)} %get-tuple-element.65), channel_id=1, source_target_pairs={{0,1},{1,0},{2,3},{3,2},{4,5},{5,4},{6,7},{7,6},{8,9},{9,8},{10,11... | collective-permute-start | bytes 344072 | tf_op jit(solution)/shard_map/ppermute | solution.py:138
  32.7 0.7 %collective-permute-done.14 = f32[2,3584]{1,0:T(2,128)S(1)} collective-permute-done((f32[2,3584]{1,0:T(2,128)S(1)}, f32[2,3584]{1,0:T(2,128)S(1)}, u32[]{:S(2)}, u32[]{:S(2)}) %collective-permute-start.14) | collective-permute-done | bytes 28704 | tf_op jit(solution)/shard_map/ppermute | solution.py:138
  33.4 0.3 collective-permute-done.13
  33.7 1.0 %collective-permute-start.15 = (f32[1,3584]{1,0:T(1,128)S(1)}, f32[1,3584]{1,0:T(1,128)S(1)}, u32[]{:S(2)}, u32[]{:S(2)}) collective-permute-start(f32[1,3584]{1,0:T(1,128)S(1)} %slice.14), channel_id=1, source_target_pairs={{0,2},{1,3},{2,0},{3,1},{4,6},{5,7},{6,4},{7,5},{8,10},{9,11},{10,... | collective-permute-start | bytes 43016 | tf_op jit(solution)/shard_map/ppermute | solution.py:138
  34.7 0.9 %select_reduce_fusion = (f32[128]{0:T(128)}, f32[128]{0:T(128)}, bf16[32,128]{1,0:T(8,128)(2,1)S(1)}) fusion(pred[16,128]{1,0:T(8,128)(4,1)S(1)} %get-tuple-element.81, pred[16,128]{1,0:T(8,128)(4,1)S(1)} %get-tuple-element.79, f32[128]{0:T(128)S(1)} %copy-done.2, f32[16,128]{1,0:T(8,128)S(1)} %convolution_add_fusion, f32[8,128]{1,0:T(8,128)S(1)} %get-tuple-element.69, ...), kind=kOutput, calls=%fused_computation.20 | convolution fusion | flops 29425408 | bytes 1177600 | tf_op jit(solution)/shard_map/dot_general | solution.py:27
  35.6 1.9 %collective-permute-done.15 = f32[1,3584]{1,0:T(1,128)S(1)} collective-permute-done((f32[1,3584]{1,0:T(1,128)S(1)}, f32[1,3584]{1,0:T(1,128)S(1)}, u32[]{:S(2)}, u32[]{:S(2)}) %collective-permute-start.15) | collective-permute-done | bytes 14368 | tf_op jit(solution)/shard_map/ppermute | solution.py:138
  37.5 1.4 %collective-permute-start.16 = (f32[1,3584]{1,0:T(1,128)S(1)}, f32[1,3584]{1,0:T(1,128)S(1)}, u32[]{:S(2)}, u32[]{:S(2)}) collective-permute-start(f32[1,3584]{1,0:T(1,128)S(1)} %slice_add_fusion), channel_id=1, source_target_pairs={{0,4},{1,5},{2,6},{3,7},{4,0},{5,1},{6,2},{7,3},{8,12},{9,13},{10,... | collective-permute-start | bytes 43016 | tf_op jit(solution)/shard_map/ppermute | solution.py:138
  38.9 1.4 %convolution_convert_fusion = bf16[128,3584]{1,0:T(8,128)(2,1)} fusion(bf16[32,3584]{1,0:T(8,128)(2,1)S(1)} %constant_dynamic-update-slice_fusion.2, f32[16,128]{1,0:T(8,128)S(1)} %convolution_add_fusion, f32[8,128]{1,0:T(8,128)S(1)} %get-tuple-element.69, f32[8,128]{1,0:T(8,128)S(1)} %get-tuple-element.68, pred[16,128]{1,0:T(8,128)(4,1)S(1)} %get-tuple-element.81, ...), kind=kOutput, calls=%fused_computation | convolution fusion | flops 29851648 | bytes 1167360 | tf_op jit(solution)/shard_map/dot_general | solution.py:31
  40.3 1.1 %collective-permute-done.16 = f32[1,3584]{1,0:T(1,128)S(1)} collective-permute-done((f32[1,3584]{1,0:T(1,128)S(1)}, f32[1,3584]{1,0:T(1,128)S(1)}, u32[]{:S(2)}, u32[]{:S(2)}) %collective-permute-start.16) | collective-permute-done | bytes 14368 | tf_op jit(solution)/shard_map/ppermute | solution.py:138
  41.3 2.1 %collective-permute-start.17 = (f32[1,3584]{1,0:T(1,128)S(1)}, f32[1,3584]{1,0:T(1,128)S(1)}, u32[]{:S(2)}, u32[]{:S(2)}) collective-permute-start(f32[1,3584]{1,0:T(1,128)S(1)} %add.109), channel_id=1, source_target_pairs={{0,8},{1,9},{2,10},{3,11},{4,12},{5,13},{6,14},{7,15},{8,0},{9,1},... | collective-permute-start | bytes 43016 | tf_op jit(solution)/shard_map/ppermute | solution.py:138
  43.4 1.4 %convolution_convert_fusion.1 = bf16[3584,128]{1,0:T(8,128)(2,1)} fusion(bf16[32,128]{1,0:T(8,128)(2,1)S(1)} %select_convert_fusion.1, bf16[16,3584]{1,0:T(8,128)(2,1)S(1)} %get-tuple-element.83, bf16[16,3584]{1,0:T(8,128)(2,1)S(1)} %get-tuple-element.82), kind=kOutput, calls=%fused_computation.1 | convolution fusion | flops 30277632 | bytes 1155072 | tf_op jit(solution)/shard_map/dot_general | solution.py:31
  44.8 1.2 %collective-permute-done.17 = f32[1,3584]{1,0:T(1,128)S(1)} collective-permute-done((f32[1,3584]{1,0:T(1,128)S(1)}, f32[1,3584]{1,0:T(1,128)S(1)}, u32[]{:S(2)}, u32[]{:S(2)}) %collective-permute-start.17) | collective-permute-done | bytes 14368 | tf_op jit(solution)/shard_map/ppermute | solution.py:138
  46.0 0.7 %subtract_reduce_fusion.1 = f32[3584]{0:T(1024)} fusion(f32[1,3584]{1,0:T(1,128)S(1)} %add.109, f32[1,3584]{1,0:T(1,128)S(1)} %collective-permute-done.17, f32[2,3584]{1,0:T(2,128)S(1)} %add.104), kind=kLoop, calls=%fused_computation.18 | loop fusion | flops 7168 | bytes 57344 | tf_op jit(solution)/shard_map/sub | solution.py:247
  (29 shorter events, 0.3 us)
Async XLA Ops:
  0.6 5.8 %collective-permute-start = (bf16[2,3584]{1,0:T(2,128)(2,1)}, bf16[2,3584]{1,0:T(2,128)(2,1)S(1)}, u32[]{:S(2)}, u32[]{:S(2)}) collective-permute-start(bf16[2,3584]{1,0:T(2,128)(2,1)} %refs_0_.1), channel_id=1, source_target_pairs={{0,2},{1,3},{2,0},{3,1},{4,6},{5,7},{6,4},{7,5},{8,10},{9,11},{10,... | collective-permute-start | bytes 43016 | tf_op jit(solution)/shard_map/ppermute | solution.py:138
  3.7 9.5 %collective-permute-start.2 = (bf16[3584,128]{1,0:T(8,128)(2,1)}, bf16[3584,128]{1,0:T(8,128)(2,1)S(1)}, u32[]{:S(2)}, u32[]{:S(2)}) collective-permute-start(bf16[3584,128]{1,0:T(8,128)(2,1)} %refs_0_.3), channel_id=1, source_target_pairs={{0,1},{1,0},{2,3},{3,2},{4,5},{5,4},{6,7},{7,6},{8,9},{9,8},{10,11... | collective-permute-start | bytes 2752520 | tf_op jit(solution)/shard_map/ppermute | solution.py:138
  3.7 9.5 %collective-permute-start.4 = (bf16[128,3584]{1,0:T(8,128)(2,1)}, bf16[128,3584]{1,0:T(8,128)(2,1)S(1)}, u32[]{:S(2)}, u32[]{:S(2)}) collective-permute-start(bf16[128,3584]{1,0:T(8,128)(2,1)} %refs_1_.3), channel_id=1, source_target_pairs={{0,1},{1,0},{2,3},{3,2},{4,5},{5,4},{6,7},{7,6},{8,9},{9,8},{10,11... | collective-permute-start | bytes 2752520 | tf_op jit(solution)/shard_map/ppermute | solution.py:138
  4.2 9.0 %collective-permute-start.3 = (f32[1,128]{1,0:T(1,128)}, f32[1,128]{1,0:T(1,128)S(1)}, u32[]{:S(2)}, u32[]{:S(2)}) collective-permute-start(f32[1,128]{1,0:T(1,128)} %bitcast.17), channel_id=1, source_target_pairs={{0,1},{1,0},{2,3},{3,2},{4,5},{5,4},{6,7},{7,6},{8,9},{9,8},{10,11... | collective-permute-start | bytes 1544 | tf_op jit(solution)/shard_map/ppermute | solution.py:138
  6.5 3.9 %collective-permute-start.1 = (bf16[4,3584]{1,0:T(4,128)(2,1)S(1)}, bf16[4,3584]{1,0:T(4,128)(2,1)S(1)}, u32[]{:S(2)}, u32[]{:S(2)}) collective-permute-start(bf16[4,3584]{1,0:T(4,128)(2,1)S(1)} %maximum_select_fusion.1), channel_id=1, source_target_pairs={{0,4},{1,5},{2,6},{3,7},{4,0},{5,1},{6,2},{7,3},{8,12},{9,13},{10,... | collective-permute-start | bytes 86024 | tf_op jit(solution)/shard_map/ppermute | solution.py:138
  10.5 5.2 %collective-permute-start.5 = (bf16[8,3584]{1,0:T(8,128)(2,1)S(1)}, bf16[8,3584]{1,0:T(8,128)(2,1)S(1)}, u32[]{:S(2)}, u32[]{:S(2)}) collective-permute-start(bf16[8,3584]{1,0:T(8,128)(2,1)S(1)} %maximum_select_fusion.rows), channel_id=1, source_target_pairs={{0,8},{1,9},{2,10},{3,11},{4,12},{5,13},{6,14},{7,15},{8,0},{9,1},... | collective-permute-start | bytes 172040 | tf_op jit(solution)/shard_map/ppermute | solution.py:138
  13.9 4.7 %collective-permute-start.7 = (bf16[8,3584]{1,0:T(8,128)(2,1)S(1)}, bf16[8,3584]{1,0:T(8,128)(2,1)S(1)}, u32[]{:S(2)}, u32[]{:S(2)}) collective-permute-start(bf16[8,3584]{1,0:T(8,128)(2,1)S(1)} %get-tuple-element.54), channel_id=1, source_target_pairs={{0,2},{1,3},{2,0},{3,1},{4,6},{5,7},{6,4},{7,5},{8,10},{9,11},{10,... | collective-permute-start | bytes 172040 | tf_op jit(solution)/shard_map/ppermute | solution.py:138
  15.6 6.6 %copy-start.2 = (f32[128]{0:T(128)S(1)}, f32[128]{0:T(128)}, u32[]{:S(2)}) copy-start(f32[128]{0:T(128)} %param.11) | copy-start | bytes 1540
  16.3 11.6 %copy-start = (bf16[3584,128]{1,0:T(8,128)(2,1)S(1)}, bf16[3584,128]{1,0:T(8,128)(2,1)}, u32[]{:S(2)}) copy-start(bf16[3584,128]{1,0:T(8,128)(2,1)} %refs_0_.3) | copy-start | bytes 2752516
  16.3 11.6 %copy-start.1 = (f32[128]{0:T(128)S(1)}, f32[128]{0:T(128)}, u32[]{:S(2)}) copy-start(f32[128]{0:T(128)} %refs_2_) | copy-start | bytes 1540
  16.3 4.2 %collective-permute-start.9 = (bf16[8,3584]{1,0:T(8,128)(2,1)S(1)}, bf16[8,3584]{1,0:T(8,128)(2,1)S(1)}, u32[]{:S(2)}, u32[]{:S(2)}) collective-permute-start(bf16[8,3584]{1,0:T(8,128)(2,1)S(1)} %get-tuple-element.56), channel_id=1, source_target_pairs={{0,2},{1,3},{2,0},{3,1},{4,6},{5,7},{6,4},{7,5},{8,10},{9,11},{10,... | collective-permute-start | bytes 172040 | tf_op jit(solution)/shard_map/ppermute | solution.py:138
  17.5 10.3 %collective-permute-start.6 = (bf16[16,3584]{1,0:T(8,128)(2,1)S(1)}, bf16[16,3584]{1,0:T(8,128)(2,1)S(1)}, u32[]{:S(2)}, u32[]{:S(2)}) collective-permute-start(bf16[16,3584]{1,0:T(8,128)(2,1)S(1)} %constant_dynamic-update-slice_fusion), channel_id=1, source_target_pairs={{0,1},{1,0},{2,3},{3,2},{4,5},{5,4},{6,7},{7,6},{8,9},{9,8},{10,11... | collective-permute-start | bytes 344072 | tf_op jit(solution)/shard_map/ppermute | solution.py:138
  18.5 4.8 %collective-permute-start.8 = (bf16[8,3584]{1,0:T(8,128)(2,1)S(1)}, bf16[8,3584]{1,0:T(8,128)(2,1)S(1)}, u32[]{:S(2)}, u32[]{:S(2)}) collective-permute-start(bf16[8,3584]{1,0:T(8,128)(2,1)S(1)} %add.100), channel_id=1, source_target_pairs={{0,4},{1,5},{2,6},{3,7},{4,0},{5,1},{6,2},{7,3},{8,12},{9,13},{10,... | collective-permute-start | bytes 172040 | tf_op jit(solution)/shard_map/ppermute | solution.py:138
  20.6 4.9 %collective-permute-start.10 = (bf16[8,3584]{1,0:T(8,128)(2,1)S(1)}, bf16[8,3584]{1,0:T(8,128)(2,1)S(1)}, u32[]{:S(2)}, u32[]{:S(2)}) collective-permute-start(bf16[8,3584]{1,0:T(8,128)(2,1)S(1)} %add.102), channel_id=1, source_target_pairs={{0,4},{1,5},{2,6},{3,7},{4,0},{5,1},{6,2},{7,3},{8,12},{9,13},{10,... | collective-permute-start | bytes 172040 | tf_op jit(solution)/shard_map/ppermute | solution.py:138
  23.4 7.6 %collective-permute-start.12 = (bf16[8,3584]{1,0:T(8,128)(2,1)S(1)}, bf16[8,3584]{1,0:T(8,128)(2,1)S(1)}, u32[]{:S(2)}, u32[]{:S(2)}) collective-permute-start(bf16[8,3584]{1,0:T(8,128)(2,1)S(1)} %add.101.low), channel_id=1, source_target_pairs={{0,8},{1,9},{2,10},{3,11},{4,12},{5,13},{6,14},{7,15},{8,0},{9,1},... | collective-permute-start | bytes 172040 | tf_op jit(solution)/shard_map/ppermute | solution.py:138
  25.5 5.5 %collective-permute-start.11 = (bf16[8,3584]{1,0:T(8,128)(2,1)S(1)}, bf16[8,3584]{1,0:T(8,128)(2,1)S(1)}, u32[]{:S(2)}, u32[]{:S(2)}) collective-permute-start(bf16[8,3584]{1,0:T(8,128)(2,1)S(1)} %add.103.high), channel_id=1, source_target_pairs={{0,8},{1,9},{2,10},{3,11},{4,12},{5,13},{6,14},{7,15},{8,0},{9,1},... | collective-permute-start | bytes 172040 | tf_op jit(solution)/shard_map/ppermute | solution.py:138
  32.1 1.3 %collective-permute-start.14 = (f32[2,3584]{1,0:T(2,128)S(1)}, f32[2,3584]{1,0:T(2,128)S(1)}, u32[]{:S(2)}, u32[]{:S(2)}) collective-permute-start(f32[2,3584]{1,0:T(2,128)S(1)} %get-tuple-element.66), channel_id=1, source_target_pairs={{0,1},{1,0},{2,3},{3,2},{4,5},{5,4},{6,7},{7,6},{8,9},{9,8},{10,11... | collective-permute-start | bytes 86024 | tf_op jit(solution)/shard_map/ppermute | solution.py:138
  32.2 1.5 %collective-permute-start.13 = (bf16[16,3584]{1,0:T(8,128)(2,1)S(1)}, bf16[16,3584]{1,0:T(8,128)(2,1)S(1)}, u32[]{:S(2)}, u32[]{:S(2)}) collective-permute-start(bf16[16,3584]{1,0:T(8,128)(2,1)S(1)} %get-tuple-element.65), channel_id=1, source_target_pairs={{0,1},{1,0},{2,3},{3,2},{4,5},{5,4},{6,7},{7,6},{8,9},{9,8},{10,11... | collective-permute-start | bytes 344072 | tf_op jit(solution)/shard_map/ppermute | solution.py:138
  33.7 3.8 %collective-permute-start.15 = (f32[1,3584]{1,0:T(1,128)S(1)}, f32[1,3584]{1,0:T(1,128)S(1)}, u32[]{:S(2)}, u32[]{:S(2)}) collective-permute-start(f32[1,3584]{1,0:T(1,128)S(1)} %slice.14), channel_id=1, source_target_pairs={{0,2},{1,3},{2,0},{3,1},{4,6},{5,7},{6,4},{7,5},{8,10},{9,11},{10,... | collective-permute-start | bytes 43016 | tf_op jit(solution)/shard_map/ppermute | solution.py:138
  37.5 3.8 %collective-permute-start.16 = (f32[1,3584]{1,0:T(1,128)S(1)}, f32[1,3584]{1,0:T(1,128)S(1)}, u32[]{:S(2)}, u32[]{:S(2)}) collective-permute-start(f32[1,3584]{1,0:T(1,128)S(1)} %slice_add_fusion), channel_id=1, source_target_pairs={{0,4},{1,5},{2,6},{3,7},{4,0},{5,1},{6,2},{7,3},{8,12},{9,13},{10,... | collective-permute-start | bytes 43016 | tf_op jit(solution)/shard_map/ppermute | solution.py:138
  41.3 4.7 %collective-permute-start.17 = (f32[1,3584]{1,0:T(1,128)S(1)}, f32[1,3584]{1,0:T(1,128)S(1)}, u32[]{:S(2)}, u32[]{:S(2)}) collective-permute-start(f32[1,3584]{1,0:T(1,128)S(1)} %add.109), channel_id=1, source_target_pairs={{0,8},{1,9},{2,10},{3,11},{4,12},{5,13},{6,14},{7,15},{8,0},{9,1},... | collective-permute-start | bytes 43016 | tf_op jit(solution)/shard_map/ppermute | solution.py:138

commit v5 on v4

--- a/solution.py
+++ b/solution.py
@@ -47,33 +47,79 @@
 
 def backward_kernel(
     low, low_received, rows, gates, high, high_received, rows_far, gates_far, decoder_bias,
-    encoder, encoder_other, decoder, decoder_other, errors, sums
+    encoder_turned, decoder_turned, errors, part
 ):
-    width = encoder.shape[1]
-
     def error(total, received, block):
         total = total[...].astype(F32) + received[...].astype(F32)
-        return (total + decoder_bias[...] - block[...].astype(F32)).astype(BF16).astype(F32)
-
-    near_part = error(low, low_received, rows)
-    far_part = error(high, high_received, rows_far)
-    sums[0:1, :] = jnp.sum(near_part, axis=0, keepdims=True) + jnp.sum(
-        far_part, axis=0, keepdims=True
-    )
-    found = jnp.concatenate([near_part, far_part], axis=0).astype(BF16)
+        return total + decoder_bias[...] - block[...].astype(F32)
+
+    found = jnp.concatenate(
+        [error(low, low_received, rows), error(high, high_received, rows_far)], axis=0
+    ).astype(BF16)
     errors[...] = found
     gate = jnp.concatenate([gates[...], gates_far[...]], axis=0)
-
-    def product(gate, decoder_block, encoder_block):
-        grad = jnp.sum(dot_last(found, decoder_block[...]) * gate, axis=0, keepdims=True)
-        upper = grad.astype(BF16).astype(F32)
-        row = lax.broadcasted_iota(jnp.int32, (8, width), 0)
-        both = jnp.where(row == 0, upper, jnp.where(row == 1, grad - upper, 0.0))
-        return dot_last(both.astype(BF16), encoder_block[...])
-
-    both = product(gate[:, :width], decoder, encoder)
-    both += product(gate[:, width:], decoder_other, encoder_other)
-    sums[1:2, :] = jnp.sum(both, axis=0, keepdims=True)
+    width = gate.shape[1] // 2
+    mine, other = dot(found, decoder_turned[:, :width]), dot(found, decoder_turned[:, width:])
+    code_grad = jnp.concatenate([mine, other], axis=1)
+    grad = jnp.sum(code_grad * gate, axis=0, keepdims=True)
+    upper = grad.astype(BF16).astype(F32)
+    row = lax.broadcasted_iota(jnp.int32, (8, grad.shape[1]), 0)
+    both = jnp.where(row == 0, upper, jnp.where(row == 1, grad - upper, 0.0))
+    spread = dot(both.astype(BF16), encoder_turned[...])
+    part[...] = spread[0:1, :] + spread[1:2, :]
+
+
+def sum_kernel(errors, errors_other, total):
+    half = errors.shape[0] // 2
+
+    def summed(ref):
+        block = ref[...].astype(F32)
+        first = jnp.sum(block[:half], axis=0, keepdims=True)
+        return first + jnp.sum(block[half:], axis=0, keepdims=True)
+
+    total[...] = summed(errors) + summed(errors_other)
+
+
+def turn_kernel(
+    encoder_far, decoder_far, encoder_other, decoder_other, encoder_turned, decoder_turned,
+    encoder, decoder, ready
+):
+    first = pltpu.make_async_copy(decoder_far, decoder, ready.at[0])
+    second = pltpu.make_async_copy(encoder_far, encoder, ready.at[1])
+    first.start()
+    second.start()
+    width = encoder_other.shape[1]
+    decoder_turned[:, width:] = decoder_other[...].T
+    encoder_turned[width:, :] = encoder_other[...].T
+    first.wait()
+    decoder_turned[:, :width] = decoder[...].T
+    second.wait()
+    encoder_turned[:width, :] = encoder[...].T
+
+
+def turn(encoder, decoder, encoder_other, decoder_other):
+    depth, width = encoder.shape
+    far = pl.BlockSpec(memory_space=pltpu.HBM)
+    whole = pl.BlockSpec(memory_space=pltpu.VMEM)
+    return pl.pallas_call(
+        turn_kernel,
+        in_specs=[far, far, whole, whole],
+        out_specs=[whole, whole],
+        out_shape=[pltpu.VMEM((2 * width, depth), BF16), pltpu.VMEM((depth, 2 * width), BF16)],
+        scratch_shapes=[
+            pltpu.VMEM(encoder.shape, BF16),
+            pltpu.VMEM(decoder.shape, BF16),
+            pltpu.SemaphoreType.DMA((2,)),
+        ],
+        cost_estimate=cost(8 * size(encoder)),
+        compiler_params=pltpu.CompilerParams(vmem_limit_bytes=LIMIT),
+    )(
+        *[pltpu.with_memory_space_constraint(array, pltpu.HBM) for array in (encoder, decoder)],
+        *[
+            pltpu.with_memory_space_constraint(array, pltpu.VMEM)
+            for array in (encoder_other, decoder_other)
+        ],
+    )
 
 
 def size(array):
@@ -148,11 +194,22 @@
     bias_other = swap(encoder_bias[None], 1)
 
     per_device, depth = rows_in.shape
+    ids = active_ids.reshape(2, count // 4, 2, per_device, active_ids.shape[1])
+    side = jnp.where((me & hops[-1]) == 0, 0, 1)
+
+    def listed(half, part):
+        one = lax.dynamic_index_in_dim(ids, half, 0, keepdims=False)
+        one = lax.dynamic_index_in_dim(one, part, 1, keepdims=False)
+        return one.reshape(count // 4 * per_device, -1)
+
+    lists = jnp.concatenate([listed(side, core), listed(1 - side, core)])
+    lists_other = jnp.concatenate([listed(side, 1 - core), listed(1 - side, 1 - core)])
+
     block, bias_row = stage(rows_in, decoder_bias)
     for bit in hops[:-1]:
         if bit == hops[-2]:
             weights = (encoder_weight, decoder_weight, encoder_bias)
-            block, weights = lax.optimization_barrier((block, weights))
+            block, weights, lists = lax.optimization_barrier((block, weights, lists))
         other = swap(rows_in if bit == hops[0] else block, bit)
         low = jnp.concatenate([block, other], axis=0)
         high = jnp.concatenate([other, block], axis=0)
@@ -165,19 +222,9 @@
     rows_far = swap(block, hops[-1])
     half_rows = rows.shape[0]
 
-    ids = active_ids.reshape(2, half_rows // per_device, 2, per_device, active_ids.shape[1])
-    side = jnp.where((me & hops[-1]) == 0, 0, 1)
-
-    def listed(half, part):
-        one = lax.dynamic_index_in_dim(ids, half, 0, keepdims=False)
-        one = lax.dynamic_index_in_dim(one, part, 1, keepdims=False)
-        return one.reshape(half_rows, -1)
-
     def center(part):
         return (part.astype(F32) - bias_row).astype(BF16)
 
-    lists = jnp.concatenate([listed(side, core), listed(1 - side, core)])
-    lists_other = jnp.concatenate([listed(side, 1 - core), listed(1 - side, 1 - core)])
     gate_mine = opened(lists, me * width, width)
     gates = jnp.concatenate([gate_mine, opened(lists, (me ^ 1) * width, width)], axis=1)
     gates = gates.astype(F32)
@@ -194,15 +241,26 @@
     preact_near, low = forward(rows, gates)
     preact_far, high = forward(after(low, rows_far), gates_far)
     every_row = jnp.concatenate([rows, after(high, rows_far)])
+    rows_other = swap(every_row, 1)
     for bit in hops[:-1]:
         low, high_received = lax.optimization_barrier(low + swap(low, bit)), swap(high, bit)
         high = lax.optimization_barrier(high + after(low, high_received))
     high_received = swap(low, hops[-1])
     high, weights = lax.optimization_barrier((high, (encoder_weight, decoder_weight)))
     low_received = swap(high, hops[-1])
-    encoder_near, decoder_near = stage(*weights)
-
-    rows_other = swap(every_row, 1)
+    encoder_turned, decoder_turned = turn(*weights, encoder_other, decoder_other)
+
+    errors, part = near(
+        backward_kernel,
+        (low, low_received, rows, gates, high, high_received, rows_far, gates_far, bias_row,
+         encoder_turned, decoder_turned),
+        (((2 * half_rows, depth), BF16), ((1, depth), F32)),
+    )
+    errors_other = swap(errors, 1)
+    part = part + swap(part, 1)
+    errors_other, part = lax.optimization_barrier((errors_other, part))
+
+    rows_other, lists_other, _ = lax.optimization_barrier((rows_other, lists_other, errors))
     centered_other = center(rows_other)
     gate_rest = opened(lists_other, me * width, width)
     preact_rest = dot(centered_other, encoder_weight) + encoder_bias
@@ -211,21 +269,10 @@
     every_centered = jnp.concatenate([center(every_row), centered_other])
     codes = jnp.where(gate, preact, 0.0).astype(BF16)
 
-    errors, sums = near(
-        backward_kernel,
-        (low, low_received, rows, gates, high, high_received, rows_far, gates_far, bias_row,
-         encoder_near, encoder_other, decoder_near, decoder_other),
-        (((2 * half_rows, depth), BF16), ((2, depth), F32)),
-    )
-    errors_other = swap(errors, 1)
-    sums = sums + swap(sums, 1)
-    errors_other, sums = lax.optimization_barrier((errors_other, sums))
-    part = sums[1:]
-
     every_error = jnp.concatenate([errors, errors_other])
 
     def small_outputs():
-        code_grad = dot_last(every_error, decoder_near)
+        code_grad = dot_last(every_error, decoder_weight)
         distance = (preact - threshold) / EPSILON
         kernel = jnp.exp(-0.5 * distance * distance) / (EPSILON * math.sqrt(2.0 * math.pi))
         grad_threshold = jnp.sum(-threshold * code_grad * kernel - SPARSITY * kernel, axis=0)
@@ -242,9 +289,10 @@
     small, part = lax.optimization_barrier((small_outputs(), part))
     part = part + swap(part, hops[1])
     grad_decoder, part = lax.optimization_barrier((decoder_output(), part))
+    (error_sum,) = near(sum_kernel, (errors, errors_other), (((1, depth), F32),))
     for bit in hops[2:]:
         part = part + swap(part, bit)
-    grad_decoder_bias = (sums[:1] - part).reshape(depth)
+    grad_decoder_bias = (error_sum - part).reshape(depth)
     grad_encoder = encoder_output()
     grad_threshold, grad_encoder_bias, _ = small
     return (grad_encoder, grad_encoder_bias, grad_threshold, grad_decoder, grad_decoder_bias)

time: 47 us -> 46 us (0.979)
  waiting for transfers between devices: 10.3 us -> 6.66 us
  starting transfers between devices: 22.9 us -> 25 us
  other arithmetic: 1.7 us -> 2.39 us
    ppermute x18, waiting for transfers between devices: 10.3 us -> 6.66 us  [swap(): return lax.ppermute(array, 'latent', [(i, i ^ bit) for i in range(count)])]
    ppermute x18, starting transfers between devices: 22.9 us -> 25 us  [swap(): return lax.ppermute(array, 'latent', [(i, i ^ bit) for i in range(count)])]
    pallas_call x0 -> x1, Pallas kernels: none -> 1.79 us  [turn(): pl.pallas_call(turn_kernel, in_specs=[far, far, whole, whole], out_specs=...]
    pallas_call x3 -> x2, Pallas kernels: 3.72 us -> 2.23 us  [stage(): pl.pallas_call(stage_kernel, in_specs=[pl.BlockSpec(memory_space=pltpu.HB...]
    neg x1, other arithmetic: 0.01 us -> 0.66 us  [small_outputs(): -threshold * code_grad * kernel - SPARSITY * kernel]
    pallas_call x3 -> x4, Pallas kernels: 2.51 us -> 2.19 us  [near(): pl.pallas_call(kernel, in_specs=[whole] * len(arrays), out_specs=[whole]...]
  transfers between devices with their start and end apart: 18 -> 18, of which waited for: 11 -> 10; matrix products, arithmetic and copies ran while one was open for 12% -> 14% of each run, Pallas kernels for 11% -> 14%
where the time goes in v5:
time: 46 us; the launch traced here: 45.7 us
  starting transfers between devices  25 us (54%)
  waiting for transfers between devices  6.66 us (14%)
  Pallas kernels  6.22 us (14%)
  matrix products  3.89 us (8%)
  other arithmetic  2.39 us (5%)
  between operations  0.83 us (2%)
  local copies, waits for them, and re-layouts  0.79 us (2%)
    ppermute x18, starting transfers between devices, swap(): return lax.ppermute(array, 'latent', [(i, i ^ bit) for i in range(count)])  25 us
    ppermute x18, waiting for transfers between devices, swap(): return lax.ppermute(array, 'latent', [(i, i ^ bit) for i in range(count)])  6.66 us
    dot_general x2, matrix products, dot_rows(): lax.dot_general(a, b, (((0,), (0,)), ((), ())), preferred_element_type=F32)  2.73 us
    pallas_call x2, Pallas kernels, stage(): pl.pallas_call(stage_kernel, in_specs=[pl.BlockSpec(memory_space=pltpu.HB...  2.23 us
    pallas_call x4, Pallas kernels, near(): pl.pallas_call(kernel, in_specs=[whole] * len(arrays), out_specs=[whole]...  2.19 us
    pallas_call x1, Pallas kernels, turn(): pl.pallas_call(turn_kernel, in_specs=[far, far, whole, whole], out_specs=...  1.79 us
    dot_general x1, matrix products, dot_last(): lax.dot_general(a, b, (((1,), (1,)), ((), ())), preferred_element_type=F32)  0.93 us
  transfers between devices with their start and end apart: 18, of which 10 were waited for; matrix products, arithmetic and copies ran while one was open for 14% of the time, Pallas kernels for 14%

profile of v5, /device:TPU:0, one launch (start us, length us, event | category | flops | bytes accessed | tf_op | source)
XLA Modules:
  0.0 45.7 jit_solution(339313711880945030)
XLA Ops:
  0.6 3.0 %collective-permute-start = (bf16[2,3584]{1,0:T(2,128)(2,1)}, bf16[2,3584]{1,0:T(2,128)(2,1)S(1)}, u32[]{:S(2)}, u32[]{:S(2)}) collective-permute-start(bf16[2,3584]{1,0:T(2,128)(2,1)} %refs_0_.1), channel_id=1, source_target_pairs={{0,2},{1,3},{2,0},{3,1},{4,6},{5,7},{6,4},{7,5},{8,10},{9,11},{10,... | collective-permute-start | bytes 43016 | tf_op jit(solution)/shard_map/ppermute | solution.py:184
  3.7 0.5 %collective-permute-start.4 = (bf16[128,3584]{1,0:T(8,128)(2,1)}, bf16[128,3584]{1,0:T(8,128)(2,1)S(1)}, u32[]{:S(2)}, u32[]{:S(2)}) collective-permute-start(bf16[128,3584]{1,0:T(8,128)(2,1)} %decoder_far), channel_id=1, source_target_pairs={{0,1},{1,0},{2,3},{3,2},{4,5},{5,4},{6,7},{7,6},{8,9},{9,8},{10,11... | collective-permute-start | bytes 2752520 | tf_op jit(solution)/shard_map/ppermute | solution.py:184
  4.2 0.0 collective-permute-start.3
  4.2 0.7 %constant_dynamic-slice_fusion.1 = (s32[1,4,1,2,128]{4,3,2,1,0:T(2,128)S(1)}, s32[1,4,1,2,128]{4,3,2,1,0:T(2,128)S(1)}, s32[1,4,1,2,128]{4,3,2,1,0:T(2,128)S(1)}, s32[1,4,1,2,128]{4,3,2,1,0:T(2,128)S(1)}) fusion(s32[2,4,2,2,128]{4,3,2,1,0:T(2,128)} %bitcast.12, s32[]{:T(128)S(6)} %select_n.55, s32[]{:T(128)S(6)} %select_n.62, s32[]{:T(128)S(6)} %select_n.59, ...), kind=kLoop, calls=%fused_computation.29 | loop fusion | bytes 32784 | tf_op jit(solution)/shard_map/jit(dynamic_index_in_dim)/dynamic_slice | solution.py:202
  4.9 0.7 %shard_map.110 = (bf16[2,3584]{1,0:T(2,128)(2,1)S(1)}, f32[1,3584]{1,0:T(1,128)S(1)}) custom-call(bf16[2,3584]{1,0:T(2,128)(2,1)} %refs_0_.1, f32[3584]{0:T(1024)} %refs_1_.1), custom_call_target="tpu_custom_call" | custom-call | bytes 57344 | tf_op jit(solution)/shard_map/pallas_call | solution.py:149
  5.7 0.7 %neg.3 = f32[128]{0:T(128)S(1)} negate(f32[128]{0:T(128)} %param.11) | non-fusion elementwise | flops 128 | bytes 1024 | tf_op jit(solution)/shard_map/neg | solution.py:278
  6.4 0.1 maximum_select_fusion.1
  6.5 1.6 %collective-permute-start.1 = (bf16[4,3584]{1,0:T(4,128)(2,1)S(1)}, bf16[4,3584]{1,0:T(4,128)(2,1)S(1)}, u32[]{:S(2)}, u32[]{:S(2)}) collective-permute-start(bf16[4,3584]{1,0:T(4,128)(2,1)S(1)} %maximum_select_fusion.1), channel_id=1, source_target_pairs={{0,4},{1,5},{2,6},{3,7},{4,0},{5,1},{6,2},{7,3},{8,12},{9,13},{10,... | collective-permute-start | bytes 86024 | tf_op jit(solution)/shard_map/ppermute | solution.py:184
  8.1 0.4 compare_reduce_fusion.2
  8.5 1.5 %shard_map.111 = (bf16[3584,128]{1,0:T(8,128)(2,1)S(1)}, bf16[128,3584]{1,0:T(8,128)(2,1)S(1)}, f32[1,128]{1,0:T(1,128)S(1)}) custom-call(bf16[3584,128]{1,0:T(8,128)(2,1)} %encoder_far, bf16[128,3584]{1,0:T(8,128)(2,1)} %decoder_far, f32[128]{0:T(128)} %refs_2_), custom_call_target="tpu_custom_call" | custom-call | bytes 3671040 | tf_op jit(solution)/shard_map/pallas_call | solution.py:149
  10.0 0.4 collective-permute-done.1
  10.4 0.1 maximum_select_fusion.rows
  10.5 2.7 %collective-permute-start.5 = (bf16[8,3584]{1,0:T(8,128)(2,1)S(1)}, bf16[8,3584]{1,0:T(8,128)(2,1)S(1)}, u32[]{:S(2)}, u32[]{:S(2)}) collective-permute-start(bf16[8,3584]{1,0:T(8,128)(2,1)S(1)} %maximum_select_fusion.rows), channel_id=1, source_target_pairs={{0,8},{1,9},{2,10},{3,11},{4,12},{5,13},{6,14},{7,15},{8,0},{9,1},... | collective-permute-start | bytes 172040 | tf_op jit(solution)/shard_map/ppermute | solution.py:184
  13.1 0.0 collective-permute-done.4.decoder_other
  13.1 0.7 %shard_map.112 = (f32[8,128]{1,0:T(8,128)S(1)}, bf16[8,3584]{1,0:T(8,128)(2,1)S(1)}) custom-call(bf16[8,3584]{1,0:T(8,128)(2,1)S(1)} %maximum_select_fusion.rows, f32[1,3584]{1,0:T(1,128)S(1)} %get-tuple-element.53.decoder_bias, f32[8,256]{1,0:T(8,128)S(1)} %get-tuple-element.94.gates, bf16[3584,128]{1,0:T(8,128)(2,1)S(1)} %get-tuple-element.55.encoder, ...), custom_call_target="tpu_custom_call" | custom-call | bytes 3750912 | tf_op jit(solution)/shard_map/pallas_call | solution.py:162
  13.8 1.2 %collective-permute-start.7 = (bf16[8,3584]{1,0:T(8,128)(2,1)S(1)}, bf16[8,3584]{1,0:T(8,128)(2,1)S(1)}, u32[]{:S(2)}, u32[]{:S(2)}) collective-permute-start(bf16[8,3584]{1,0:T(8,128)(2,1)S(1)} %get-tuple-element.58), channel_id=1, source_target_pairs={{0,2},{1,3},{2,0},{3,1},{4,6},{5,7},{6,4},{7,5},{8,10},{9,11},{10,... | collective-permute-start | bytes 172040 | tf_op jit(solution)/shard_map/ppermute | solution.py:184
  15.1 0.7 %collective-permute-done.5.rows.rows_far = bf16[8,3584]{1,0:T(8,128)(2,1)S(1)} collective-permute-done((bf16[8,3584]{1,0:T(8,128)(2,1)S(1)}, bf16[8,3584]{1,0:T(8,128)(2,1)S(1)}, u32[]{:S(2)}, u32[]{:S(2)}) %collective-permute-start.5) | collective-permute-done | bytes 57376 | tf_op jit(solution)/shard_map/ppermute | solution.py:184
  15.7 0.7 %shard_map.113 = (f32[8,128]{1,0:T(8,128)S(1)}, bf16[8,3584]{1,0:T(8,128)(2,1)S(1)}) custom-call(bf16[8,3584]{1,0:T(8,128)(2,1)S(1)} %collective-permute-done.5.rows.rows_far, f32[1,3584]{1,0:T(1,128)S(1)} %get-tuple-element.53.decoder_bias, f32[8,256]{1,0:T(8,128)S(1)} %get-tuple-element.93.gates.gates_far, ...), custom_call_target="tpu_custom_call" | custom-call | bytes 3750912 | tf_op jit(solution)/shard_map/pallas_call | solution.py:162
  16.4 1.1 %collective-permute-start.9 = (bf16[8,3584]{1,0:T(8,128)(2,1)S(1)}, bf16[8,3584]{1,0:T(8,128)(2,1)S(1)}, u32[]{:S(2)}, u32[]{:S(2)}) collective-permute-start(bf16[8,3584]{1,0:T(8,128)(2,1)S(1)} %get-tuple-element.60), channel_id=1, source_target_pairs={{0,2},{1,3},{2,0},{3,1},{4,6},{5,7},{6,4},{7,5},{8,10},{9,11},{10,... | collective-permute-start | bytes 172040 | tf_op jit(solution)/shard_map/ppermute | solution.py:184
  17.5 0.9 %collective-permute-done.7 = bf16[8,3584]{1,0:T(8,128)(2,1)S(1)} collective-permute-done((bf16[8,3584]{1,0:T(8,128)(2,1)S(1)}, bf16[8,3584]{1,0:T(8,128)(2,1)S(1)}, u32[]{:S(2)}, u32[]{:S(2)}) %collective-permute-start.7) | collective-permute-done | bytes 57376 | tf_op jit(solution)/shard_map/ppermute | solution.py:184
  18.5 1.6 %collective-permute-start.8 = (bf16[8,3584]{1,0:T(8,128)(2,1)S(1)}, bf16[8,3584]{1,0:T(8,128)(2,1)S(1)}, u32[]{:S(2)}, u32[]{:S(2)}) collective-permute-start(bf16[8,3584]{1,0:T(8,128)(2,1)S(1)} %add.101), channel_id=1, source_target_pairs={{0,4},{1,5},{2,6},{3,7},{4,0},{5,1},{6,2},{7,3},{8,12},{9,13},{10,... | collective-permute-start | bytes 172040 | tf_op jit(solution)/shard_map/ppermute | solution.py:184
  20.1 0.5 %collective-permute-done.9 = bf16[8,3584]{1,0:T(8,128)(2,1)S(1)} collective-permute-done((bf16[8,3584]{1,0:T(8,128)(2,1)S(1)}, bf16[8,3584]{1,0:T(8,128)(2,1)S(1)}, u32[]{:S(2)}, u32[]{:S(2)}) %collective-permute-start.9) | collective-permute-done | bytes 57376 | tf_op jit(solution)/shard_map/ppermute | solution.py:184
  20.6 1.5 %collective-permute-start.10 = (bf16[8,3584]{1,0:T(8,128)(2,1)S(1)}, bf16[8,3584]{1,0:T(8,128)(2,1)S(1)}, u32[]{:S(2)}, u32[]{:S(2)}) collective-permute-start(bf16[8,3584]{1,0:T(8,128)(2,1)S(1)} %add.103), channel_id=1, source_target_pairs={{0,4},{1,5},{2,6},{3,7},{4,0},{5,1},{6,2},{7,3},{8,12},{9,13},{10,... | collective-permute-start | bytes 172040 | tf_op jit(solution)/shard_map/ppermute | solution.py:184
  22.2 0.5 %collective-permute-done.8 = bf16[8,3584]{1,0:T(8,128)(2,1)S(1)} collective-permute-done((bf16[8,3584]{1,0:T(8,128)(2,1)S(1)}, bf16[8,3584]{1,0:T(8,128)(2,1)S(1)}, u32[]{:S(2)}, u32[]{:S(2)}) %collective-permute-start.8) | collective-permute-done | bytes 57376 | tf_op jit(solution)/shard_map/ppermute | solution.py:184
  22.7 2.6 %collective-permute-start.12 = (bf16[8,3584]{1,0:T(8,128)(2,1)S(1)}, bf16[8,3584]{1,0:T(8,128)(2,1)S(1)}, u32[]{:S(2)}, u32[]{:S(2)}) collective-permute-start(bf16[8,3584]{1,0:T(8,128)(2,1)S(1)} %add.102.low), channel_id=1, source_target_pairs={{0,8},{1,9},{2,10},{3,11},{4,12},{5,13},{6,14},{7,15},{8,0},{9,1},... | collective-permute-start | bytes 172040 | tf_op jit(solution)/shard_map/ppermute | solution.py:184
  25.4 2.6 %collective-permute-start.11 = (bf16[8,3584]{1,0:T(8,128)(2,1)S(1)}, bf16[8,3584]{1,0:T(8,128)(2,1)S(1)}, u32[]{:S(2)}, u32[]{:S(2)}) collective-permute-start(bf16[8,3584]{1,0:T(8,128)(2,1)S(1)} %add.104.high), channel_id=1, source_target_pairs={{0,8},{1,9},{2,10},{3,11},{4,12},{5,13},{6,14},{7,15},{8,0},{9,1},... | collective-permute-start | bytes 172040 | tf_op jit(solution)/shard_map/ppermute | solution.py:184
  28.0 1.8 %shard_map.114 = (bf16[256,3584]{1,0:T(8,128)(2,1)S(1)}, bf16[3584,256]{1,0:T(8,128)(2,1)S(1)}) custom-call(bf16[3584,128]{1,0:T(8,128)(2,1)} %encoder_far, bf16[128,3584]{1,0:T(8,128)(2,1)} %decoder_far, bf16[3584,128]{1,0:T(8,128)(2,1)S(1)} %collective-permute-done.2.encoder_other, bf16[128,3584]{1,0:T(8,128)(2,1)S(1)} %collective-permute-done.4.decoder_other), custom_call_target="tpu_custom_call" | custom-call | bytes 7340032 | tf_op jit(solution)/shard_map/pallas_call | solution.py:104
  29.8 0.8 %collective-permute-done.11.low_received = bf16[8,3584]{1,0:T(8,128)(2,1)S(1)} collective-permute-done((bf16[8,3584]{1,0:T(8,128)(2,1)S(1)}, bf16[8,3584]{1,0:T(8,128)(2,1)S(1)}, u32[]{:S(2)}, u32[]{:S(2)}) %collective-permute-start.11) | collective-permute-done | bytes 57376 | tf_op jit(solution)/shard_map/ppermute | solution.py:184
  30.5 0.0 collective-permute-done.12.high_received
  30.5 0.7 %shard_map.115 = (bf16[16,3584]{1,0:T(8,128)(2,1)S(1)}, f32[1,3584]{1,0:T(1,128)S(1)}) custom-call(bf16[8,3584]{1,0:T(8,128)(2,1)S(1)} %add.102.low, bf16[8,3584]{1,0:T(8,128)(2,1)S(1)} %collective-permute-done.11.low_received, bf16[8,3584]{1,0:T(8,128)(2,1)S(1)} %maximum_select_fusion.rows, f32[8,256]{1,0:T(8,128)S(1)} %get-tuple-element.94.gates, ...), custom_call_target="tpu_custom_call" | custom-call | bytes 4044800 | tf_op jit(solution)/shard_map/pallas_call | solution.py:162
  31.3 0.0 copy-start.3
  31.3 0.1 collective-permute-start.13
  31.4 0.6 %collective-permute-start.14 = (f32[1,3584]{1,0:T(1,128)S(1)}, f32[1,3584]{1,0:T(1,128)S(1)}, u32[]{:S(2)}, u32[]{:S(2)}) collective-permute-start(f32[1,3584]{1,0:T(1,128)S(1)} %get-tuple-element.71), channel_id=1, source_target_pairs={{0,1},{1,0},{2,3},{3,2},{4,5},{5,4},{6,7},{7,6},{8,9},{9,8},{10,11... | collective-permute-start | bytes 43016 | tf_op jit(solution)/shard_map/ppermute | solution.py:184
  31.9 0.0 collective-permute-done.6
  32.0 0.2 convolution_add_fusion
  32.2 0.4 compare_reduce_fusion
  32.6 0.2 collective-permute-done.14
  32.8 1.2 %collective-permute-start.15 = (f32[1,3584]{1,0:T(1,128)S(1)}, f32[1,3584]{1,0:T(1,128)S(1)}, u32[]{:S(2)}, u32[]{:S(2)}) collective-permute-start(f32[1,3584]{1,0:T(1,128)S(1)} %add.105), channel_id=1, source_target_pairs={{0,2},{1,3},{2,0},{3,1},{4,6},{5,7},{6,4},{7,5},{8,10},{9,11},{10,... | collective-permute-start | bytes 43016 | tf_op jit(solution)/shard_map/ppermute | solution.py:184
  34.1 0.9 %select_reduce_fusion = (f32[128]{0:T(128)}, f32[128]{0:T(128)}, bf16[32,128]{1,0:T(8,128)(2,1)S(1)}) fusion(pred[16,128]{1,0:T(8,128)(4,1)S(1)} %compare_reduce_fusion, pred[16,128]{1,0:T(8,128)(4,1)S(1)} %get-tuple-element.85, f32[128]{0:T(128)S(1)} %copy-done.3, f32[16,128]{1,0:T(8,128)S(1)} %convolution_add_fusion, f32[8,128]{1,0:T(8,128)S(1)} %get-tuple-element.74, ...), kind=kOutput, calls=%fused_computation.20 | convolution fusion | flops 29425408 | bytes 1177600 | tf_op jit(solution)/shard_map/dot_general | solution.py:27
  35.0 1.6 %collective-permute-done.15 = f32[1,3584]{1,0:T(1,128)S(1)} collective-permute-done((f32[1,3584]{1,0:T(1,128)S(1)}, f32[1,3584]{1,0:T(1,128)S(1)}, u32[]{:S(2)}, u32[]{:S(2)}) %collective-permute-start.15) | collective-permute-done | bytes 14368 | tf_op jit(solution)/shard_map/ppermute | solution.py:184
  36.6 1.8 %collective-permute-start.16 = (f32[1,3584]{1,0:T(1,128)S(1)}, f32[1,3584]{1,0:T(1,128)S(1)}, u32[]{:S(2)}, u32[]{:S(2)}) collective-permute-start(f32[1,3584]{1,0:T(1,128)S(1)} %add.108), channel_id=1, source_target_pairs={{0,4},{1,5},{2,6},{3,7},{4,0},{5,1},{6,2},{7,3},{8,12},{9,13},{10,... | collective-permute-start | bytes 43016 | tf_op jit(solution)/shard_map/ppermute | solution.py:184
  38.4 1.3 %convolution_convert_fusion = bf16[128,3584]{1,0:T(8,128)(2,1)} fusion(bf16[32,3584]{1,0:T(8,128)(2,1)S(1)} %constant_dynamic-update-slice_fusion.2, f32[16,128]{1,0:T(8,128)S(1)} %convolution_add_fusion, f32[8,128]{1,0:T(8,128)S(1)} %get-tuple-element.74, f32[8,128]{1,0:T(8,128)S(1)} %get-tuple-element.73, pred[16,128]{1,0:T(8,128)(4,1)S(1)} %compare_reduce_fusion, ...), kind=kOutput, calls=%fused_computation | convolution fusion | flops 29851648 | bytes 1167360 | tf_op jit(solution)/shard_map/dot_general | solution.py:31
  39.8 0.1 shard_map.116
  39.9 0.5 collective-permute-done.16
  40.4 2.7 %collective-permute-start.17 = (f32[1,3584]{1,0:T(1,128)S(1)}, f32[1,3584]{1,0:T(1,128)S(1)}, u32[]{:S(2)}, u32[]{:S(2)}) collective-permute-start(f32[1,3584]{1,0:T(1,128)S(1)} %add.109), channel_id=1, source_target_pairs={{0,8},{1,9},{2,10},{3,11},{4,12},{5,13},{6,14},{7,15},{8,0},{9,1},... | collective-permute-start | bytes 43016 | tf_op jit(solution)/shard_map/ppermute | solution.py:184
  43.1 1.4 %convolution_convert_fusion.1 = bf16[3584,128]{1,0:T(8,128)(2,1)} fusion(bf16[32,128]{1,0:T(8,128)(2,1)S(1)} %select_convert_fusion.1, bf16[16,3584]{1,0:T(8,128)(2,1)S(1)} %get-tuple-element.88, bf16[16,3584]{1,0:T(8,128)(2,1)S(1)} %get-tuple-element.87), kind=kOutput, calls=%fused_computation.1 | convolution fusion | flops 30277632 | bytes 1155072 | tf_op jit(solution)/shard_map/dot_general | solution.py:31
  44.4 0.6 %collective-permute-done.17 = f32[1,3584]{1,0:T(1,128)S(1)} collective-permute-done((f32[1,3584]{1,0:T(1,128)S(1)}, f32[1,3584]{1,0:T(1,128)S(1)}, u32[]{:S(2)}, u32[]{:S(2)}) %collective-permute-start.17) | collective-permute-done | bytes 14368 | tf_op jit(solution)/shard_map/ppermute | solution.py:184
  45.1 0.7 %subtract_reduce_fusion.1 = f32[3584]{0:T(1024)} fusion(f32[1,3584]{1,0:T(1,128)S(1)} %shard_map.116, f32[1,3584]{1,0:T(1,128)S(1)} %add.109, f32[1,3584]{1,0:T(1,128)S(1)} %collective-permute-done.17), kind=kLoop, calls=%fused_computation.18 | loop fusion | flops 7168 | bytes 57344 | tf_op jit(solution)/shard_map/sub | solution.py:295
  (34 shorter events, 0.3 us)
Async XLA Ops:
  0.6 5.8 %collective-permute-start = (bf16[2,3584]{1,0:T(2,128)(2,1)}, bf16[2,3584]{1,0:T(2,128)(2,1)S(1)}, u32[]{:S(2)}, u32[]{:S(2)}) collective-permute-start(bf16[2,3584]{1,0:T(2,128)(2,1)} %refs_0_.1), channel_id=1, source_target_pairs={{0,2},{1,3},{2,0},{3,1},{4,6},{5,7},{6,4},{7,5},{8,10},{9,11},{10,... | collective-permute-start | bytes 43016 | tf_op jit(solution)/shard_map/ppermute | solution.py:184
  3.7 9.5 %collective-permute-start.2 = (bf16[3584,128]{1,0:T(8,128)(2,1)}, bf16[3584,128]{1,0:T(8,128)(2,1)S(1)}, u32[]{:S(2)}, u32[]{:S(2)}) collective-permute-start(bf16[3584,128]{1,0:T(8,128)(2,1)} %encoder_far), channel_id=1, source_target_pairs={{0,1},{1,0},{2,3},{3,2},{4,5},{5,4},{6,7},{7,6},{8,9},{9,8},{10,11... | collective-permute-start | bytes 2752520 | tf_op jit(solution)/shard_map/ppermute | solution.py:184
  3.7 9.5 %collective-permute-start.4 = (bf16[128,3584]{1,0:T(8,128)(2,1)}, bf16[128,3584]{1,0:T(8,128)(2,1)S(1)}, u32[]{:S(2)}, u32[]{:S(2)}) collective-permute-start(bf16[128,3584]{1,0:T(8,128)(2,1)} %decoder_far), channel_id=1, source_target_pairs={{0,1},{1,0},{2,3},{3,2},{4,5},{5,4},{6,7},{7,6},{8,9},{9,8},{10,11... | collective-permute-start | bytes 2752520 | tf_op jit(solution)/shard_map/ppermute | solution.py:184
  4.2 9.0 %collective-permute-start.3 = (f32[1,128]{1,0:T(1,128)}, f32[1,128]{1,0:T(1,128)S(1)}, u32[]{:S(2)}, u32[]{:S(2)}) collective-permute-start(f32[1,128]{1,0:T(1,128)} %bitcast.17), channel_id=1, source_target_pairs={{0,1},{1,0},{2,3},{3,2},{4,5},{5,4},{6,7},{7,6},{8,9},{9,8},{10,11... | collective-permute-start | bytes 1544 | tf_op jit(solution)/shard_map/ppermute | solution.py:184
  6.5 3.9 %collective-permute-start.1 = (bf16[4,3584]{1,0:T(4,128)(2,1)S(1)}, bf16[4,3584]{1,0:T(4,128)(2,1)S(1)}, u32[]{:S(2)}, u32[]{:S(2)}) collective-permute-start(bf16[4,3584]{1,0:T(4,128)(2,1)S(1)} %maximum_select_fusion.1), channel_id=1, source_target_pairs={{0,4},{1,5},{2,6},{3,7},{4,0},{5,1},{6,2},{7,3},{8,12},{9,13},{10,... | collective-permute-start | bytes 86024 | tf_op jit(solution)/shard_map/ppermute | solution.py:184
  10.5 5.2 %collective-permute-start.5 = (bf16[8,3584]{1,0:T(8,128)(2,1)S(1)}, bf16[8,3584]{1,0:T(8,128)(2,1)S(1)}, u32[]{:S(2)}, u32[]{:S(2)}) collective-permute-start(bf16[8,3584]{1,0:T(8,128)(2,1)S(1)} %maximum_select_fusion.rows), channel_id=1, source_target_pairs={{0,8},{1,9},{2,10},{3,11},{4,12},{5,13},{6,14},{7,15},{8,0},{9,1},... | collective-permute-start | bytes 172040 | tf_op jit(solution)/shard_map/ppermute | solution.py:184
  13.8 4.6 %collective-permute-start.7 = (bf16[8,3584]{1,0:T(8,128)(2,1)S(1)}, bf16[8,3584]{1,0:T(8,128)(2,1)S(1)}, u32[]{:S(2)}, u32[]{:S(2)}) collective-permute-start(bf16[8,3584]{1,0:T(8,128)(2,1)S(1)} %get-tuple-element.58), channel_id=1, source_target_pairs={{0,2},{1,3},{2,0},{3,1},{4,6},{5,7},{6,4},{7,5},{8,10},{9,11},{10,... | collective-permute-start | bytes 172040 | tf_op jit(solution)/shard_map/ppermute | solution.py:184
  16.4 4.2 %collective-permute-start.9 = (bf16[8,3584]{1,0:T(8,128)(2,1)S(1)}, bf16[8,3584]{1,0:T(8,128)(2,1)S(1)}, u32[]{:S(2)}, u32[]{:S(2)}) collective-permute-start(bf16[8,3584]{1,0:T(8,128)(2,1)S(1)} %get-tuple-element.60), channel_id=1, source_target_pairs={{0,2},{1,3},{2,0},{3,1},{4,6},{5,7},{6,4},{7,5},{8,10},{9,11},{10,... | collective-permute-start | bytes 172040 | tf_op jit(solution)/shard_map/ppermute | solution.py:184
  18.5 4.2 %collective-permute-start.8 = (bf16[8,3584]{1,0:T(8,128)(2,1)S(1)}, bf16[8,3584]{1,0:T(8,128)(2,1)S(1)}, u32[]{:S(2)}, u32[]{:S(2)}) collective-permute-start(bf16[8,3584]{1,0:T(8,128)(2,1)S(1)} %add.101), channel_id=1, source_target_pairs={{0,4},{1,5},{2,6},{3,7},{4,0},{5,1},{6,2},{7,3},{8,12},{9,13},{10,... | collective-permute-start | bytes 172040 | tf_op jit(solution)/shard_map/ppermute | solution.py:184
  20.6 4.7 %collective-permute-start.10 = (bf16[8,3584]{1,0:T(8,128)(2,1)S(1)}, bf16[8,3584]{1,0:T(8,128)(2,1)S(1)}, u32[]{:S(2)}, u32[]{:S(2)}) collective-permute-start(bf16[8,3584]{1,0:T(8,128)(2,1)S(1)} %add.103), channel_id=1, source_target_pairs={{0,4},{1,5},{2,6},{3,7},{4,0},{5,1},{6,2},{7,3},{8,12},{9,13},{10,... | collective-permute-start | bytes 172040 | tf_op jit(solution)/shard_map/ppermute | solution.py:184
  22.7 7.8 %collective-permute-start.12 = (bf16[8,3584]{1,0:T(8,128)(2,1)S(1)}, bf16[8,3584]{1,0:T(8,128)(2,1)S(1)}, u32[]{:S(2)}, u32[]{:S(2)}) collective-permute-start(bf16[8,3584]{1,0:T(8,128)(2,1)S(1)} %add.102.low), channel_id=1, source_target_pairs={{0,8},{1,9},{2,10},{3,11},{4,12},{5,13},{6,14},{7,15},{8,0},{9,1},... | collective-permute-start | bytes 172040 | tf_op jit(solution)/shard_map/ppermute | solution.py:184
  25.4 5.1 %collective-permute-start.11 = (bf16[8,3584]{1,0:T(8,128)(2,1)S(1)}, bf16[8,3584]{1,0:T(8,128)(2,1)S(1)}, u32[]{:S(2)}, u32[]{:S(2)}) collective-permute-start(bf16[8,3584]{1,0:T(8,128)(2,1)S(1)} %add.104.high), channel_id=1, source_target_pairs={{0,8},{1,9},{2,10},{3,11},{4,12},{5,13},{6,14},{7,15},{8,0},{9,1},... | collective-permute-start | bytes 172040 | tf_op jit(solution)/shard_map/ppermute | solution.py:184
  28.0 4.0 %collective-permute-start.6 = (bf16[16,3584]{1,0:T(8,128)(2,1)S(1)}, bf16[16,3584]{1,0:T(8,128)(2,1)S(1)}, u32[]{:S(2)}, u32[]{:S(2)}) collective-permute-start(bf16[16,3584]{1,0:T(8,128)(2,1)S(1)} %constant_dynamic-update-slice_fusion), channel_id=1, source_target_pairs={{0,1},{1,0},{2,3},{3,2},{4,5},{5,4},{6,7},{7,6},{8,9},{9,8},{10,11... | collective-permute-start | bytes 344072 | tf_op jit(solution)/shard_map/ppermute | solution.py:184
  30.5 1.4 %copy-start = (bf16[3584,128]{1,0:T(8,128)(2,1)S(1)}, bf16[3584,128]{1,0:T(8,128)(2,1)}, u32[]{:S(2)}) copy-start(bf16[3584,128]{1,0:T(8,128)(2,1)} %encoder_far) | copy-start | bytes 2752516
  30.5 1.4 %copy-start.2 = (f32[128]{0:T(128)S(1)}, f32[128]{0:T(128)}, u32[]{:S(2)}) copy-start(f32[128]{0:T(128)} %refs_2_) | copy-start | bytes 1540
  31.3 2.8 %copy-start.1 = (bf16[128,3584]{1,0:T(8,128)(2,1)S(1)}, bf16[128,3584]{1,0:T(8,128)(2,1)}, u32[]{:S(2)}) copy-start(bf16[128,3584]{1,0:T(8,128)(2,1)} %decoder_far) | copy-start | bytes 2752516
  31.3 2.8 %copy-start.3 = (f32[128]{0:T(128)S(1)}, f32[128]{0:T(128)}, u32[]{:S(2)}) copy-start(f32[128]{0:T(128)} %param.11) | copy-start | bytes 1540
  31.3 1.5 %collective-permute-start.13 = (bf16[16,3584]{1,0:T(8,128)(2,1)S(1)}, bf16[16,3584]{1,0:T(8,128)(2,1)S(1)}, u32[]{:S(2)}, u32[]{:S(2)}) collective-permute-start(bf16[16,3584]{1,0:T(8,128)(2,1)S(1)} %get-tuple-element.69.errors), channel_id=1, source_target_pairs={{0,1},{1,0},{2,3},{3,2},{4,5},{5,4},{6,7},{7,6},{8,9},{9,8},{10,11... | collective-permute-start | bytes 344072 | tf_op jit(solution)/shard_map/ppermute | solution.py:184
  31.4 1.4 %collective-permute-start.14 = (f32[1,3584]{1,0:T(1,128)S(1)}, f32[1,3584]{1,0:T(1,128)S(1)}, u32[]{:S(2)}, u32[]{:S(2)}) collective-permute-start(f32[1,3584]{1,0:T(1,128)S(1)} %get-tuple-element.71), channel_id=1, source_target_pairs={{0,1},{1,0},{2,3},{3,2},{4,5},{5,4},{6,7},{7,6},{8,9},{9,8},{10,11... | collective-permute-start | bytes 43016 | tf_op jit(solution)/shard_map/ppermute | solution.py:184
  32.8 3.8 %collective-permute-start.15 = (f32[1,3584]{1,0:T(1,128)S(1)}, f32[1,3584]{1,0:T(1,128)S(1)}, u32[]{:S(2)}, u32[]{:S(2)}) collective-permute-start(f32[1,3584]{1,0:T(1,128)S(1)} %add.105), channel_id=1, source_target_pairs={{0,2},{1,3},{2,0},{3,1},{4,6},{5,7},{6,4},{7,5},{8,10},{9,11},{10,... | collective-permute-start | bytes 43016 | tf_op jit(solution)/shard_map/ppermute | solution.py:184
  36.6 3.8 %collective-permute-start.16 = (f32[1,3584]{1,0:T(1,128)S(1)}, f32[1,3584]{1,0:T(1,128)S(1)}, u32[]{:S(2)}, u32[]{:S(2)}) collective-permute-start(f32[1,3584]{1,0:T(1,128)S(1)} %add.108), channel_id=1, source_target_pairs={{0,4},{1,5},{2,6},{3,7},{4,0},{5,1},{6,2},{7,3},{8,12},{9,13},{10,... | collective-permute-start | bytes 43016 | tf_op jit(solution)/shard_map/ppermute | solution.py:184
  40.4 4.7 %collective-permute-start.17 = (f32[1,3584]{1,0:T(1,128)S(1)}, f32[1,3584]{1,0:T(1,128)S(1)}, u32[]{:S(2)}, u32[]{:S(2)}) collective-permute-start(f32[1,3584]{1,0:T(1,128)S(1)} %add.109), channel_id=1, source_target_pairs={{0,8},{1,9},{2,10},{3,11},{4,12},{5,13},{6,14},{7,15},{8,0},{9,1},... | collective-permute-start | bytes 43016 | tf_op jit(solution)/shard_map/ppermute | solution.py:184

commit v6 on v5

--- a/solution.py
+++ b/solution.py
@@ -194,33 +194,38 @@
     bias_other = swap(encoder_bias[None], 1)
 
     per_device, depth = rows_in.shape
-    ids = active_ids.reshape(2, count // 4, 2, per_device, active_ids.shape[1])
+    slots = count // 4
     side = jnp.where((me & hops[-1]) == 0, 0, 1)
 
-    def listed(half, part):
-        one = lax.dynamic_index_in_dim(ids, half, 0, keepdims=False)
-        one = lax.dynamic_index_in_dim(one, part, 1, keepdims=False)
-        return one.reshape(count // 4 * per_device, -1)
-
-    lists = jnp.concatenate([listed(side, core), listed(1 - side, core)])
-    lists_other = jnp.concatenate([listed(side, 1 - core), listed(1 - side, 1 - core)])
-
-    block, bias_row = stage(rows_in, decoder_bias)
+    block, bias_row, ids = stage(rows_in, decoder_bias, active_ids)
     for bit in hops[:-1]:
         if bit == hops[-2]:
             weights = (encoder_weight, decoder_weight, encoder_bias)
-            block, weights, lists = lax.optimization_barrier((block, weights, lists))
+            block, weights = lax.optimization_barrier((block, weights))
         other = swap(rows_in if bit == hops[0] else block, bit)
         low = jnp.concatenate([block, other], axis=0)
         high = jnp.concatenate([other, block], axis=0)
         block = jnp.where((me & bit) == 0, low, high)
     encoder_near, decoder_near, encoder_row = stage(*weights)
-    block, encoder_near, decoder_near, encoder_row = lax.optimization_barrier(
-        (block, encoder_near, decoder_near, encoder_row)
+    block, ids, encoder_near, decoder_near, encoder_row = lax.optimization_barrier(
+        (block, ids, encoder_near, decoder_near, encoder_row)
     )
     rows = block
     rows_far = swap(block, hops[-1])
     half_rows = rows.shape[0]
+
+    def quarter(half, part):
+        firsts = [((half * slots + slot) * 2 + part) * per_device for slot in range(slots)]
+        return jnp.concatenate([ids[first : first + per_device] for first in firsts])
+
+    quarters = [[quarter(half, part) for part in range(2)] for half in range(2)]
+
+    def listed(half, part):
+        near, far = [jnp.where(part == 0, *pair) for pair in quarters]
+        return jnp.where(half == 0, near, far)
+
+    lists = jnp.concatenate([listed(side, core), listed(1 - side, core)])
+    lists_other = jnp.concatenate([listed(side, 1 - core), listed(1 - side, 1 - core)])
 
     def center(part):
         return (part.astype(F32) - bias_row).astype(BF16)
@@ -260,7 +265,9 @@
     part = part + swap(part, 1)
     errors_other, part = lax.optimization_barrier((errors_other, part))
 
-    rows_other, lists_other, _ = lax.optimization_barrier((rows_other, lists_other, errors))
+    rows_other, lists_other, threshold, _ = lax.optimization_barrier(
+        (rows_other, lists_other, threshold, errors)
+    )
     centered_other = center(rows_other)
     gate_rest = opened(lists_other, me * width, width)
     preact_rest = dot(centered_other, encoder_weight) + encoder_bias
@@ -285,13 +292,13 @@
     def encoder_output():
         return dot_rows(every_centered, small[2]).astype(BF16)
 
-    part = part + swap(part, hops[0])
+    part = part + swap(part, hops[0] | 1)
     small, part = lax.optimization_barrier((small_outputs(), part))
-    part = part + swap(part, hops[1])
+    part = part + swap(part, hops[1] | 1)
     grad_decoder, part = lax.optimization_barrier((decoder_output(), part))
     (error_sum,) = near(sum_kernel, (errors, errors_other), (((1, depth), F32),))
     for bit in hops[2:]:
-        part = part + swap(part, bit)
+        part = part + swap(part, bit | 1)
     grad_decoder_bias = (error_sum - part).reshape(depth)
     grad_encoder = encoder_output()
     grad_threshold, grad_encoder_bias, _ = small

time: 46 us -> 44.1 us (0.959)
  waiting for transfers between devices: 6.66 us -> 5.81 us
  local copies, waits for them, and re-layouts: 0.79 us -> 0.06 us
  other arithmetic: 2.39 us -> 1.81 us
    ppermute x18, waiting for transfers between devices: 6.66 us -> 5.81 us  [swap(): return lax.ppermute(array, 'latent', [(i, i ^ bit) for i in range(count)])]
    dynamic_slice x1 -> x0, local copies, waits for them, and re-layouts: 0.74 us -> none  [listed(): one = lax.dynamic_index_in_dim(one, part, 1, keepdims=False)]
    neg x1, other arithmetic: 0.66 us -> 0.01 us  [small_outputs(): -threshold * code_grad * kernel - SPARSITY * kernel]
  transfers between devices with their start and end apart: 18 -> 18, of which waited for: 10 -> 11; matrix products, arithmetic and copies ran while one was open for 14% -> 12% of each run, Pallas kernels for 14% -> 14%
where the time goes in v6:
time: 44.1 us; the launch traced here: 43.8 us
  starting transfers between devices  25.1 us (57%)
  Pallas kernels  6.25 us (14%)
  waiting for transfers between devices  5.81 us (13%)
  matrix products  3.89 us (9%)
  other arithmetic  1.81 us (4%)
  between operations  0.87 us (2%)
    ppermute x18, starting transfers between devices, swap(): return lax.ppermute(array, 'latent', [(i, i ^ bit) for i in range(count)])  25.1 us
    ppermute x18, waiting for transfers between devices, swap(): return lax.ppermute(array, 'latent', [(i, i ^ bit) for i in range(count)])  5.81 us
    dot_general x2, matrix products, dot_rows(): lax.dot_general(a, b, (((0,), (0,)), ((), ())), preferred_element_type=F32)  2.73 us
    pallas_call x2, Pallas kernels, stage(): pl.pallas_call(stage_kernel, in_specs=[pl.BlockSpec(memory_space=pltpu.HB...  2.26 us
    pallas_call x4, Pallas kernels, near(): pl.pallas_call(kernel, in_specs=[whole] * len(arrays), out_specs=[whole]...  2.2 us
    pallas_call x1, Pallas kernels, turn(): pl.pallas_call(turn_kernel, in_specs=[far, far, whole, whole], out_specs=...  1.79 us
    dot_general x1, matrix products, dot_last(): lax.dot_general(a, b, (((1,), (1,)), ((), ())), preferred_element_type=F32)  0.93 us
  transfers between devices with their start and end apart: 18, of which 11 were waited for; matrix products, arithmetic and copies ran while one was open for 12% of the time, Pallas kernels for 14%

profile of v6, /device:TPU:0, one launch (start us, length us, event | category | flops | bytes accessed | tf_op | source)
XLA Modules:
  0.0 43.8 jit_solution(405143879670002913)
XLA Ops:
  0.6 3.0 %collective-permute-start = (bf16[2,3584]{1,0:T(2,128)(2,1)}, bf16[2,3584]{1,0:T(2,128)(2,1)S(1)}, u32[]{:S(2)}, u32[]{:S(2)}) collective-permute-start(bf16[2,3584]{1,0:T(2,128)(2,1)} %refs_0_.1), channel_id=1, source_target_pairs={{0,2},{1,3},{2,0},{3,1},{4,6},{5,7},{6,4},{7,5},{8,10},{9,11},{10,... | collective-permute-start | bytes 43016 | tf_op jit(solution)/shard_map/ppermute | solution.py:184
  3.7 0.0 collective-permute-start.2
  3.7 0.5 %collective-permute-start.4 = (bf16[128,3584]{1,0:T(8,128)(2,1)}, bf16[128,3584]{1,0:T(8,128)(2,1)S(1)}, u32[]{:S(2)}, u32[]{:S(2)}) collective-permute-start(bf16[128,3584]{1,0:T(8,128)(2,1)} %decoder_far), channel_id=1, source_target_pairs={{0,1},{1,0},{2,3},{3,2},{4,5},{5,4},{6,7},{7,6},{8,9},{9,8},{10,11... | collective-permute-start | bytes 2752520 | tf_op jit(solution)/shard_map/ppermute | solution.py:184
  4.2 0.0 collective-permute-start.3
  4.2 0.8 %shard_map.110 = (bf16[2,3584]{1,0:T(2,128)(2,1)S(1)}, f32[1,3584]{1,0:T(1,128)S(1)}, s32[32,128]{1,0:T(8,128)S(1)}) custom-call(bf16[2,3584]{1,0:T(2,128)(2,1)} %refs_0_.1, f32[3584]{0:T(1024)} %refs_1_.1, s32[32,128]{1,0:T(8,128)} %refs_2_.1), custom_call_target="tpu_custom_call" | custom-call | bytes 90112 | tf_op jit(solution)/shard_map/pallas_call | solution.py:149
  5.0 0.6 %collective-permute-done = bf16[2,3584]{1,0:T(2,128)(2,1)S(1)} collective-permute-done((bf16[2,3584]{1,0:T(2,128)(2,1)}, bf16[2,3584]{1,0:T(2,128)(2,1)S(1)}, u32[]{:S(2)}, u32[]{:S(2)}) %collective-permute-start) | collective-permute-done | bytes 14368 | tf_op jit(solution)/shard_map/ppermute | solution.py:184
  5.6 0.1 maximum_select_fusion.1
  5.6 2.1 %collective-permute-start.1 = (bf16[4,3584]{1,0:T(4,128)(2,1)S(1)}, bf16[4,3584]{1,0:T(4,128)(2,1)S(1)}, u32[]{:S(2)}, u32[]{:S(2)}) collective-permute-start(bf16[4,3584]{1,0:T(4,128)(2,1)S(1)} %maximum_select_fusion.1), channel_id=1, source_target_pairs={{0,4},{1,5},{2,6},{3,7},{4,0},{5,1},{6,2},{7,3},{8,12},{9,13},{10,... | collective-permute-start | bytes 86024 | tf_op jit(solution)/shard_map/ppermute | solution.py:184
  7.8 1.5 %shard_map.111 = (bf16[3584,128]{1,0:T(8,128)(2,1)S(1)}, bf16[128,3584]{1,0:T(8,128)(2,1)S(1)}, f32[1,128]{1,0:T(1,128)S(1)}) custom-call(bf16[3584,128]{1,0:T(8,128)(2,1)} %encoder_far, bf16[128,3584]{1,0:T(8,128)(2,1)} %decoder_far, f32[128]{0:T(128)} %refs_2_.2), custom_call_target="tpu_custom_call" | custom-call | bytes 3671040 | tf_op jit(solution)/shard_map/pallas_call | solution.py:149
  9.3 0.3 collective-permute-done.1
  9.6 0.1 maximum_select_fusion.rows
  9.8 3.1 %collective-permute-start.5 = (bf16[8,3584]{1,0:T(8,128)(2,1)S(1)}, bf16[8,3584]{1,0:T(8,128)(2,1)S(1)}, u32[]{:S(2)}, u32[]{:S(2)}) collective-permute-start(bf16[8,3584]{1,0:T(8,128)(2,1)S(1)} %maximum_select_fusion.rows), channel_id=1, source_target_pairs={{0,8},{1,9},{2,10},{3,11},{4,12},{5,13},{6,14},{7,15},{8,0},{9,1},... | collective-permute-start | bytes 172040 | tf_op jit(solution)/shard_map/ppermute | solution.py:184
  12.9 0.4 compare_reduce_fusion.2
  13.3 0.0 collective-permute-done.4.decoder_other
  13.3 0.7 %shard_map.112 = (f32[8,128]{1,0:T(8,128)S(1)}, bf16[8,3584]{1,0:T(8,128)(2,1)S(1)}) custom-call(bf16[8,3584]{1,0:T(8,128)(2,1)S(1)} %maximum_select_fusion.rows, f32[1,3584]{1,0:T(1,128)S(1)} %get-tuple-element.56.decoder_bias, f32[8,256]{1,0:T(8,128)S(1)} %get-tuple-element.94.gates, bf16[3584,128]{1,0:T(8,128)(2,1)S(1)} %get-tuple-element.58.encoder, ...), custom_call_target="tpu_custom_call" | custom-call | bytes 3750912 | tf_op jit(solution)/shard_map/pallas_call | solution.py:162
  14.0 1.6 %collective-permute-start.7 = (bf16[8,3584]{1,0:T(8,128)(2,1)S(1)}, bf16[8,3584]{1,0:T(8,128)(2,1)S(1)}, u32[]{:S(2)}, u32[]{:S(2)}) collective-permute-start(bf16[8,3584]{1,0:T(8,128)(2,1)S(1)} %get-tuple-element.61), channel_id=1, source_target_pairs={{0,2},{1,3},{2,0},{3,1},{4,6},{5,7},{6,4},{7,5},{8,10},{9,11},{10,... | collective-permute-start | bytes 172040 | tf_op jit(solution)/shard_map/ppermute | solution.py:184
  15.6 0.0 collective-permute-done.5.rows.rows_far
  15.6 0.7 %shard_map.113 = (f32[8,128]{1,0:T(8,128)S(1)}, bf16[8,3584]{1,0:T(8,128)(2,1)S(1)}) custom-call(bf16[8,3584]{1,0:T(8,128)(2,1)S(1)} %collective-permute-done.5.rows.rows_far, f32[1,3584]{1,0:T(1,128)S(1)} %get-tuple-element.56.decoder_bias, f32[8,256]{1,0:T(8,128)S(1)} %get-tuple-element.93.gates.gates_far, ...), custom_call_target="tpu_custom_call" | custom-call | bytes 3750912 | tf_op jit(solution)/shard_map/pallas_call | solution.py:162
  16.3 1.3 %collective-permute-start.9 = (bf16[8,3584]{1,0:T(8,128)(2,1)S(1)}, bf16[8,3584]{1,0:T(8,128)(2,1)S(1)}, u32[]{:S(2)}, u32[]{:S(2)}) collective-permute-start(bf16[8,3584]{1,0:T(8,128)(2,1)S(1)} %get-tuple-element.63), channel_id=1, source_target_pairs={{0,2},{1,3},{2,0},{3,1},{4,6},{5,7},{6,4},{7,5},{8,10},{9,11},{10,... | collective-permute-start | bytes 172040 | tf_op jit(solution)/shard_map/ppermute | solution.py:184
  17.6 0.6 %collective-permute-done.7 = bf16[8,3584]{1,0:T(8,128)(2,1)S(1)} collective-permute-done((bf16[8,3584]{1,0:T(8,128)(2,1)S(1)}, bf16[8,3584]{1,0:T(8,128)(2,1)S(1)}, u32[]{:S(2)}, u32[]{:S(2)}) %collective-permute-start.7) | collective-permute-done | bytes 57376 | tf_op jit(solution)/shard_map/ppermute | solution.py:184
  18.3 1.6 %collective-permute-start.8 = (bf16[8,3584]{1,0:T(8,128)(2,1)S(1)}, bf16[8,3584]{1,0:T(8,128)(2,1)S(1)}, u32[]{:S(2)}, u32[]{:S(2)}) collective-permute-start(bf16[8,3584]{1,0:T(8,128)(2,1)S(1)} %add.60), channel_id=1, source_target_pairs={{0,4},{1,5},{2,6},{3,7},{4,0},{5,1},{6,2},{7,3},{8,12},{9,13},{10,... | collective-permute-start | bytes 172040 | tf_op jit(solution)/shard_map/ppermute | solution.py:184
  19.9 0.6 %collective-permute-done.9 = bf16[8,3584]{1,0:T(8,128)(2,1)S(1)} collective-permute-done((bf16[8,3584]{1,0:T(8,128)(2,1)S(1)}, bf16[8,3584]{1,0:T(8,128)(2,1)S(1)}, u32[]{:S(2)}, u32[]{:S(2)}) %collective-permute-start.9) | collective-permute-done | bytes 57376 | tf_op jit(solution)/shard_map/ppermute | solution.py:184
  20.5 1.6 %collective-permute-start.10 = (bf16[8,3584]{1,0:T(8,128)(2,1)S(1)}, bf16[8,3584]{1,0:T(8,128)(2,1)S(1)}, u32[]{:S(2)}, u32[]{:S(2)}) collective-permute-start(bf16[8,3584]{1,0:T(8,128)(2,1)S(1)} %add.62), channel_id=1, source_target_pairs={{0,4},{1,5},{2,6},{3,7},{4,0},{5,1},{6,2},{7,3},{8,12},{9,13},{10,... | collective-permute-start | bytes 172040 | tf_op jit(solution)/shard_map/ppermute | solution.py:184
  22.2 1.0 %collective-permute-done.8 = bf16[8,3584]{1,0:T(8,128)(2,1)S(1)} collective-permute-done((bf16[8,3584]{1,0:T(8,128)(2,1)S(1)}, bf16[8,3584]{1,0:T(8,128)(2,1)S(1)}, u32[]{:S(2)}, u32[]{:S(2)}) %collective-permute-start.8) | collective-permute-done | bytes 57376 | tf_op jit(solution)/shard_map/ppermute | solution.py:184
  23.1 1.9 %collective-permute-start.12 = (bf16[8,3584]{1,0:T(8,128)(2,1)S(1)}, bf16[8,3584]{1,0:T(8,128)(2,1)S(1)}, u32[]{:S(2)}, u32[]{:S(2)}) collective-permute-start(bf16[8,3584]{1,0:T(8,128)(2,1)S(1)} %add.61.low), channel_id=1, source_target_pairs={{0,8},{1,9},{2,10},{3,11},{4,12},{5,13},{6,14},{7,15},{8,0},{9,1},... | collective-permute-start | bytes 172040 | tf_op jit(solution)/shard_map/ppermute | solution.py:184
  25.1 0.1 collective-permute-done.10
  25.2 2.1 %collective-permute-start.11 = (bf16[8,3584]{1,0:T(8,128)(2,1)S(1)}, bf16[8,3584]{1,0:T(8,128)(2,1)S(1)}, u32[]{:S(2)}, u32[]{:S(2)}) collective-permute-start(bf16[8,3584]{1,0:T(8,128)(2,1)S(1)} %add.63.high), channel_id=1, source_target_pairs={{0,8},{1,9},{2,10},{3,11},{4,12},{5,13},{6,14},{7,15},{8,0},{9,1},... | collective-permute-start | bytes 172040 | tf_op jit(solution)/shard_map/ppermute | solution.py:184
  27.3 1.8 %shard_map.114 = (bf16[256,3584]{1,0:T(8,128)(2,1)S(1)}, bf16[3584,256]{1,0:T(8,128)(2,1)S(1)}) custom-call(bf16[3584,128]{1,0:T(8,128)(2,1)} %encoder_far, bf16[128,3584]{1,0:T(8,128)(2,1)} %decoder_far, bf16[3584,128]{1,0:T(8,128)(2,1)S(1)} %collective-permute-done.2.encoder_other, bf16[128,3584]{1,0:T(8,128)(2,1)S(1)} %collective-permute-done.4.decoder_other), custom_call_target="tpu_custom_call" | custom-call | bytes 7340032 | tf_op jit(solution)/shard_map/pallas_call | solution.py:104
  29.1 1.3 %collective-permute-done.11.low_received = bf16[8,3584]{1,0:T(8,128)(2,1)S(1)} collective-permute-done((bf16[8,3584]{1,0:T(8,128)(2,1)S(1)}, bf16[8,3584]{1,0:T(8,128)(2,1)S(1)}, u32[]{:S(2)}, u32[]{:S(2)}) %collective-permute-start.11) | collective-permute-done | bytes 57376 | tf_op jit(solution)/shard_map/ppermute | solution.py:184
  30.3 0.0 collective-permute-done.12.high_received
  30.3 0.7 %shard_map.115 = (bf16[16,3584]{1,0:T(8,128)(2,1)S(1)}, f32[1,3584]{1,0:T(1,128)S(1)}) custom-call(bf16[8,3584]{1,0:T(8,128)(2,1)S(1)} %add.61.low, bf16[8,3584]{1,0:T(8,128)(2,1)S(1)} %collective-permute-done.11.low_received, bf16[8,3584]{1,0:T(8,128)(2,1)S(1)} %maximum_select_fusion.rows, f32[8,256]{1,0:T(8,128)S(1)} %get-tuple-element.94.gates, ...), custom_call_target="tpu_custom_call" | custom-call | bytes 4044800 | tf_op jit(solution)/shard_map/pallas_call | solution.py:162
  31.0 0.1 collective-permute-start.13
  31.1 0.6 %collective-permute-start.14 = (f32[1,3584]{1,0:T(1,128)S(1)}, f32[1,3584]{1,0:T(1,128)S(1)}, u32[]{:S(2)}, u32[]{:S(2)}) collective-permute-start(f32[1,3584]{1,0:T(1,128)S(1)} %get-tuple-element.75), channel_id=1, source_target_pairs={{0,1},{1,0},{2,3},{3,2},{4,5},{5,4},{6,7},{7,6},{8,9},{9,8},{10,11... | collective-permute-start | bytes 43016 | tf_op jit(solution)/shard_map/ppermute | solution.py:184
  31.8 0.2 convolution_add_fusion
  32.0 0.4 compare_reduce_fusion
  32.4 0.2 collective-permute-done.14
  32.5 0.0 collective-permute-done.13.errors_other
  32.6 1.5 %collective-permute-start.15 = (f32[1,3584]{1,0:T(1,128)S(1)}, f32[1,3584]{1,0:T(1,128)S(1)}, u32[]{:S(2)}, u32[]{:S(2)}) collective-permute-start(f32[1,3584]{1,0:T(1,128)S(1)} %add.64), channel_id=1, source_target_pairs={{0,3},{1,2},{2,1},{3,0},{4,7},{5,6},{6,5},{7,4},{8,11},{9,10},{10,... | collective-permute-start | bytes 43016 | tf_op jit(solution)/shard_map/ppermute | solution.py:184
  34.1 0.9 %select_reduce_fusion = (f32[128]{0:T(128)}, f32[128]{0:T(128)}, bf16[32,128]{1,0:T(8,128)(2,1)S(1)}) fusion(pred[16,128]{1,0:T(8,128)(4,1)S(1)} %compare_reduce_fusion, pred[16,128]{1,0:T(8,128)(4,1)S(1)} %get-tuple-element.89, f32[128]{0:T(128)S(1)} %copy-done.3, f32[16,128]{1,0:T(8,128)S(1)} %convolution_add_fusion, f32[8,128]{1,0:T(8,128)S(1)} %get-tuple-element.78, ...), kind=kOutput, calls=%fused_computation.20 | convolution fusion | flops 29425408 | bytes 1177600 | tf_op jit(solution)/shard_map/dot_general | solution.py:27
  35.0 0.8 %collective-permute-done.15 = f32[1,3584]{1,0:T(1,128)S(1)} collective-permute-done((f32[1,3584]{1,0:T(1,128)S(1)}, f32[1,3584]{1,0:T(1,128)S(1)}, u32[]{:S(2)}, u32[]{:S(2)}) %collective-permute-start.15) | collective-permute-done | bytes 14368 | tf_op jit(solution)/shard_map/ppermute | solution.py:184
  35.8 1.5 %collective-permute-start.16 = (f32[1,3584]{1,0:T(1,128)S(1)}, f32[1,3584]{1,0:T(1,128)S(1)}, u32[]{:S(2)}, u32[]{:S(2)}) collective-permute-start(f32[1,3584]{1,0:T(1,128)S(1)} %add.67), channel_id=1, source_target_pairs={{0,5},{1,4},{2,7},{3,6},{4,1},{5,0},{6,3},{7,2},{8,13},{9,12},{10,... | collective-permute-start | bytes 43016 | tf_op jit(solution)/shard_map/ppermute | solution.py:184
  37.3 1.4 %convolution_convert_fusion = bf16[128,3584]{1,0:T(8,128)(2,1)} fusion(bf16[32,3584]{1,0:T(8,128)(2,1)S(1)} %constant_dynamic-update-slice_fusion.2, f32[16,128]{1,0:T(8,128)S(1)} %convolution_add_fusion, f32[8,128]{1,0:T(8,128)S(1)} %get-tuple-element.78, f32[8,128]{1,0:T(8,128)S(1)} %get-tuple-element.77, pred[16,128]{1,0:T(8,128)(4,1)S(1)} %compare_reduce_fusion, ...), kind=kOutput, calls=%fused_computation | convolution fusion | flops 29851648 | bytes 1167360 | tf_op jit(solution)/shard_map/dot_general | solution.py:31
  38.6 0.1 shard_map.116
  38.8 0.2 collective-permute-done.16
  39.0 2.5 %collective-permute-start.17 = (f32[1,3584]{1,0:T(1,128)S(1)}, f32[1,3584]{1,0:T(1,128)S(1)}, u32[]{:S(2)}, u32[]{:S(2)}) collective-permute-start(f32[1,3584]{1,0:T(1,128)S(1)} %add.68), channel_id=1, source_target_pairs={{0,9},{1,8},{2,11},{3,10},{4,13},{5,12},{6,15},{7,14},{8,1},{9,0},... | collective-permute-start | bytes 43016 | tf_op jit(solution)/shard_map/ppermute | solution.py:184
  41.5 1.4 %convolution_convert_fusion.1 = bf16[3584,128]{1,0:T(8,128)(2,1)} fusion(bf16[32,128]{1,0:T(8,128)(2,1)S(1)} %select_convert_fusion.1, bf16[16,3584]{1,0:T(8,128)(2,1)S(1)} %get-tuple-element.92, bf16[16,3584]{1,0:T(8,128)(2,1)S(1)} %get-tuple-element.91), kind=kOutput, calls=%fused_computation.1 | convolution fusion | flops 30277632 | bytes 1155072 | tf_op jit(solution)/shard_map/dot_general | solution.py:31
  42.9 0.2 collective-permute-done.17
  43.1 0.7 %subtract_reduce_fusion.1 = f32[3584]{0:T(1024)} fusion(f32[1,3584]{1,0:T(1,128)S(1)} %shard_map.116, f32[1,3584]{1,0:T(1,128)S(1)} %add.68, f32[1,3584]{1,0:T(1,128)S(1)} %collective-permute-done.17), kind=kLoop, calls=%fused_computation.18 | loop fusion | flops 7168 | bytes 57344 | tf_op jit(solution)/shard_map/sub | solution.py:302
  (38 shorter events, 0.4 us)
Async XLA Ops:
  0.6 4.9 %collective-permute-start = (bf16[2,3584]{1,0:T(2,128)(2,1)}, bf16[2,3584]{1,0:T(2,128)(2,1)S(1)}, u32[]{:S(2)}, u32[]{:S(2)}) collective-permute-start(bf16[2,3584]{1,0:T(2,128)(2,1)} %refs_0_.1), channel_id=1, source_target_pairs={{0,2},{1,3},{2,0},{3,1},{4,6},{5,7},{6,4},{7,5},{8,10},{9,11},{10,... | collective-permute-start | bytes 43016 | tf_op jit(solution)/shard_map/ppermute | solution.py:184
  3.7 9.7 %collective-permute-start.2 = (bf16[3584,128]{1,0:T(8,128)(2,1)}, bf16[3584,128]{1,0:T(8,128)(2,1)S(1)}, u32[]{:S(2)}, u32[]{:S(2)}) collective-permute-start(bf16[3584,128]{1,0:T(8,128)(2,1)} %encoder_far), channel_id=1, source_target_pairs={{0,1},{1,0},{2,3},{3,2},{4,5},{5,4},{6,7},{7,6},{8,9},{9,8},{10,11... | collective-permute-start | bytes 2752520 | tf_op jit(solution)/shard_map/ppermute | solution.py:184
  3.7 9.7 %collective-permute-start.4 = (bf16[128,3584]{1,0:T(8,128)(2,1)}, bf16[128,3584]{1,0:T(8,128)(2,1)S(1)}, u32[]{:S(2)}, u32[]{:S(2)}) collective-permute-start(bf16[128,3584]{1,0:T(8,128)(2,1)} %decoder_far), channel_id=1, source_target_pairs={{0,1},{1,0},{2,3},{3,2},{4,5},{5,4},{6,7},{7,6},{8,9},{9,8},{10,11... | collective-permute-start | bytes 2752520 | tf_op jit(solution)/shard_map/ppermute | solution.py:184
  4.2 9.1 %collective-permute-start.3 = (f32[1,128]{1,0:T(1,128)}, f32[1,128]{1,0:T(1,128)S(1)}, u32[]{:S(2)}, u32[]{:S(2)}) collective-permute-start(f32[1,128]{1,0:T(1,128)} %bitcast.7), channel_id=1, source_target_pairs={{0,1},{1,0},{2,3},{3,2},{4,5},{5,4},{6,7},{7,6},{8,9},{9,8},{10,11... | collective-permute-start | bytes 1544 | tf_op jit(solution)/shard_map/ppermute | solution.py:184
  5.6 4.0 %collective-permute-start.1 = (bf16[4,3584]{1,0:T(4,128)(2,1)S(1)}, bf16[4,3584]{1,0:T(4,128)(2,1)S(1)}, u32[]{:S(2)}, u32[]{:S(2)}) collective-permute-start(bf16[4,3584]{1,0:T(4,128)(2,1)S(1)} %maximum_select_fusion.1), channel_id=1, source_target_pairs={{0,4},{1,5},{2,6},{3,7},{4,0},{5,1},{6,2},{7,3},{8,12},{9,13},{10,... | collective-permute-start | bytes 86024 | tf_op jit(solution)/shard_map/ppermute | solution.py:184
  9.8 5.8 %collective-permute-start.5 = (bf16[8,3584]{1,0:T(8,128)(2,1)S(1)}, bf16[8,3584]{1,0:T(8,128)(2,1)S(1)}, u32[]{:S(2)}, u32[]{:S(2)}) collective-permute-start(bf16[8,3584]{1,0:T(8,128)(2,1)S(1)} %maximum_select_fusion.rows), channel_id=1, source_target_pairs={{0,8},{1,9},{2,10},{3,11},{4,12},{5,13},{6,14},{7,15},{8,0},{9,1},... | collective-permute-start | bytes 172040 | tf_op jit(solution)/shard_map/ppermute | solution.py:184
  14.0 4.2 %collective-permute-start.7 = (bf16[8,3584]{1,0:T(8,128)(2,1)S(1)}, bf16[8,3584]{1,0:T(8,128)(2,1)S(1)}, u32[]{:S(2)}, u32[]{:S(2)}) collective-permute-start(bf16[8,3584]{1,0:T(8,128)(2,1)S(1)} %get-tuple-element.61), channel_id=1, source_target_pairs={{0,2},{1,3},{2,0},{3,1},{4,6},{5,7},{6,4},{7,5},{8,10},{9,11},{10,... | collective-permute-start | bytes 172040 | tf_op jit(solution)/shard_map/ppermute | solution.py:184
  16.3 4.2 %collective-permute-start.9 = (bf16[8,3584]{1,0:T(8,128)(2,1)S(1)}, bf16[8,3584]{1,0:T(8,128)(2,1)S(1)}, u32[]{:S(2)}, u32[]{:S(2)}) collective-permute-start(bf16[8,3584]{1,0:T(8,128)(2,1)S(1)} %get-tuple-element.63), channel_id=1, source_target_pairs={{0,2},{1,3},{2,0},{3,1},{4,6},{5,7},{6,4},{7,5},{8,10},{9,11},{10,... | collective-permute-start | bytes 172040 | tf_op jit(solution)/shard_map/ppermute | solution.py:184
  18.3 4.9 %collective-permute-start.8 = (bf16[8,3584]{1,0:T(8,128)(2,1)S(1)}, bf16[8,3584]{1,0:T(8,128)(2,1)S(1)}, u32[]{:S(2)}, u32[]{:S(2)}) collective-permute-start(bf16[8,3584]{1,0:T(8,128)(2,1)S(1)} %add.60), channel_id=1, source_target_pairs={{0,4},{1,5},{2,6},{3,7},{4,0},{5,1},{6,2},{7,3},{8,12},{9,13},{10,... | collective-permute-start | bytes 172040 | tf_op jit(solution)/shard_map/ppermute | solution.py:184
  20.5 4.6 %collective-permute-start.10 = (bf16[8,3584]{1,0:T(8,128)(2,1)S(1)}, bf16[8,3584]{1,0:T(8,128)(2,1)S(1)}, u32[]{:S(2)}, u32[]{:S(2)}) collective-permute-start(bf16[8,3584]{1,0:T(8,128)(2,1)S(1)} %add.62), channel_id=1, source_target_pairs={{0,4},{1,5},{2,6},{3,7},{4,0},{5,1},{6,2},{7,3},{8,12},{9,13},{10,... | collective-permute-start | bytes 172040 | tf_op jit(solution)/shard_map/ppermute | solution.py:184
  23.1 7.2 %collective-permute-start.12 = (bf16[8,3584]{1,0:T(8,128)(2,1)S(1)}, bf16[8,3584]{1,0:T(8,128)(2,1)S(1)}, u32[]{:S(2)}, u32[]{:S(2)}) collective-permute-start(bf16[8,3584]{1,0:T(8,128)(2,1)S(1)} %add.61.low), channel_id=1, source_target_pairs={{0,8},{1,9},{2,10},{3,11},{4,12},{5,13},{6,14},{7,15},{8,0},{9,1},... | collective-permute-start | bytes 172040 | tf_op jit(solution)/shard_map/ppermute | solution.py:184
  25.2 5.1 %collective-permute-start.11 = (bf16[8,3584]{1,0:T(8,128)(2,1)S(1)}, bf16[8,3584]{1,0:T(8,128)(2,1)S(1)}, u32[]{:S(2)}, u32[]{:S(2)}) collective-permute-start(bf16[8,3584]{1,0:T(8,128)(2,1)S(1)} %add.63.high), channel_id=1, source_target_pairs={{0,8},{1,9},{2,10},{3,11},{4,12},{5,13},{6,14},{7,15},{8,0},{9,1},... | collective-permute-start | bytes 172040 | tf_op jit(solution)/shard_map/ppermute | solution.py:184
  27.2 4.4 %collective-permute-start.6 = (bf16[16,3584]{1,0:T(8,128)(2,1)S(1)}, bf16[16,3584]{1,0:T(8,128)(2,1)S(1)}, u32[]{:S(2)}, u32[]{:S(2)}) collective-permute-start(bf16[16,3584]{1,0:T(8,128)(2,1)S(1)} %constant_dynamic-update-slice_fusion), channel_id=1, source_target_pairs={{0,1},{1,0},{2,3},{3,2},{4,5},{5,4},{6,7},{7,6},{8,9},{9,8},{10,11... | collective-permute-start | bytes 344072 | tf_op jit(solution)/shard_map/ppermute | solution.py:184
  30.3 1.4 %copy-start = (bf16[3584,128]{1,0:T(8,128)(2,1)S(1)}, bf16[3584,128]{1,0:T(8,128)(2,1)}, u32[]{:S(2)}) copy-start(bf16[3584,128]{1,0:T(8,128)(2,1)} %encoder_far) | copy-start | bytes 2752516
  30.3 1.4 %copy-start.2 = (f32[128]{0:T(128)S(1)}, f32[128]{0:T(128)}, u32[]{:S(2)}) copy-start(f32[128]{0:T(128)} %refs_2_.2) | copy-start | bytes 1540
  30.3 2.0 %copy-start.3 = (f32[128]{0:T(128)S(1)}, f32[128]{0:T(128)}, u32[]{:S(2)}) copy-start(f32[128]{0:T(128)} %param.11) | copy-start | bytes 1540
  31.0 3.0 %copy-start.1 = (bf16[128,3584]{1,0:T(8,128)(2,1)S(1)}, bf16[128,3584]{1,0:T(8,128)(2,1)}, u32[]{:S(2)}) copy-start(bf16[128,3584]{1,0:T(8,128)(2,1)} %decoder_far) | copy-start | bytes 2752516
  31.0 1.5 %collective-permute-start.13 = (bf16[16,3584]{1,0:T(8,128)(2,1)S(1)}, bf16[16,3584]{1,0:T(8,128)(2,1)S(1)}, u32[]{:S(2)}, u32[]{:S(2)}) collective-permute-start(bf16[16,3584]{1,0:T(8,128)(2,1)S(1)} %get-tuple-element.72.errors), channel_id=1, source_target_pairs={{0,1},{1,0},{2,3},{3,2},{4,5},{5,4},{6,7},{7,6},{8,9},{9,8},{10,11... | collective-permute-start | bytes 344072 | tf_op jit(solution)/shard_map/ppermute | solution.py:184
  31.1 1.4 %collective-permute-start.14 = (f32[1,3584]{1,0:T(1,128)S(1)}, f32[1,3584]{1,0:T(1,128)S(1)}, u32[]{:S(2)}, u32[]{:S(2)}) collective-permute-start(f32[1,3584]{1,0:T(1,128)S(1)} %get-tuple-element.75), channel_id=1, source_target_pairs={{0,1},{1,0},{2,3},{3,2},{4,5},{5,4},{6,7},{7,6},{8,9},{9,8},{10,11... | collective-permute-start | bytes 43016 | tf_op jit(solution)/shard_map/ppermute | solution.py:184
  32.6 3.2 %collective-permute-start.15 = (f32[1,3584]{1,0:T(1,128)S(1)}, f32[1,3584]{1,0:T(1,128)S(1)}, u32[]{:S(2)}, u32[]{:S(2)}) collective-permute-start(f32[1,3584]{1,0:T(1,128)S(1)} %add.64), channel_id=1, source_target_pairs={{0,3},{1,2},{2,1},{3,0},{4,7},{5,6},{6,5},{7,4},{8,11},{9,10},{10,... | collective-permute-start | bytes 43016 | tf_op jit(solution)/shard_map/ppermute | solution.py:184
  35.8 3.2 %collective-permute-start.16 = (f32[1,3584]{1,0:T(1,128)S(1)}, f32[1,3584]{1,0:T(1,128)S(1)}, u32[]{:S(2)}, u32[]{:S(2)}) collective-permute-start(f32[1,3584]{1,0:T(1,128)S(1)} %add.67), channel_id=1, source_target_pairs={{0,5},{1,4},{2,7},{3,6},{4,1},{5,0},{6,3},{7,2},{8,13},{9,12},{10,... | collective-permute-start | bytes 43016 | tf_op jit(solution)/shard_map/ppermute | solution.py:184
  39.0 4.1 %collective-permute-start.17 = (f32[1,3584]{1,0:T(1,128)S(1)}, f32[1,3584]{1,0:T(1,128)S(1)}, u32[]{:S(2)}, u32[]{:S(2)}) collective-permute-start(f32[1,3584]{1,0:T(1,128)S(1)} %add.68), channel_id=1, source_target_pairs={{0,9},{1,8},{2,11},{3,10},{4,13},{5,12},{6,15},{7,14},{8,1},{9,0},... | collective-permute-start | bytes 43016 | tf_op jit(solution)/shard_map/ppermute | solution.py:184

commit v7 on v6

--- a/solution.py
+++ b/solution.py
@@ -178,7 +178,6 @@
 ):
     width = encoder_weight.shape[1]
     me = lax.axis_index("latent")
-    core = me & 1
 
     def swap(array, bit):
         return lax.ppermute(array, "latent", [(i, i ^ bit) for i in range(count)])
@@ -188,6 +187,7 @@
     while bit < count:
         hops.append(bit)
         bit *= 2
+    gathering = hops[1:] + hops[:1]
 
     encoder_other = swap(encoder_weight, 1)
     decoder_other = swap(decoder_weight, 1)
@@ -195,14 +195,17 @@
 
     per_device, depth = rows_in.shape
     slots = count // 4
-    side = jnp.where((me & hops[-1]) == 0, 0, 1)
+    kind = me & 1
+    for bit in hops:
+        kind = kind ^ jnp.where((me & bit) == 0, 0, 1)
+    side = jnp.where((me & gathering[-1]) == 0, 0, 1)
 
     block, bias_row, ids = stage(rows_in, decoder_bias, active_ids)
-    for bit in hops[:-1]:
-        if bit == hops[-2]:
+    for bit in gathering[:-1]:
+        if bit == gathering[-2]:
             weights = (encoder_weight, decoder_weight, encoder_bias)
             block, weights = lax.optimization_barrier((block, weights))
-        other = swap(rows_in if bit == hops[0] else block, bit)
+        other = swap(rows_in if bit == gathering[0] else block, bit | 1)
         low = jnp.concatenate([block, other], axis=0)
         high = jnp.concatenate([other, block], axis=0)
         block = jnp.where((me & bit) == 0, low, high)
@@ -211,21 +214,25 @@
         (block, ids, encoder_near, decoder_near, encoder_row)
     )
     rows = block
-    rows_far = swap(block, hops[-1])
+    rows_far = swap(block, gathering[-1] | 1)
     half_rows = rows.shape[0]
 
-    def quarter(half, part):
-        firsts = [((half * slots + slot) * 2 + part) * per_device for slot in range(slots)]
-        return jnp.concatenate([ids[first : first + per_device] for first in firsts])
-
-    quarters = [[quarter(half, part) for part in range(2)] for half in range(2)]
-
-    def listed(half, part):
-        near, far = [jnp.where(part == 0, *pair) for pair in quarters]
+    def quarter(half, kind):
+        lines = []
+        for slot in range(slots):
+            first = (slot * 2 + half) * 2
+            first += (bin(first).count("1") + kind) % 2
+            lines.append(ids[first * per_device : (first + 1) * per_device])
+        return jnp.concatenate(lines)
+
+    quarters = [[quarter(half, kind) for kind in range(2)] for half in range(2)]
+
+    def listed(half, kind):
+        near, far = [jnp.where(kind == 0, *pair) for pair in quarters]
         return jnp.where(half == 0, near, far)
 
-    lists = jnp.concatenate([listed(side, core), listed(1 - side, core)])
-    lists_other = jnp.concatenate([listed(side, 1 - core), listed(1 - side, 1 - core)])
+    lists = jnp.concatenate([listed(side, kind), listed(1 - side, kind)])
+    lists_other = jnp.concatenate([listed(side, 1 - kind), listed(1 - side, 1 - kind)])
 
     def center(part):
         return (part.astype(F32) - bias_row).astype(BF16)
@@ -247,12 +254,12 @@
     preact_far, high = forward(after(low, rows_far), gates_far)
     every_row = jnp.concatenate([rows, after(high, rows_far)])
     rows_other = swap(every_row, 1)
-    for bit in hops[:-1]:
-        low, high_received = lax.optimization_barrier(low + swap(low, bit)), swap(high, bit)
+    for bit in gathering[:-1]:
+        low, high_received = lax.optimization_barrier(low + swap(low, bit | 1)), swap(high, bit | 1)
         high = lax.optimization_barrier(high + after(low, high_received))
-    high_received = swap(low, hops[-1])
+    high_received = swap(low, gathering[-1] | 1)
     high, weights = lax.optimization_barrier((high, (encoder_weight, decoder_weight)))
-    low_received = swap(high, hops[-1])
+    low_received = swap(high, gathering[-1] | 1)
     encoder_turned, decoder_turned = turn(*weights, encoder_other, decoder_other)
 
     errors, part = near(

time: 44.1 us -> 43.1 us (0.977)
  waiting for transfers between devices: 5.81 us -> 1.13 us
  starting transfers between devices: 25.1 us -> 28.7 us
    ppermute x18, waiting for transfers between devices: 5.81 us -> 1.13 us  [swap(): return lax.ppermute(array, 'latent', [(i, i ^ bit) for i in range(count)])]
    ppermute x18, starting transfers between devices: 25.1 us -> 28.7 us  [swap(): return lax.ppermute(array, 'latent', [(i, i ^ bit) for i in range(count)])]
  transfers between devices with their start and end apart: 18 -> 18, of which waited for: 11 -> 5; matrix products, arithmetic and copies ran while one was open for 12% -> 12% of each run, Pallas kernels for 14% -> 15%
where the time goes in v7:
time: 43.1 us; the launch traced here: 42.8 us
  starting transfers between devices  28.7 us (67%)
  Pallas kernels  6.25 us (15%)
  matrix products  3.89 us (9%)
  other arithmetic  1.81 us (4%)
  waiting for transfers between devices  1.13 us (3%)
  between operations  0.9 us (2%)
    ppermute x18, starting transfers between devices, swap(): return lax.ppermute(array, 'latent', [(i, i ^ bit) for i in range(count)])  28.7 us
    dot_general x2, matrix products, dot_rows(): lax.dot_general(a, b, (((0,), (0,)), ((), ())), preferred_element_type=F32)  2.73 us
    pallas_call x2, Pallas kernels, stage(): pl.pallas_call(stage_kernel, in_specs=[pl.BlockSpec(memory_space=pltpu.HB...  2.26 us
    pallas_call x4, Pallas kernels, near(): pl.pallas_call(kernel, in_specs=[whole] * len(arrays), out_specs=[whole]...  2.2 us
    pallas_call x1, Pallas kernels, turn(): pl.pallas_call(turn_kernel, in_specs=[far, far, whole, whole], out_specs=...  1.79 us
    ppermute x18, waiting for transfers between devices, swap(): return lax.ppermute(array, 'latent', [(i, i ^ bit) for i in range(count)])  1.13 us
    dot_general x1, matrix products, dot_last(): lax.dot_general(a, b, (((1,), (1,)), ((), ())), preferred_element_type=F32)  0.93 us
  transfers between devices with their start and end apart: 18, of which 5 were waited for; matrix products, arithmetic and copies ran while one was open for 12% of the time, Pallas kernels for 15%

profile of v7, /device:TPU:0, one launch (start us, length us, event | category | flops | bytes accessed | tf_op | source)
XLA Modules:
  0.0 42.8 jit_solution(11639200037737525084)
XLA Ops:
  0.6 2.5 %collective-permute-start = (bf16[2,3584]{1,0:T(2,128)(2,1)}, bf16[2,3584]{1,0:T(2,128)(2,1)S(1)}, u32[]{:S(2)}, u32[]{:S(2)}) collective-permute-start(bf16[2,3584]{1,0:T(2,128)(2,1)} %refs_0_.1), channel_id=1, source_target_pairs={{0,5},{1,4},{2,7},{3,6},{4,1},{5,0},{6,3},{7,2},{8,13},{9,12},{10,... | collective-permute-start | bytes 43016 | tf_op jit(solution)/shard_map/ppermute | solution.py:183
  3.2 0.7 %collective-permute-start.2 = (bf16[3584,128]{1,0:T(8,128)(2,1)}, bf16[3584,128]{1,0:T(8,128)(2,1)S(1)}, u32[]{:S(2)}, u32[]{:S(2)}) collective-permute-start(bf16[3584,128]{1,0:T(8,128)(2,1)} %encoder_far), channel_id=1, source_target_pairs={{0,1},{1,0},{2,3},{3,2},{4,5},{5,4},{6,7},{7,6},{8,9},{9,8},{10,11... | collective-permute-start | bytes 2752520 | tf_op jit(solution)/shard_map/ppermute | solution.py:183
  3.8 0.5 %collective-permute-start.3 = (f32[1,128]{1,0:T(1,128)}, f32[1,128]{1,0:T(1,128)S(1)}, u32[]{:S(2)}, u32[]{:S(2)}) collective-permute-start(f32[1,128]{1,0:T(1,128)} %bitcast.7), channel_id=1, source_target_pairs={{0,1},{1,0},{2,3},{3,2},{4,5},{5,4},{6,7},{7,6},{8,9},{9,8},{10,11... | collective-permute-start | bytes 1544 | tf_op jit(solution)/shard_map/ppermute | solution.py:183
  4.3 0.8 %shard_map.110 = (bf16[2,3584]{1,0:T(2,128)(2,1)S(1)}, f32[1,3584]{1,0:T(1,128)S(1)}, s32[32,128]{1,0:T(8,128)S(1)}) custom-call(bf16[2,3584]{1,0:T(2,128)(2,1)} %refs_0_.1, f32[3584]{0:T(1024)} %refs_1_.1, s32[32,128]{1,0:T(8,128)} %refs_2_.1), custom_call_target="tpu_custom_call" | custom-call | bytes 90112 | tf_op jit(solution)/shard_map/pallas_call | solution.py:149
  5.1 0.0 collective-permute-done
  5.1 0.1 maximum_select_fusion.1
  5.2 2.7 %collective-permute-start.1 = (bf16[4,3584]{1,0:T(4,128)(2,1)S(1)}, bf16[4,3584]{1,0:T(4,128)(2,1)S(1)}, u32[]{:S(2)}, u32[]{:S(2)}) collective-permute-start(bf16[4,3584]{1,0:T(4,128)(2,1)S(1)} %maximum_select_fusion.1), channel_id=1, source_target_pairs={{0,9},{1,8},{2,11},{3,10},{4,13},{5,12},{6,15},{7,14},{8,1},{9,0},... | collective-permute-start | bytes 86024 | tf_op jit(solution)/shard_map/ppermute | solution.py:183
  8.0 1.5 %shard_map.111 = (bf16[3584,128]{1,0:T(8,128)(2,1)S(1)}, bf16[128,3584]{1,0:T(8,128)(2,1)S(1)}, f32[1,128]{1,0:T(1,128)S(1)}) custom-call(bf16[3584,128]{1,0:T(8,128)(2,1)} %encoder_far, bf16[128,3584]{1,0:T(8,128)(2,1)} %decoder_far, f32[128]{0:T(128)} %refs_2_.2), custom_call_target="tpu_custom_call" | custom-call | bytes 3671040 | tf_op jit(solution)/shard_map/pallas_call | solution.py:149
  9.5 0.0 collective-permute-done.1
  9.5 0.1 maximum_select_fusion.rows
  9.6 1.6 %collective-permute-start.5 = (bf16[8,3584]{1,0:T(8,128)(2,1)S(1)}, bf16[8,3584]{1,0:T(8,128)(2,1)S(1)}, u32[]{:S(2)}, u32[]{:S(2)}) collective-permute-start(bf16[8,3584]{1,0:T(8,128)(2,1)S(1)} %maximum_select_fusion.rows), channel_id=1, source_target_pairs={{0,3},{1,2},{2,1},{3,0},{4,7},{5,6},{6,5},{7,4},{8,11},{9,10},{10,... | collective-permute-start | bytes 172040 | tf_op jit(solution)/shard_map/ppermute | solution.py:183
  11.3 0.4 compare_reduce_fusion.2
  11.8 0.0 collective-permute-done.4.decoder_other
  11.8 0.7 %shard_map.112 = (f32[8,128]{1,0:T(8,128)S(1)}, bf16[8,3584]{1,0:T(8,128)(2,1)S(1)}) custom-call(bf16[8,3584]{1,0:T(8,128)(2,1)S(1)} %maximum_select_fusion.rows, f32[1,3584]{1,0:T(1,128)S(1)} %get-tuple-element.56.decoder_bias, f32[8,256]{1,0:T(8,128)S(1)} %get-tuple-element.94.gates, bf16[3584,128]{1,0:T(8,128)(2,1)S(1)} %get-tuple-element.58.encoder, ...), custom_call_target="tpu_custom_call" | custom-call | bytes 3750912 | tf_op jit(solution)/shard_map/pallas_call | solution.py:162
  12.4 1.7 %collective-permute-start.7 = (bf16[8,3584]{1,0:T(8,128)(2,1)S(1)}, bf16[8,3584]{1,0:T(8,128)(2,1)S(1)}, u32[]{:S(2)}, u32[]{:S(2)}) collective-permute-start(bf16[8,3584]{1,0:T(8,128)(2,1)S(1)} %get-tuple-element.61), channel_id=1, source_target_pairs={{0,5},{1,4},{2,7},{3,6},{4,1},{5,0},{6,3},{7,2},{8,13},{9,12},{10,... | collective-permute-start | bytes 172040 | tf_op jit(solution)/shard_map/ppermute | solution.py:183
  14.2 0.7 %shard_map.113 = (f32[8,128]{1,0:T(8,128)S(1)}, bf16[8,3584]{1,0:T(8,128)(2,1)S(1)}) custom-call(bf16[8,3584]{1,0:T(8,128)(2,1)S(1)} %collective-permute-done.5.rows.rows_far, f32[1,3584]{1,0:T(1,128)S(1)} %get-tuple-element.56.decoder_bias, f32[8,256]{1,0:T(8,128)S(1)} %get-tuple-element.93.gates.gates_far, ...), custom_call_target="tpu_custom_call" | custom-call | bytes 3750912 | tf_op jit(solution)/shard_map/pallas_call | solution.py:162
  14.9 1.2 %collective-permute-start.9 = (bf16[8,3584]{1,0:T(8,128)(2,1)S(1)}, bf16[8,3584]{1,0:T(8,128)(2,1)S(1)}, u32[]{:S(2)}, u32[]{:S(2)}) collective-permute-start(bf16[8,3584]{1,0:T(8,128)(2,1)S(1)} %get-tuple-element.63), channel_id=1, source_target_pairs={{0,5},{1,4},{2,7},{3,6},{4,1},{5,0},{6,3},{7,2},{8,13},{9,12},{10,... | collective-permute-start | bytes 172040 | tf_op jit(solution)/shard_map/ppermute | solution.py:183
  16.1 0.1 collective-permute-done.7
  16.3 3.2 %collective-permute-start.8 = (bf16[8,3584]{1,0:T(8,128)(2,1)S(1)}, bf16[8,3584]{1,0:T(8,128)(2,1)S(1)}, u32[]{:S(2)}, u32[]{:S(2)}) collective-permute-start(bf16[8,3584]{1,0:T(8,128)(2,1)S(1)} %add.60), channel_id=1, source_target_pairs={{0,9},{1,8},{2,11},{3,10},{4,13},{5,12},{6,15},{7,14},{8,1},{9,0},... | collective-permute-start | bytes 172040 | tf_op jit(solution)/shard_map/ppermute | solution.py:183
  19.5 0.0 collective-permute-done.9
  19.5 2.5 %collective-permute-start.10 = (bf16[8,3584]{1,0:T(8,128)(2,1)S(1)}, bf16[8,3584]{1,0:T(8,128)(2,1)S(1)}, u32[]{:S(2)}, u32[]{:S(2)}) collective-permute-start(bf16[8,3584]{1,0:T(8,128)(2,1)S(1)} %add.62), channel_id=1, source_target_pairs={{0,9},{1,8},{2,11},{3,10},{4,13},{5,12},{6,15},{7,14},{8,1},{9,0},... | collective-permute-start | bytes 172040 | tf_op jit(solution)/shard_map/ppermute | solution.py:183
  22.0 0.0 collective-permute-done.8
  22.0 2.3 %collective-permute-start.12 = (bf16[8,3584]{1,0:T(8,128)(2,1)S(1)}, bf16[8,3584]{1,0:T(8,128)(2,1)S(1)}, u32[]{:S(2)}, u32[]{:S(2)}) collective-permute-start(bf16[8,3584]{1,0:T(8,128)(2,1)S(1)} %add.61.low), channel_id=1, source_target_pairs={{0,3},{1,2},{2,1},{3,0},{4,7},{5,6},{6,5},{7,4},{8,11},{9,10},{10,... | collective-permute-start | bytes 172040 | tf_op jit(solution)/shard_map/ppermute | solution.py:183
  24.3 0.0 collective-permute-done.10
  24.3 2.6 %collective-permute-start.11 = (bf16[8,3584]{1,0:T(8,128)(2,1)S(1)}, bf16[8,3584]{1,0:T(8,128)(2,1)S(1)}, u32[]{:S(2)}, u32[]{:S(2)}) collective-permute-start(bf16[8,3584]{1,0:T(8,128)(2,1)S(1)} %add.63.high), channel_id=1, source_target_pairs={{0,3},{1,2},{2,1},{3,0},{4,7},{5,6},{6,5},{7,4},{8,11},{9,10},{10,... | collective-permute-start | bytes 172040 | tf_op jit(solution)/shard_map/ppermute | solution.py:183
  26.9 0.4 collective-permute-start.6
  27.3 1.8 %shard_map.114 = (bf16[256,3584]{1,0:T(8,128)(2,1)S(1)}, bf16[3584,256]{1,0:T(8,128)(2,1)S(1)}) custom-call(bf16[3584,128]{1,0:T(8,128)(2,1)} %encoder_far, bf16[128,3584]{1,0:T(8,128)(2,1)} %decoder_far, bf16[3584,128]{1,0:T(8,128)(2,1)S(1)} %collective-permute-done.2.encoder_other, bf16[128,3584]{1,0:T(8,128)(2,1)S(1)} %collective-permute-done.4.decoder_other), custom_call_target="tpu_custom_call" | custom-call | bytes 7340032 | tf_op jit(solution)/shard_map/pallas_call | solution.py:104
  29.1 0.0 collective-permute-done.12.high_received
  29.1 0.0 copy-start
  29.1 0.0 copy-start.2
  29.1 0.0 copy-start.3
  29.1 0.7 %shard_map.115 = (bf16[16,3584]{1,0:T(8,128)(2,1)S(1)}, f32[1,3584]{1,0:T(1,128)S(1)}) custom-call(bf16[8,3584]{1,0:T(8,128)(2,1)S(1)} %add.61.low, bf16[8,3584]{1,0:T(8,128)(2,1)S(1)} %collective-permute-done.11.low_received, bf16[8,3584]{1,0:T(8,128)(2,1)S(1)} %maximum_select_fusion.rows, f32[8,256]{1,0:T(8,128)S(1)} %get-tuple-element.94.gates, ...), custom_call_target="tpu_custom_call" | custom-call | bytes 4044800 | tf_op jit(solution)/shard_map/pallas_call | solution.py:162
  29.9 0.2 collective-permute-start.13
  30.1 0.4 collective-permute-start.14
  30.6 0.2 convolution_add_fusion
  30.8 0.4 compare_reduce_fusion
  31.2 0.2 collective-permute-done.14
  31.4 1.9 %collective-permute-start.15 = (f32[1,3584]{1,0:T(1,128)S(1)}, f32[1,3584]{1,0:T(1,128)S(1)}, u32[]{:S(2)}, u32[]{:S(2)}) collective-permute-start(f32[1,3584]{1,0:T(1,128)S(1)} %add.64), channel_id=1, source_target_pairs={{0,3},{1,2},{2,1},{3,0},{4,7},{5,6},{6,5},{7,4},{8,11},{9,10},{10,... | collective-permute-start | bytes 43016 | tf_op jit(solution)/shard_map/ppermute | solution.py:183
  33.4 0.9 %select_reduce_fusion = (f32[128]{0:T(128)}, f32[128]{0:T(128)}, bf16[32,128]{1,0:T(8,128)(2,1)S(1)}) fusion(pred[16,128]{1,0:T(8,128)(4,1)S(1)} %compare_reduce_fusion, pred[16,128]{1,0:T(8,128)(4,1)S(1)} %get-tuple-element.89, f32[128]{0:T(128)S(1)} %copy-done.3, f32[16,128]{1,0:T(8,128)S(1)} %convolution_add_fusion, f32[8,128]{1,0:T(8,128)S(1)} %get-tuple-element.78, ...), kind=kOutput, calls=%fused_computation.20 | convolution fusion | flops 29425408 | bytes 1177600 | tf_op jit(solution)/shard_map/dot_general | solution.py:27
  34.3 0.5 %collective-permute-done.15 = f32[1,3584]{1,0:T(1,128)S(1)} collective-permute-done((f32[1,3584]{1,0:T(1,128)S(1)}, f32[1,3584]{1,0:T(1,128)S(1)}, u32[]{:S(2)}, u32[]{:S(2)}) %collective-permute-start.15) | collective-permute-done | bytes 14368 | tf_op jit(solution)/shard_map/ppermute | solution.py:183
  34.8 1.5 %collective-permute-start.16 = (f32[1,3584]{1,0:T(1,128)S(1)}, f32[1,3584]{1,0:T(1,128)S(1)}, u32[]{:S(2)}, u32[]{:S(2)}) collective-permute-start(f32[1,3584]{1,0:T(1,128)S(1)} %add.67), channel_id=1, source_target_pairs={{0,5},{1,4},{2,7},{3,6},{4,1},{5,0},{6,3},{7,2},{8,13},{9,12},{10,... | collective-permute-start | bytes 43016 | tf_op jit(solution)/shard_map/ppermute | solution.py:183
  36.3 1.4 %convolution_convert_fusion = bf16[128,3584]{1,0:T(8,128)(2,1)} fusion(bf16[32,3584]{1,0:T(8,128)(2,1)S(1)} %constant_dynamic-update-slice_fusion.2, f32[16,128]{1,0:T(8,128)S(1)} %convolution_add_fusion, f32[8,128]{1,0:T(8,128)S(1)} %get-tuple-element.78, f32[8,128]{1,0:T(8,128)S(1)} %get-tuple-element.77, pred[16,128]{1,0:T(8,128)(4,1)S(1)} %compare_reduce_fusion, ...), kind=kOutput, calls=%fused_computation | convolution fusion | flops 29851648 | bytes 1167360 | tf_op jit(solution)/shard_map/dot_general | solution.py:31
  37.6 0.1 shard_map.116
  37.7 0.2 collective-permute-done.16
  38.0 2.6 %collective-permute-start.17 = (f32[1,3584]{1,0:T(1,128)S(1)}, f32[1,3584]{1,0:T(1,128)S(1)}, u32[]{:S(2)}, u32[]{:S(2)}) collective-permute-start(f32[1,3584]{1,0:T(1,128)S(1)} %add.68), channel_id=1, source_target_pairs={{0,9},{1,8},{2,11},{3,10},{4,13},{5,12},{6,15},{7,14},{8,1},{9,0},... | collective-permute-start | bytes 43016 | tf_op jit(solution)/shard_map/ppermute | solution.py:183
  40.7 1.4 %convolution_convert_fusion.1 = bf16[3584,128]{1,0:T(8,128)(2,1)} fusion(bf16[32,128]{1,0:T(8,128)(2,1)S(1)} %select_convert_fusion.1, bf16[16,3584]{1,0:T(8,128)(2,1)S(1)} %get-tuple-element.92, bf16[16,3584]{1,0:T(8,128)(2,1)S(1)} %get-tuple-element.91), kind=kOutput, calls=%fused_computation.1 | convolution fusion | flops 30277632 | bytes 1155072 | tf_op jit(solution)/shard_map/dot_general | solution.py:31
  42.0 0.1 collective-permute-done.17
  42.1 0.7 %subtract_reduce_fusion.1 = f32[3584]{0:T(1024)} fusion(f32[1,3584]{1,0:T(1,128)S(1)} %shard_map.116, f32[1,3584]{1,0:T(1,128)S(1)} %add.68, f32[1,3584]{1,0:T(1,128)S(1)} %collective-permute-done.17), kind=kLoop, calls=%fused_computation.18 | loop fusion | flops 7168 | bytes 57344 | tf_op jit(solution)/shard_map/sub | solution.py:309
  (38 shorter events, 0.4 us)
Async XLA Ops:
  0.6 4.5 %collective-permute-start = (bf16[2,3584]{1,0:T(2,128)(2,1)}, bf16[2,3584]{1,0:T(2,128)(2,1)S(1)}, u32[]{:S(2)}, u32[]{:S(2)}) collective-permute-start(bf16[2,3584]{1,0:T(2,128)(2,1)} %refs_0_.1), channel_id=1, source_target_pairs={{0,5},{1,4},{2,7},{3,6},{4,1},{5,0},{6,3},{7,2},{8,13},{9,12},{10,... | collective-permute-start | bytes 43016 | tf_op jit(solution)/shard_map/ppermute | solution.py:183
  3.2 8.6 %collective-permute-start.2 = (bf16[3584,128]{1,0:T(8,128)(2,1)}, bf16[3584,128]{1,0:T(8,128)(2,1)S(1)}, u32[]{:S(2)}, u32[]{:S(2)}) collective-permute-start(bf16[3584,128]{1,0:T(8,128)(2,1)} %encoder_far), channel_id=1, source_target_pairs={{0,1},{1,0},{2,3},{3,2},{4,5},{5,4},{6,7},{7,6},{8,9},{9,8},{10,11... | collective-permute-start | bytes 2752520 | tf_op jit(solution)/shard_map/ppermute | solution.py:183
  3.8 7.9 %collective-permute-start.4 = (bf16[128,3584]{1,0:T(8,128)(2,1)}, bf16[128,3584]{1,0:T(8,128)(2,1)S(1)}, u32[]{:S(2)}, u32[]{:S(2)}) collective-permute-start(bf16[128,3584]{1,0:T(8,128)(2,1)} %decoder_far), channel_id=1, source_target_pairs={{0,1},{1,0},{2,3},{3,2},{4,5},{5,4},{6,7},{7,6},{8,9},{9,8},{10,11... | collective-permute-start | bytes 2752520 | tf_op jit(solution)/shard_map/ppermute | solution.py:183
  3.8 7.9 %collective-permute-start.3 = (f32[1,128]{1,0:T(1,128)}, f32[1,128]{1,0:T(1,128)S(1)}, u32[]{:S(2)}, u32[]{:S(2)}) collective-permute-start(f32[1,128]{1,0:T(1,128)} %bitcast.7), channel_id=1, source_target_pairs={{0,1},{1,0},{2,3},{3,2},{4,5},{5,4},{6,7},{7,6},{8,9},{9,8},{10,11... | collective-permute-start | bytes 1544 | tf_op jit(solution)/shard_map/ppermute | solution.py:183
  5.2 4.3 %collective-permute-start.1 = (bf16[4,3584]{1,0:T(4,128)(2,1)S(1)}, bf16[4,3584]{1,0:T(4,128)(2,1)S(1)}, u32[]{:S(2)}, u32[]{:S(2)}) collective-permute-start(bf16[4,3584]{1,0:T(4,128)(2,1)S(1)} %maximum_select_fusion.1), channel_id=1, source_target_pairs={{0,9},{1,8},{2,11},{3,10},{4,13},{5,12},{6,15},{7,14},{8,1},{9,0},... | collective-permute-start | bytes 86024 | tf_op jit(solution)/shard_map/ppermute | solution.py:183
  9.6 4.6 %collective-permute-start.5 = (bf16[8,3584]{1,0:T(8,128)(2,1)S(1)}, bf16[8,3584]{1,0:T(8,128)(2,1)S(1)}, u32[]{:S(2)}, u32[]{:S(2)}) collective-permute-start(bf16[8,3584]{1,0:T(8,128)(2,1)S(1)} %maximum_select_fusion.rows), channel_id=1, source_target_pairs={{0,3},{1,2},{2,1},{3,0},{4,7},{5,6},{6,5},{7,4},{8,11},{9,10},{10,... | collective-permute-start | bytes 172040 | tf_op jit(solution)/shard_map/ppermute | solution.py:183
  12.4 3.8 %collective-permute-start.7 = (bf16[8,3584]{1,0:T(8,128)(2,1)S(1)}, bf16[8,3584]{1,0:T(8,128)(2,1)S(1)}, u32[]{:S(2)}, u32[]{:S(2)}) collective-permute-start(bf16[8,3584]{1,0:T(8,128)(2,1)S(1)} %get-tuple-element.61), channel_id=1, source_target_pairs={{0,5},{1,4},{2,7},{3,6},{4,1},{5,0},{6,3},{7,2},{8,13},{9,12},{10,... | collective-permute-start | bytes 172040 | tf_op jit(solution)/shard_map/ppermute | solution.py:183
  14.9 4.6 %collective-permute-start.9 = (bf16[8,3584]{1,0:T(8,128)(2,1)S(1)}, bf16[8,3584]{1,0:T(8,128)(2,1)S(1)}, u32[]{:S(2)}, u32[]{:S(2)}) collective-permute-start(bf16[8,3584]{1,0:T(8,128)(2,1)S(1)} %get-tuple-element.63), channel_id=1, source_target_pairs={{0,5},{1,4},{2,7},{3,6},{4,1},{5,0},{6,3},{7,2},{8,13},{9,12},{10,... | collective-permute-start | bytes 172040 | tf_op jit(solution)/shard_map/ppermute | solution.py:183
  16.3 5.7 %collective-permute-start.8 = (bf16[8,3584]{1,0:T(8,128)(2,1)S(1)}, bf16[8,3584]{1,0:T(8,128)(2,1)S(1)}, u32[]{:S(2)}, u32[]{:S(2)}) collective-permute-start(bf16[8,3584]{1,0:T(8,128)(2,1)S(1)} %add.60), channel_id=1, source_target_pairs={{0,9},{1,8},{2,11},{3,10},{4,13},{5,12},{6,15},{7,14},{8,1},{9,0},... | collective-permute-start | bytes 172040 | tf_op jit(solution)/shard_map/ppermute | solution.py:183
  19.5 4.8 %collective-permute-start.10 = (bf16[8,3584]{1,0:T(8,128)(2,1)S(1)}, bf16[8,3584]{1,0:T(8,128)(2,1)S(1)}, u32[]{:S(2)}, u32[]{:S(2)}) collective-permute-start(bf16[8,3584]{1,0:T(8,128)(2,1)S(1)} %add.62), channel_id=1, source_target_pairs={{0,9},{1,8},{2,11},{3,10},{4,13},{5,12},{6,15},{7,14},{8,1},{9,0},... | collective-permute-start | bytes 172040 | tf_op jit(solution)/shard_map/ppermute | solution.py:183
  22.0 7.1 %collective-permute-start.12 = (bf16[8,3584]{1,0:T(8,128)(2,1)S(1)}, bf16[8,3584]{1,0:T(8,128)(2,1)S(1)}, u32[]{:S(2)}, u32[]{:S(2)}) collective-permute-start(bf16[8,3584]{1,0:T(8,128)(2,1)S(1)} %add.61.low), channel_id=1, source_target_pairs={{0,3},{1,2},{2,1},{3,0},{4,7},{5,6},{6,5},{7,4},{8,11},{9,10},{10,... | collective-permute-start | bytes 172040 | tf_op jit(solution)/shard_map/ppermute | solution.py:183
  24.3 4.8 %collective-permute-start.11 = (bf16[8,3584]{1,0:T(8,128)(2,1)S(1)}, bf16[8,3584]{1,0:T(8,128)(2,1)S(1)}, u32[]{:S(2)}, u32[]{:S(2)}) collective-permute-start(bf16[8,3584]{1,0:T(8,128)(2,1)S(1)} %add.63.high), channel_id=1, source_target_pairs={{0,3},{1,2},{2,1},{3,0},{4,7},{5,6},{6,5},{7,4},{8,11},{9,10},{10,... | collective-permute-start | bytes 172040 | tf_op jit(solution)/shard_map/ppermute | solution.py:183
  26.9 3.6 %collective-permute-start.6 = (bf16[16,3584]{1,0:T(8,128)(2,1)S(1)}, bf16[16,3584]{1,0:T(8,128)(2,1)S(1)}, u32[]{:S(2)}, u32[]{:S(2)}) collective-permute-start(bf16[16,3584]{1,0:T(8,128)(2,1)S(1)} %constant_dynamic-update-slice_fusion), channel_id=1, source_target_pairs={{0,1},{1,0},{2,3},{3,2},{4,5},{5,4},{6,7},{7,6},{8,9},{9,8},{10,11... | collective-permute-start | bytes 344072 | tf_op jit(solution)/shard_map/ppermute | solution.py:183
  29.1 1.5 %copy-start = (bf16[3584,128]{1,0:T(8,128)(2,1)S(1)}, bf16[3584,128]{1,0:T(8,128)(2,1)}, u32[]{:S(2)}) copy-start(bf16[3584,128]{1,0:T(8,128)(2,1)} %encoder_far) | copy-start | bytes 2752516
  29.1 1.5 %copy-start.2 = (f32[128]{0:T(128)S(1)}, f32[128]{0:T(128)}, u32[]{:S(2)}) copy-start(f32[128]{0:T(128)} %refs_2_.2) | copy-start | bytes 1540
  29.1 2.0 %copy-start.3 = (f32[128]{0:T(128)S(1)}, f32[128]{0:T(128)}, u32[]{:S(2)}) copy-start(f32[128]{0:T(128)} %param.11) | copy-start | bytes 1540
  29.9 3.5 %copy-start.1 = (bf16[128,3584]{1,0:T(8,128)(2,1)S(1)}, bf16[128,3584]{1,0:T(8,128)(2,1)}, u32[]{:S(2)}) copy-start(bf16[128,3584]{1,0:T(8,128)(2,1)} %decoder_far) | copy-start | bytes 2752516
  29.9 1.5 %collective-permute-start.13 = (bf16[16,3584]{1,0:T(8,128)(2,1)S(1)}, bf16[16,3584]{1,0:T(8,128)(2,1)S(1)}, u32[]{:S(2)}, u32[]{:S(2)}) collective-permute-start(bf16[16,3584]{1,0:T(8,128)(2,1)S(1)} %get-tuple-element.72.errors), channel_id=1, source_target_pairs={{0,1},{1,0},{2,3},{3,2},{4,5},{5,4},{6,7},{7,6},{8,9},{9,8},{10,11... | collective-permute-start | bytes 344072 | tf_op jit(solution)/shard_map/ppermute | solution.py:183
  30.1 1.3 %collective-permute-start.14 = (f32[1,3584]{1,0:T(1,128)S(1)}, f32[1,3584]{1,0:T(1,128)S(1)}, u32[]{:S(2)}, u32[]{:S(2)}) collective-permute-start(f32[1,3584]{1,0:T(1,128)S(1)} %get-tuple-element.75), channel_id=1, source_target_pairs={{0,1},{1,0},{2,3},{3,2},{4,5},{5,4},{6,7},{7,6},{8,9},{9,8},{10,11... | collective-permute-start | bytes 43016 | tf_op jit(solution)/shard_map/ppermute | solution.py:183
  31.4 3.4 %collective-permute-start.15 = (f32[1,3584]{1,0:T(1,128)S(1)}, f32[1,3584]{1,0:T(1,128)S(1)}, u32[]{:S(2)}, u32[]{:S(2)}) collective-permute-start(f32[1,3584]{1,0:T(1,128)S(1)} %add.64), channel_id=1, source_target_pairs={{0,3},{1,2},{2,1},{3,0},{4,7},{5,6},{6,5},{7,4},{8,11},{9,10},{10,... | collective-permute-start | bytes 43016 | tf_op jit(solution)/shard_map/ppermute | solution.py:183
  34.8 3.2 %collective-permute-start.16 = (f32[1,3584]{1,0:T(1,128)S(1)}, f32[1,3584]{1,0:T(1,128)S(1)}, u32[]{:S(2)}, u32[]{:S(2)}) collective-permute-start(f32[1,3584]{1,0:T(1,128)S(1)} %add.67), channel_id=1, source_target_pairs={{0,5},{1,4},{2,7},{3,6},{4,1},{5,0},{6,3},{7,2},{8,13},{9,12},{10,... | collective-permute-start | bytes 43016 | tf_op jit(solution)/shard_map/ppermute | solution.py:183
  38.0 4.1 %collective-permute-start.17 = (f32[1,3584]{1,0:T(1,128)S(1)}, f32[1,3584]{1,0:T(1,128)S(1)}, u32[]{:S(2)}, u32[]{:S(2)}) collective-permute-start(f32[1,3584]{1,0:T(1,128)S(1)} %add.68), channel_id=1, source_target_pairs={{0,9},{1,8},{2,11},{3,10},{4,13},{5,12},{6,15},{7,14},{8,1},{9,0},... | collective-permute-start | bytes 43016 | tf_op jit(solution)/shard_map/ppermute | solution.py:183

commit v8 on v7

--- a/solution.py
+++ b/solution.py
@@ -187,7 +187,7 @@
     while bit < count:
         hops.append(bit)
         bit *= 2
-    gathering = hops[1:] + hops[:1]
+    gathering = hops[:0:-1] + hops[:1]
 
     encoder_other = swap(encoder_weight, 1)
     decoder_other = swap(decoder_weight, 1)
@@ -219,7 +219,8 @@
 
     def quarter(half, kind):
         lines = []
-        for slot in range(slots):
+        for place in range(slots):
+            slot = sum(slots // (2 << i) for i in range(slots.bit_length() - 1) if (place >> i) & 1)
             first = (slot * 2 + half) * 2
             first += (bin(first).count("1") + kind) % 2
             lines.append(ids[first * per_device : (first + 1) * per_device])
@@ -254,7 +255,7 @@
     preact_far, high = forward(after(low, rows_far), gates_far)
     every_row = jnp.concatenate([rows, after(high, rows_far)])
     rows_other = swap(every_row, 1)
-    for bit in gathering[:-1]:
+    for bit in gathering[-2::-1]:
         low, high_received = lax.optimization_barrier(low + swap(low, bit | 1)), swap(high, bit | 1)
         high = lax.optimization_barrier(high + after(low, high_received))
     high_received = swap(low, gathering[-1] | 1)

time: 43.1 us -> 42.7 us (level)
  starting transfers between devices: 28.7 us -> 27.8 us
  waiting for transfers between devices: 1.13 us -> 1.66 us
    ppermute x18, starting transfers between devices: 28.7 us -> 27.8 us  [swap(): return lax.ppermute(array, 'latent', [(i, i ^ bit) for i in range(count)])]
    ppermute x18, waiting for transfers between devices: 1.13 us -> 1.66 us  [swap(): return lax.ppermute(array, 'latent', [(i, i ^ bit) for i in range(count)])]
  transfers between devices with their start and end apart: 18 -> 18, of which waited for: 5 -> 7; matrix products, arithmetic and copies ran while one was open for 12% -> 12% of each run, Pallas kernels for 15% -> 15%
where the time goes in v8:
time: 42.7 us; the launch traced here: 42.3 us
  starting transfers between devices  27.8 us (65%)
  Pallas kernels  6.25 us (15%)
  matrix products  3.88 us (9%)
  other arithmetic  1.81 us (4%)
  waiting for transfers between devices  1.66 us (4%)
  between operations  0.9 us (2%)
    ppermute x18, starting transfers between devices, swap(): return lax.ppermute(array, 'latent', [(i, i ^ bit) for i in range(count)])  27.8 us
    dot_general x2, matrix products, dot_rows(): lax.dot_general(a, b, (((0,), (0,)), ((), ())), preferred_element_type=F32)  2.73 us
    pallas_call x2, Pallas kernels, stage(): pl.pallas_call(stage_kernel, in_specs=[pl.BlockSpec(memory_space=pltpu.HB...  2.26 us
    pallas_call x4, Pallas kernels, near(): pl.pallas_call(kernel, in_specs=[whole] * len(arrays), out_specs=[whole]...  2.2 us
    pallas_call x1, Pallas kernels, turn(): pl.pallas_call(turn_kernel, in_specs=[far, far, whole, whole], out_specs=...  1.79 us
    ppermute x18, waiting for transfers between devices, swap(): return lax.ppermute(array, 'latent', [(i, i ^ bit) for i in range(count)])  1.66 us
    dot_general x1, matrix products, dot_last(): lax.dot_general(a, b, (((1,), (1,)), ((), ())), preferred_element_type=F32)  0.93 us
  transfers between devices with their start and end apart: 18, of which 7 were waited for; matrix products, arithmetic and copies ran while one was open for 12% of the time, Pallas kernels for 15%

profile of v8, /device:TPU:0, one launch (start us, length us, event | category | flops | bytes accessed | tf_op | source)
XLA Modules:
  0.0 42.3 jit_solution(17783276198559136743)
XLA Ops:
  0.6 3.5 %collective-permute-start = (bf16[2,3584]{1,0:T(2,128)(2,1)}, bf16[2,3584]{1,0:T(2,128)(2,1)S(1)}, u32[]{:S(2)}, u32[]{:S(2)}) collective-permute-start(bf16[2,3584]{1,0:T(2,128)(2,1)} %refs_0_.1), channel_id=1, source_target_pairs={{0,9},{1,8},{2,11},{3,10},{4,13},{5,12},{6,15},{7,14},{8,1},{9,0},... | collective-permute-start | bytes 43016 | tf_op jit(solution)/shard_map/ppermute | solution.py:183
  4.2 0.7 %collective-permute-start.2 = (bf16[3584,128]{1,0:T(8,128)(2,1)}, bf16[3584,128]{1,0:T(8,128)(2,1)S(1)}, u32[]{:S(2)}, u32[]{:S(2)}) collective-permute-start(bf16[3584,128]{1,0:T(8,128)(2,1)} %encoder_far), channel_id=1, source_target_pairs={{0,1},{1,0},{2,3},{3,2},{4,5},{5,4},{6,7},{7,6},{8,9},{9,8},{10,11... | collective-permute-start | bytes 2752520 | tf_op jit(solution)/shard_map/ppermute | solution.py:183
  4.9 0.5 %collective-permute-start.3 = (f32[1,128]{1,0:T(1,128)}, f32[1,128]{1,0:T(1,128)S(1)}, u32[]{:S(2)}, u32[]{:S(2)}) collective-permute-start(f32[1,128]{1,0:T(1,128)} %bitcast.7), channel_id=1, source_target_pairs={{0,1},{1,0},{2,3},{3,2},{4,5},{5,4},{6,7},{7,6},{8,9},{9,8},{10,11... | collective-permute-start | bytes 1544 | tf_op jit(solution)/shard_map/ppermute | solution.py:183
  5.4 0.8 %shard_map.110 = (bf16[2,3584]{1,0:T(2,128)(2,1)S(1)}, f32[1,3584]{1,0:T(1,128)S(1)}, s32[32,128]{1,0:T(8,128)S(1)}) custom-call(bf16[2,3584]{1,0:T(2,128)(2,1)} %refs_0_.1, f32[3584]{0:T(1024)} %refs_1_.1, s32[32,128]{1,0:T(8,128)} %refs_2_.1), custom_call_target="tpu_custom_call" | custom-call | bytes 90112 | tf_op jit(solution)/shard_map/pallas_call | solution.py:149
  6.1 0.0 collective-permute-done
  6.2 0.1 maximum_select_fusion.1
  6.2 1.6 %collective-permute-start.1 = (bf16[4,3584]{1,0:T(4,128)(2,1)S(1)}, bf16[4,3584]{1,0:T(4,128)(2,1)S(1)}, u32[]{:S(2)}, u32[]{:S(2)}) collective-permute-start(bf16[4,3584]{1,0:T(4,128)(2,1)S(1)} %maximum_select_fusion.1), channel_id=1, source_target_pairs={{0,5},{1,4},{2,7},{3,6},{4,1},{5,0},{6,3},{7,2},{8,13},{9,12},{10,... | collective-permute-start | bytes 86024 | tf_op jit(solution)/shard_map/ppermute | solution.py:183
  7.9 1.5 %shard_map.111 = (bf16[3584,128]{1,0:T(8,128)(2,1)S(1)}, bf16[128,3584]{1,0:T(8,128)(2,1)S(1)}, f32[1,128]{1,0:T(1,128)S(1)}) custom-call(bf16[3584,128]{1,0:T(8,128)(2,1)} %encoder_far, bf16[128,3584]{1,0:T(8,128)(2,1)} %decoder_far, f32[128]{0:T(128)} %refs_2_.2), custom_call_target="tpu_custom_call" | custom-call | bytes 3671040 | tf_op jit(solution)/shard_map/pallas_call | solution.py:149
  9.4 0.2 collective-permute-done.1
  9.6 0.1 maximum_select_fusion.rows
  9.7 1.5 %collective-permute-start.5 = (bf16[8,3584]{1,0:T(8,128)(2,1)S(1)}, bf16[8,3584]{1,0:T(8,128)(2,1)S(1)}, u32[]{:S(2)}, u32[]{:S(2)}) collective-permute-start(bf16[8,3584]{1,0:T(8,128)(2,1)S(1)} %maximum_select_fusion.rows), channel_id=1, source_target_pairs={{0,3},{1,2},{2,1},{3,0},{4,7},{5,6},{6,5},{7,4},{8,11},{9,10},{10,... | collective-permute-start | bytes 172040 | tf_op jit(solution)/shard_map/ppermute | solution.py:183
  11.3 0.4 compare_reduce_fusion.2
  11.7 0.0 collective-permute-done.2.encoder_other
  11.7 0.0 collective-permute-done.4.decoder_other
  11.7 0.7 %shard_map.112 = (f32[8,128]{1,0:T(8,128)S(1)}, bf16[8,3584]{1,0:T(8,128)(2,1)S(1)}) custom-call(bf16[8,3584]{1,0:T(8,128)(2,1)S(1)} %maximum_select_fusion.rows, f32[1,3584]{1,0:T(1,128)S(1)} %get-tuple-element.56.decoder_bias, f32[8,256]{1,0:T(8,128)S(1)} %get-tuple-element.94.gates, bf16[3584,128]{1,0:T(8,128)(2,1)S(1)} %get-tuple-element.58.encoder, ...), custom_call_target="tpu_custom_call" | custom-call | bytes 3750912 | tf_op jit(solution)/shard_map/pallas_call | solution.py:162
  12.4 1.6 %collective-permute-start.7 = (bf16[8,3584]{1,0:T(8,128)(2,1)S(1)}, bf16[8,3584]{1,0:T(8,128)(2,1)S(1)}, u32[]{:S(2)}, u32[]{:S(2)}) collective-permute-start(bf16[8,3584]{1,0:T(8,128)(2,1)S(1)} %get-tuple-element.61), channel_id=1, source_target_pairs={{0,5},{1,4},{2,7},{3,6},{4,1},{5,0},{6,3},{7,2},{8,13},{9,12},{10,... | collective-permute-start | bytes 172040 | tf_op jit(solution)/shard_map/ppermute | solution.py:183
  14.1 0.7 %shard_map.113 = (f32[8,128]{1,0:T(8,128)S(1)}, bf16[8,3584]{1,0:T(8,128)(2,1)S(1)}) custom-call(bf16[8,3584]{1,0:T(8,128)(2,1)S(1)} %collective-permute-done.5.rows.rows_far, f32[1,3584]{1,0:T(1,128)S(1)} %get-tuple-element.56.decoder_bias, f32[8,256]{1,0:T(8,128)S(1)} %get-tuple-element.93.gates.gates_far, ...), custom_call_target="tpu_custom_call" | custom-call | bytes 3750912 | tf_op jit(solution)/shard_map/pallas_call | solution.py:162
  14.7 1.2 %collective-permute-start.9 = (bf16[8,3584]{1,0:T(8,128)(2,1)S(1)}, bf16[8,3584]{1,0:T(8,128)(2,1)S(1)}, u32[]{:S(2)}, u32[]{:S(2)}) collective-permute-start(bf16[8,3584]{1,0:T(8,128)(2,1)S(1)} %get-tuple-element.63), channel_id=1, source_target_pairs={{0,5},{1,4},{2,7},{3,6},{4,1},{5,0},{6,3},{7,2},{8,13},{9,12},{10,... | collective-permute-start | bytes 172040 | tf_op jit(solution)/shard_map/ppermute | solution.py:183
  16.0 0.3 collective-permute-done.7
  16.3 2.8 %collective-permute-start.8 = (bf16[8,3584]{1,0:T(8,128)(2,1)S(1)}, bf16[8,3584]{1,0:T(8,128)(2,1)S(1)}, u32[]{:S(2)}, u32[]{:S(2)}) collective-permute-start(bf16[8,3584]{1,0:T(8,128)(2,1)S(1)} %add.60), channel_id=1, source_target_pairs={{0,9},{1,8},{2,11},{3,10},{4,13},{5,12},{6,15},{7,14},{8,1},{9,0},... | collective-permute-start | bytes 172040 | tf_op jit(solution)/shard_map/ppermute | solution.py:183
  19.0 0.0 collective-permute-done.9
  19.1 2.5 %collective-permute-start.10 = (bf16[8,3584]{1,0:T(8,128)(2,1)S(1)}, bf16[8,3584]{1,0:T(8,128)(2,1)S(1)}, u32[]{:S(2)}, u32[]{:S(2)}) collective-permute-start(bf16[8,3584]{1,0:T(8,128)(2,1)S(1)} %add.62), channel_id=1, source_target_pairs={{0,9},{1,8},{2,11},{3,10},{4,13},{5,12},{6,15},{7,14},{8,1},{9,0},... | collective-permute-start | bytes 172040 | tf_op jit(solution)/shard_map/ppermute | solution.py:183
  21.5 0.0 collective-permute-done.8
  21.5 2.2 %collective-permute-start.12 = (bf16[8,3584]{1,0:T(8,128)(2,1)S(1)}, bf16[8,3584]{1,0:T(8,128)(2,1)S(1)}, u32[]{:S(2)}, u32[]{:S(2)}) collective-permute-start(bf16[8,3584]{1,0:T(8,128)(2,1)S(1)} %add.61.low), channel_id=1, source_target_pairs={{0,3},{1,2},{2,1},{3,0},{4,7},{5,6},{6,5},{7,4},{8,11},{9,10},{10,... | collective-permute-start | bytes 172040 | tf_op jit(solution)/shard_map/ppermute | solution.py:183
  23.8 0.2 collective-permute-done.10
  24.0 2.5 %collective-permute-start.11 = (bf16[8,3584]{1,0:T(8,128)(2,1)S(1)}, bf16[8,3584]{1,0:T(8,128)(2,1)S(1)}, u32[]{:S(2)}, u32[]{:S(2)}) collective-permute-start(bf16[8,3584]{1,0:T(8,128)(2,1)S(1)} %add.63.high), channel_id=1, source_target_pairs={{0,3},{1,2},{2,1},{3,0},{4,7},{5,6},{6,5},{7,4},{8,11},{9,10},{10,... | collective-permute-start | bytes 172040 | tf_op jit(solution)/shard_map/ppermute | solution.py:183
  26.5 0.4 collective-permute-start.6
  26.9 1.8 %shard_map.114 = (bf16[256,3584]{1,0:T(8,128)(2,1)S(1)}, bf16[3584,256]{1,0:T(8,128)(2,1)S(1)}) custom-call(bf16[3584,128]{1,0:T(8,128)(2,1)} %encoder_far, bf16[128,3584]{1,0:T(8,128)(2,1)} %decoder_far, bf16[3584,128]{1,0:T(8,128)(2,1)S(1)} %collective-permute-done.2.encoder_other, bf16[128,3584]{1,0:T(8,128)(2,1)S(1)} %collective-permute-done.4.decoder_other), custom_call_target="tpu_custom_call" | custom-call | bytes 7340032 | tf_op jit(solution)/shard_map/pallas_call | solution.py:104
  28.7 0.0 copy-start
  28.7 0.0 copy-start.2
  28.7 0.0 copy-start.3
  28.7 0.7 %shard_map.115 = (bf16[16,3584]{1,0:T(8,128)(2,1)S(1)}, f32[1,3584]{1,0:T(1,128)S(1)}) custom-call(bf16[8,3584]{1,0:T(8,128)(2,1)S(1)} %add.61.low, bf16[8,3584]{1,0:T(8,128)(2,1)S(1)} %collective-permute-done.11.low_received, bf16[8,3584]{1,0:T(8,128)(2,1)S(1)} %maximum_select_fusion.rows, f32[8,256]{1,0:T(8,128)S(1)} %get-tuple-element.94.gates, ...), custom_call_target="tpu_custom_call" | custom-call | bytes 4044800 | tf_op jit(solution)/shard_map/pallas_call | solution.py:162
  29.4 0.2 collective-permute-start.13
  29.7 0.4 %collective-permute-start.14 = (f32[1,3584]{1,0:T(1,128)S(1)}, f32[1,3584]{1,0:T(1,128)S(1)}, u32[]{:S(2)}, u32[]{:S(2)}) collective-permute-start(f32[1,3584]{1,0:T(1,128)S(1)} %get-tuple-element.75), channel_id=1, source_target_pairs={{0,1},{1,0},{2,3},{3,2},{4,5},{5,4},{6,7},{7,6},{8,9},{9,8},{10,11... | collective-permute-start | bytes 43016 | tf_op jit(solution)/shard_map/ppermute | solution.py:183
  30.2 0.2 convolution_add_fusion
  30.4 0.4 compare_reduce_fusion
  30.8 0.2 collective-permute-done.14
  30.9 1.9 %collective-permute-start.15 = (f32[1,3584]{1,0:T(1,128)S(1)}, f32[1,3584]{1,0:T(1,128)S(1)}, u32[]{:S(2)}, u32[]{:S(2)}) collective-permute-start(f32[1,3584]{1,0:T(1,128)S(1)} %add.64), channel_id=1, source_target_pairs={{0,3},{1,2},{2,1},{3,0},{4,7},{5,6},{6,5},{7,4},{8,11},{9,10},{10,... | collective-permute-start | bytes 43016 | tf_op jit(solution)/shard_map/ppermute | solution.py:183
  32.9 0.9 %select_reduce_fusion = (f32[128]{0:T(128)}, f32[128]{0:T(128)}, bf16[32,128]{1,0:T(8,128)(2,1)S(1)}) fusion(pred[16,128]{1,0:T(8,128)(4,1)S(1)} %compare_reduce_fusion, pred[16,128]{1,0:T(8,128)(4,1)S(1)} %get-tuple-element.89, f32[128]{0:T(128)S(1)} %copy-done.3, f32[16,128]{1,0:T(8,128)S(1)} %convolution_add_fusion, f32[8,128]{1,0:T(8,128)S(1)} %get-tuple-element.78, ...), kind=kOutput, calls=%fused_computation.20 | convolution fusion | flops 29425408 | bytes 1177600 | tf_op jit(solution)/shard_map/dot_general | solution.py:27
  33.9 0.5 %collective-permute-done.15 = f32[1,3584]{1,0:T(1,128)S(1)} collective-permute-done((f32[1,3584]{1,0:T(1,128)S(1)}, f32[1,3584]{1,0:T(1,128)S(1)}, u32[]{:S(2)}, u32[]{:S(2)}) %collective-permute-start.15) | collective-permute-done | bytes 14368 | tf_op jit(solution)/shard_map/ppermute | solution.py:183
  34.3 1.5 %collective-permute-start.16 = (f32[1,3584]{1,0:T(1,128)S(1)}, f32[1,3584]{1,0:T(1,128)S(1)}, u32[]{:S(2)}, u32[]{:S(2)}) collective-permute-start(f32[1,3584]{1,0:T(1,128)S(1)} %add.67), channel_id=1, source_target_pairs={{0,5},{1,4},{2,7},{3,6},{4,1},{5,0},{6,3},{7,2},{8,13},{9,12},{10,... | collective-permute-start | bytes 43016 | tf_op jit(solution)/shard_map/ppermute | solution.py:183
  35.8 1.3 %convolution_convert_fusion = bf16[128,3584]{1,0:T(8,128)(2,1)} fusion(bf16[32,3584]{1,0:T(8,128)(2,1)S(1)} %constant_dynamic-update-slice_fusion.2, f32[16,128]{1,0:T(8,128)S(1)} %convolution_add_fusion, f32[8,128]{1,0:T(8,128)S(1)} %get-tuple-element.78, f32[8,128]{1,0:T(8,128)S(1)} %get-tuple-element.77, pred[16,128]{1,0:T(8,128)(4,1)S(1)} %compare_reduce_fusion, ...), kind=kOutput, calls=%fused_computation | convolution fusion | flops 29851648 | bytes 1167360 | tf_op jit(solution)/shard_map/dot_general | solution.py:31
  37.2 0.1 shard_map.116
  37.3 0.2 collective-permute-done.16
  37.6 2.7 %collective-permute-start.17 = (f32[1,3584]{1,0:T(1,128)S(1)}, f32[1,3584]{1,0:T(1,128)S(1)}, u32[]{:S(2)}, u32[]{:S(2)}) collective-permute-start(f32[1,3584]{1,0:T(1,128)S(1)} %add.68), channel_id=1, source_target_pairs={{0,9},{1,8},{2,11},{3,10},{4,13},{5,12},{6,15},{7,14},{8,1},{9,0},... | collective-permute-start | bytes 43016 | tf_op jit(solution)/shard_map/ppermute | solution.py:183
  40.2 1.4 %convolution_convert_fusion.1 = bf16[3584,128]{1,0:T(8,128)(2,1)} fusion(bf16[32,128]{1,0:T(8,128)(2,1)S(1)} %select_convert_fusion.1, bf16[16,3584]{1,0:T(8,128)(2,1)S(1)} %get-tuple-element.92, bf16[16,3584]{1,0:T(8,128)(2,1)S(1)} %get-tuple-element.91), kind=kOutput, calls=%fused_computation.1 | convolution fusion | flops 30277632 | bytes 1155072 | tf_op jit(solution)/shard_map/dot_general | solution.py:31
  41.6 0.1 collective-permute-done.17
  41.7 0.7 %subtract_reduce_fusion.1 = f32[3584]{0:T(1024)} fusion(f32[1,3584]{1,0:T(1,128)S(1)} %shard_map.116, f32[1,3584]{1,0:T(1,128)S(1)} %add.68, f32[1,3584]{1,0:T(1,128)S(1)} %collective-permute-done.17), kind=kLoop, calls=%fused_computation.18 | loop fusion | flops 7168 | bytes 57344 | tf_op jit(solution)/shard_map/sub | solution.py:310
  (38 shorter events, 0.4 us)
Async XLA Ops:
  0.6 5.5 %collective-permute-start = (bf16[2,3584]{1,0:T(2,128)(2,1)}, bf16[2,3584]{1,0:T(2,128)(2,1)S(1)}, u32[]{:S(2)}, u32[]{:S(2)}) collective-permute-start(bf16[2,3584]{1,0:T(2,128)(2,1)} %refs_0_.1), channel_id=1, source_target_pairs={{0,9},{1,8},{2,11},{3,10},{4,13},{5,12},{6,15},{7,14},{8,1},{9,0},... | collective-permute-start | bytes 43016 | tf_op jit(solution)/shard_map/ppermute | solution.py:183
  4.2 7.6 %collective-permute-start.2 = (bf16[3584,128]{1,0:T(8,128)(2,1)}, bf16[3584,128]{1,0:T(8,128)(2,1)S(1)}, u32[]{:S(2)}, u32[]{:S(2)}) collective-permute-start(bf16[3584,128]{1,0:T(8,128)(2,1)} %encoder_far), channel_id=1, source_target_pairs={{0,1},{1,0},{2,3},{3,2},{4,5},{5,4},{6,7},{7,6},{8,9},{9,8},{10,11... | collective-permute-start | bytes 2752520 | tf_op jit(solution)/shard_map/ppermute | solution.py:183
  4.8 6.9 %collective-permute-start.4 = (bf16[128,3584]{1,0:T(8,128)(2,1)}, bf16[128,3584]{1,0:T(8,128)(2,1)S(1)}, u32[]{:S(2)}, u32[]{:S(2)}) collective-permute-start(bf16[128,3584]{1,0:T(8,128)(2,1)} %decoder_far), channel_id=1, source_target_pairs={{0,1},{1,0},{2,3},{3,2},{4,5},{5,4},{6,7},{7,6},{8,9},{9,8},{10,11... | collective-permute-start | bytes 2752520 | tf_op jit(solution)/shard_map/ppermute | solution.py:183
  4.9 6.9 %collective-permute-start.3 = (f32[1,128]{1,0:T(1,128)}, f32[1,128]{1,0:T(1,128)S(1)}, u32[]{:S(2)}, u32[]{:S(2)}) collective-permute-start(f32[1,128]{1,0:T(1,128)} %bitcast.7), channel_id=1, source_target_pairs={{0,1},{1,0},{2,3},{3,2},{4,5},{5,4},{6,7},{7,6},{8,9},{9,8},{10,11... | collective-permute-start | bytes 1544 | tf_op jit(solution)/shard_map/ppermute | solution.py:183
  6.2 3.4 %collective-permute-start.1 = (bf16[4,3584]{1,0:T(4,128)(2,1)S(1)}, bf16[4,3584]{1,0:T(4,128)(2,1)S(1)}, u32[]{:S(2)}, u32[]{:S(2)}) collective-permute-start(bf16[4,3584]{1,0:T(4,128)(2,1)S(1)} %maximum_select_fusion.1), channel_id=1, source_target_pairs={{0,5},{1,4},{2,7},{3,6},{4,1},{5,0},{6,3},{7,2},{8,13},{9,12},{10,... | collective-permute-start | bytes 86024 | tf_op jit(solution)/shard_map/ppermute | solution.py:183
  9.7 4.3 %collective-permute-start.5 = (bf16[8,3584]{1,0:T(8,128)(2,1)S(1)}, bf16[8,3584]{1,0:T(8,128)(2,1)S(1)}, u32[]{:S(2)}, u32[]{:S(2)}) collective-permute-start(bf16[8,3584]{1,0:T(8,128)(2,1)S(1)} %maximum_select_fusion.rows), channel_id=1, source_target_pairs={{0,3},{1,2},{2,1},{3,0},{4,7},{5,6},{6,5},{7,4},{8,11},{9,10},{10,... | collective-permute-start | bytes 172040 | tf_op jit(solution)/shard_map/ppermute | solution.py:183
  12.4 3.8 %collective-permute-start.7 = (bf16[8,3584]{1,0:T(8,128)(2,1)S(1)}, bf16[8,3584]{1,0:T(8,128)(2,1)S(1)}, u32[]{:S(2)}, u32[]{:S(2)}) collective-permute-start(bf16[8,3584]{1,0:T(8,128)(2,1)S(1)} %get-tuple-element.61), channel_id=1, source_target_pairs={{0,5},{1,4},{2,7},{3,6},{4,1},{5,0},{6,3},{7,2},{8,13},{9,12},{10,... | collective-permute-start | bytes 172040 | tf_op jit(solution)/shard_map/ppermute | solution.py:183
  14.7 4.3 %collective-permute-start.9 = (bf16[8,3584]{1,0:T(8,128)(2,1)S(1)}, bf16[8,3584]{1,0:T(8,128)(2,1)S(1)}, u32[]{:S(2)}, u32[]{:S(2)}) collective-permute-start(bf16[8,3584]{1,0:T(8,128)(2,1)S(1)} %get-tuple-element.63), channel_id=1, source_target_pairs={{0,5},{1,4},{2,7},{3,6},{4,1},{5,0},{6,3},{7,2},{8,13},{9,12},{10,... | collective-permute-start | bytes 172040 | tf_op jit(solution)/shard_map/ppermute | solution.py:183
  16.3 5.3 %collective-permute-start.8 = (bf16[8,3584]{1,0:T(8,128)(2,1)S(1)}, bf16[8,3584]{1,0:T(8,128)(2,1)S(1)}, u32[]{:S(2)}, u32[]{:S(2)}) collective-permute-start(bf16[8,3584]{1,0:T(8,128)(2,1)S(1)} %add.60), channel_id=1, source_target_pairs={{0,9},{1,8},{2,11},{3,10},{4,13},{5,12},{6,15},{7,14},{8,1},{9,0},... | collective-permute-start | bytes 172040 | tf_op jit(solution)/shard_map/ppermute | solution.py:183
  19.1 4.9 %collective-permute-start.10 = (bf16[8,3584]{1,0:T(8,128)(2,1)S(1)}, bf16[8,3584]{1,0:T(8,128)(2,1)S(1)}, u32[]{:S(2)}, u32[]{:S(2)}) collective-permute-start(bf16[8,3584]{1,0:T(8,128)(2,1)S(1)} %add.62), channel_id=1, source_target_pairs={{0,9},{1,8},{2,11},{3,10},{4,13},{5,12},{6,15},{7,14},{8,1},{9,0},... | collective-permute-start | bytes 172040 | tf_op jit(solution)/shard_map/ppermute | solution.py:183
  21.5 7.1 %collective-permute-start.12 = (bf16[8,3584]{1,0:T(8,128)(2,1)S(1)}, bf16[8,3584]{1,0:T(8,128)(2,1)S(1)}, u32[]{:S(2)}, u32[]{:S(2)}) collective-permute-start(bf16[8,3584]{1,0:T(8,128)(2,1)S(1)} %add.61.low), channel_id=1, source_target_pairs={{0,3},{1,2},{2,1},{3,0},{4,7},{5,6},{6,5},{7,4},{8,11},{9,10},{10,... | collective-permute-start | bytes 172040 | tf_op jit(solution)/shard_map/ppermute | solution.py:183
  24.0 4.7 %collective-permute-start.11 = (bf16[8,3584]{1,0:T(8,128)(2,1)S(1)}, bf16[8,3584]{1,0:T(8,128)(2,1)S(1)}, u32[]{:S(2)}, u32[]{:S(2)}) collective-permute-start(bf16[8,3584]{1,0:T(8,128)(2,1)S(1)} %add.63.high), channel_id=1, source_target_pairs={{0,3},{1,2},{2,1},{3,0},{4,7},{5,6},{6,5},{7,4},{8,11},{9,10},{10,... | collective-permute-start | bytes 172040 | tf_op jit(solution)/shard_map/ppermute | solution.py:183
  26.5 3.6 %collective-permute-start.6 = (bf16[16,3584]{1,0:T(8,128)(2,1)S(1)}, bf16[16,3584]{1,0:T(8,128)(2,1)S(1)}, u32[]{:S(2)}, u32[]{:S(2)}) collective-permute-start(bf16[16,3584]{1,0:T(8,128)(2,1)S(1)} %constant_dynamic-update-slice_fusion), channel_id=1, source_target_pairs={{0,1},{1,0},{2,3},{3,2},{4,5},{5,4},{6,7},{7,6},{8,9},{9,8},{10,11... | collective-permute-start | bytes 344072 | tf_op jit(solution)/shard_map/ppermute | solution.py:183
  28.7 1.5 %copy-start = (bf16[3584,128]{1,0:T(8,128)(2,1)S(1)}, bf16[3584,128]{1,0:T(8,128)(2,1)}, u32[]{:S(2)}) copy-start(bf16[3584,128]{1,0:T(8,128)(2,1)} %encoder_far) | copy-start | bytes 2752516
  28.7 1.5 %copy-start.2 = (f32[128]{0:T(128)S(1)}, f32[128]{0:T(128)}, u32[]{:S(2)}) copy-start(f32[128]{0:T(128)} %refs_2_.2) | copy-start | bytes 1540
  28.7 2.0 %copy-start.3 = (f32[128]{0:T(128)S(1)}, f32[128]{0:T(128)}, u32[]{:S(2)}) copy-start(f32[128]{0:T(128)} %param.11) | copy-start | bytes 1540
  29.4 3.5 %copy-start.1 = (bf16[128,3584]{1,0:T(8,128)(2,1)S(1)}, bf16[128,3584]{1,0:T(8,128)(2,1)}, u32[]{:S(2)}) copy-start(bf16[128,3584]{1,0:T(8,128)(2,1)} %decoder_far) | copy-start | bytes 2752516
  29.4 1.5 %collective-permute-start.13 = (bf16[16,3584]{1,0:T(8,128)(2,1)S(1)}, bf16[16,3584]{1,0:T(8,128)(2,1)S(1)}, u32[]{:S(2)}, u32[]{:S(2)}) collective-permute-start(bf16[16,3584]{1,0:T(8,128)(2,1)S(1)} %get-tuple-element.72.errors), channel_id=1, source_target_pairs={{0,1},{1,0},{2,3},{3,2},{4,5},{5,4},{6,7},{7,6},{8,9},{9,8},{10,11... | collective-permute-start | bytes 344072 | tf_op jit(solution)/shard_map/ppermute | solution.py:183
  29.7 1.3 %collective-permute-start.14 = (f32[1,3584]{1,0:T(1,128)S(1)}, f32[1,3584]{1,0:T(1,128)S(1)}, u32[]{:S(2)}, u32[]{:S(2)}) collective-permute-start(f32[1,3584]{1,0:T(1,128)S(1)} %get-tuple-element.75), channel_id=1, source_target_pairs={{0,1},{1,0},{2,3},{3,2},{4,5},{5,4},{6,7},{7,6},{8,9},{9,8},{10,11... | collective-permute-start | bytes 43016 | tf_op jit(solution)/shard_map/ppermute | solution.py:183
  30.9 3.4 %collective-permute-start.15 = (f32[1,3584]{1,0:T(1,128)S(1)}, f32[1,3584]{1,0:T(1,128)S(1)}, u32[]{:S(2)}, u32[]{:S(2)}) collective-permute-start(f32[1,3584]{1,0:T(1,128)S(1)} %add.64), channel_id=1, source_target_pairs={{0,3},{1,2},{2,1},{3,0},{4,7},{5,6},{6,5},{7,4},{8,11},{9,10},{10,... | collective-permute-start | bytes 43016 | tf_op jit(solution)/shard_map/ppermute | solution.py:183
  34.3 3.2 %collective-permute-start.16 = (f32[1,3584]{1,0:T(1,128)S(1)}, f32[1,3584]{1,0:T(1,128)S(1)}, u32[]{:S(2)}, u32[]{:S(2)}) collective-permute-start(f32[1,3584]{1,0:T(1,128)S(1)} %add.67), channel_id=1, source_target_pairs={{0,5},{1,4},{2,7},{3,6},{4,1},{5,0},{6,3},{7,2},{8,13},{9,12},{10,... | collective-permute-start | bytes 43016 | tf_op jit(solution)/shard_map/ppermute | solution.py:183
  37.6 4.1 %collective-permute-start.17 = (f32[1,3584]{1,0:T(1,128)S(1)}, f32[1,3584]{1,0:T(1,128)S(1)}, u32[]{:S(2)}, u32[]{:S(2)}) collective-permute-start(f32[1,3584]{1,0:T(1,128)S(1)} %add.68), channel_id=1, source_target_pairs={{0,9},{1,8},{2,11},{3,10},{4,13},{5,12},{6,15},{7,14},{8,1},{9,0},... | collective-permute-start | bytes 43016 | tf_op jit(solution)/shard_map/ppermute | solution.py:183

commit v9 on v8

--- a/solution.py
+++ b/solution.py
@@ -190,7 +190,6 @@
     gathering = hops[:0:-1] + hops[:1]
 
     encoder_other = swap(encoder_weight, 1)
-    decoder_other = swap(decoder_weight, 1)
     bias_other = swap(encoder_bias[None], 1)
 
     per_device, depth = rows_in.shape
@@ -205,6 +204,7 @@
         if bit == gathering[-2]:
             weights = (encoder_weight, decoder_weight, encoder_bias)
             block, weights = lax.optimization_barrier((block, weights))
+            decoder_other = swap(weights[1], 1)
         other = swap(rows_in if bit == gathering[0] else block, bit | 1)
         low = jnp.concatenate([block, other], axis=0)
         high = jnp.concatenate([other, block], axis=0)

time: 42.7 us -> 42.7 us (level)
  no operation moved by 1% of the time
where the time goes in v9:
time: 42.7 us; the launch traced here: 42.4 us
  starting transfers between devices  27.5 us (64%)
  Pallas kernels  6.24 us (15%)
  matrix products  3.89 us (9%)
  waiting for transfers between devices  2 us (5%)
  other arithmetic  1.81 us (4%)
  between operations  0.9 us (2%)
    ppermute x18, starting transfers between devices, swap(): return lax.ppermute(array, 'latent', [(i, i ^ bit) for i in range(count)])  27.5 us
    dot_general x2, matrix products, dot_rows(): lax.dot_general(a, b, (((0,), (0,)), ((), ())), preferred_element_type=F32)  2.73 us
    pallas_call x2, Pallas kernels, stage(): pl.pallas_call(stage_kernel, in_specs=[pl.BlockSpec(memory_space=pltpu.HB...  2.26 us
    pallas_call x4, Pallas kernels, near(): pl.pallas_call(kernel, in_specs=[whole] * len(arrays), out_specs=[whole]...  2.2 us
    ppermute x18, waiting for transfers between devices, swap(): return lax.ppermute(array, 'latent', [(i, i ^ bit) for i in range(count)])  2 us
    pallas_call x1, Pallas kernels, turn(): pl.pallas_call(turn_kernel, in_specs=[far, far, whole, whole], out_specs=...  1.79 us
    dot_general x1, matrix products, dot_last(): lax.dot_general(a, b, (((1,), (1,)), ((), ())), preferred_element_type=F32)  0.93 us
  transfers between devices with their start and end apart: 18, of which 7 were waited for; matrix products, arithmetic and copies ran while one was open for 12% of the time, Pallas kernels for 15%

profile of v9, /device:TPU:0, one launch (start us, length us, event | category | flops | bytes accessed | tf_op | source)
XLA Modules:
  0.0 42.4 jit_solution(12781077354150999147)
XLA Ops:
  0.6 3.5 %collective-permute-start = (bf16[2,3584]{1,0:T(2,128)(2,1)}, bf16[2,3584]{1,0:T(2,128)(2,1)S(1)}, u32[]{:S(2)}, u32[]{:S(2)}) collective-permute-start(bf16[2,3584]{1,0:T(2,128)(2,1)} %refs_0_.1), channel_id=1, source_target_pairs={{0,9},{1,8},{2,11},{3,10},{4,13},{5,12},{6,15},{7,14},{8,1},{9,0},... | collective-permute-start | bytes 43016 | tf_op jit(solution)/shard_map/ppermute | solution.py:183
  4.2 0.7 %collective-permute-start.2 = (bf16[3584,128]{1,0:T(8,128)(2,1)}, bf16[3584,128]{1,0:T(8,128)(2,1)S(1)}, u32[]{:S(2)}, u32[]{:S(2)}) collective-permute-start(bf16[3584,128]{1,0:T(8,128)(2,1)} %encoder_far), channel_id=1, source_target_pairs={{0,1},{1,0},{2,3},{3,2},{4,5},{5,4},{6,7},{7,6},{8,9},{9,8},{10,11... | collective-permute-start | bytes 2752520 | tf_op jit(solution)/shard_map/ppermute | solution.py:183
  4.9 0.8 %shard_map.110 = (bf16[2,3584]{1,0:T(2,128)(2,1)S(1)}, f32[1,3584]{1,0:T(1,128)S(1)}, s32[32,128]{1,0:T(8,128)S(1)}) custom-call(bf16[2,3584]{1,0:T(2,128)(2,1)} %refs_0_.1, f32[3584]{0:T(1024)} %refs_1_.1, s32[32,128]{1,0:T(8,128)} %refs_2_.1), custom_call_target="tpu_custom_call" | custom-call | bytes 90112 | tf_op jit(solution)/shard_map/pallas_call | solution.py:149
  5.6 0.2 collective-permute-done
  5.8 0.1 maximum_select_fusion.1
  5.9 1.9 %collective-permute-start.1 = (bf16[4,3584]{1,0:T(4,128)(2,1)S(1)}, bf16[4,3584]{1,0:T(4,128)(2,1)S(1)}, u32[]{:S(2)}, u32[]{:S(2)}) collective-permute-start(bf16[4,3584]{1,0:T(4,128)(2,1)S(1)} %maximum_select_fusion.1), channel_id=1, source_target_pairs={{0,5},{1,4},{2,7},{3,6},{4,1},{5,0},{6,3},{7,2},{8,13},{9,12},{10,... | collective-permute-start | bytes 86024 | tf_op jit(solution)/shard_map/ppermute | solution.py:183
  7.9 0.5 %collective-permute-start.4 = (bf16[128,3584]{1,0:T(8,128)(2,1)}, bf16[128,3584]{1,0:T(8,128)(2,1)S(1)}, u32[]{:S(2)}, u32[]{:S(2)}) collective-permute-start(bf16[128,3584]{1,0:T(8,128)(2,1)} %decoder_far), channel_id=1, source_target_pairs={{0,1},{1,0},{2,3},{3,2},{4,5},{5,4},{6,7},{7,6},{8,9},{9,8},{10,11... | collective-permute-start | bytes 2752520 | tf_op jit(solution)/shard_map/ppermute | solution.py:183
  8.3 1.5 %shard_map.111 = (bf16[3584,128]{1,0:T(8,128)(2,1)S(1)}, bf16[128,3584]{1,0:T(8,128)(2,1)S(1)}, f32[1,128]{1,0:T(1,128)S(1)}) custom-call(bf16[3584,128]{1,0:T(8,128)(2,1)} %encoder_far, bf16[128,3584]{1,0:T(8,128)(2,1)} %decoder_far, f32[128]{0:T(128)} %refs_2_.2), custom_call_target="tpu_custom_call" | custom-call | bytes 3671040 | tf_op jit(solution)/shard_map/pallas_call | solution.py:149
  9.8 0.1 maximum_select_fusion.rows
  10.0 1.3 %collective-permute-start.5 = (bf16[8,3584]{1,0:T(8,128)(2,1)S(1)}, bf16[8,3584]{1,0:T(8,128)(2,1)S(1)}, u32[]{:S(2)}, u32[]{:S(2)}) collective-permute-start(bf16[8,3584]{1,0:T(8,128)(2,1)S(1)} %maximum_select_fusion.rows), channel_id=1, source_target_pairs={{0,3},{1,2},{2,1},{3,0},{4,7},{5,6},{6,5},{7,4},{8,11},{9,10},{10,... | collective-permute-start | bytes 172040 | tf_op jit(solution)/shard_map/ppermute | solution.py:183
  11.3 0.4 compare_reduce_fusion.2
  11.7 0.0 collective-permute-done.2.encoder_other
  11.7 0.0 collective-permute-done.4.decoder_other
  11.7 0.7 %shard_map.112 = (f32[8,128]{1,0:T(8,128)S(1)}, bf16[8,3584]{1,0:T(8,128)(2,1)S(1)}) custom-call(bf16[8,3584]{1,0:T(8,128)(2,1)S(1)} %maximum_select_fusion.rows, f32[1,3584]{1,0:T(1,128)S(1)} %get-tuple-element.56.decoder_bias, f32[8,256]{1,0:T(8,128)S(1)} %get-tuple-element.94.gates, bf16[3584,128]{1,0:T(8,128)(2,1)S(1)} %get-tuple-element.58.encoder, ...), custom_call_target="tpu_custom_call" | custom-call | bytes 3750912 | tf_op jit(solution)/shard_map/pallas_call | solution.py:162
  12.4 1.6 %collective-permute-start.7 = (bf16[8,3584]{1,0:T(8,128)(2,1)S(1)}, bf16[8,3584]{1,0:T(8,128)(2,1)S(1)}, u32[]{:S(2)}, u32[]{:S(2)}) collective-permute-start(bf16[8,3584]{1,0:T(8,128)(2,1)S(1)} %get-tuple-element.61), channel_id=1, source_target_pairs={{0,5},{1,4},{2,7},{3,6},{4,1},{5,0},{6,3},{7,2},{8,13},{9,12},{10,... | collective-permute-start | bytes 172040 | tf_op jit(solution)/shard_map/ppermute | solution.py:183
  14.1 0.7 %shard_map.113 = (f32[8,128]{1,0:T(8,128)S(1)}, bf16[8,3584]{1,0:T(8,128)(2,1)S(1)}) custom-call(bf16[8,3584]{1,0:T(8,128)(2,1)S(1)} %collective-permute-done.5.rows.rows_far, f32[1,3584]{1,0:T(1,128)S(1)} %get-tuple-element.56.decoder_bias, f32[8,256]{1,0:T(8,128)S(1)} %get-tuple-element.93.gates.gates_far, ...), custom_call_target="tpu_custom_call" | custom-call | bytes 3750912 | tf_op jit(solution)/shard_map/pallas_call | solution.py:162
  14.7 1.2 %collective-permute-start.9 = (bf16[8,3584]{1,0:T(8,128)(2,1)S(1)}, bf16[8,3584]{1,0:T(8,128)(2,1)S(1)}, u32[]{:S(2)}, u32[]{:S(2)}) collective-permute-start(bf16[8,3584]{1,0:T(8,128)(2,1)S(1)} %get-tuple-element.63), channel_id=1, source_target_pairs={{0,5},{1,4},{2,7},{3,6},{4,1},{5,0},{6,3},{7,2},{8,13},{9,12},{10,... | collective-permute-start | bytes 172040 | tf_op jit(solution)/shard_map/ppermute | solution.py:183
  16.0 0.3 collective-permute-done.7
  16.3 2.9 %collective-permute-start.8 = (bf16[8,3584]{1,0:T(8,128)(2,1)S(1)}, bf16[8,3584]{1,0:T(8,128)(2,1)S(1)}, u32[]{:S(2)}, u32[]{:S(2)}) collective-permute-start(bf16[8,3584]{1,0:T(8,128)(2,1)S(1)} %add.60), channel_id=1, source_target_pairs={{0,9},{1,8},{2,11},{3,10},{4,13},{5,12},{6,15},{7,14},{8,1},{9,0},... | collective-permute-start | bytes 172040 | tf_op jit(solution)/shard_map/ppermute | solution.py:183
  19.1 0.0 collective-permute-done.9
  19.2 2.4 %collective-permute-start.10 = (bf16[8,3584]{1,0:T(8,128)(2,1)S(1)}, bf16[8,3584]{1,0:T(8,128)(2,1)S(1)}, u32[]{:S(2)}, u32[]{:S(2)}) collective-permute-start(bf16[8,3584]{1,0:T(8,128)(2,1)S(1)} %add.62), channel_id=1, source_target_pairs={{0,9},{1,8},{2,11},{3,10},{4,13},{5,12},{6,15},{7,14},{8,1},{9,0},... | collective-permute-start | bytes 172040 | tf_op jit(solution)/shard_map/ppermute | solution.py:183
  21.5 0.0 collective-permute-done.8
  21.5 2.2 %collective-permute-start.12 = (bf16[8,3584]{1,0:T(8,128)(2,1)S(1)}, bf16[8,3584]{1,0:T(8,128)(2,1)S(1)}, u32[]{:S(2)}, u32[]{:S(2)}) collective-permute-start(bf16[8,3584]{1,0:T(8,128)(2,1)S(1)} %add.61.low), channel_id=1, source_target_pairs={{0,3},{1,2},{2,1},{3,0},{4,7},{5,6},{6,5},{7,4},{8,11},{9,10},{10,... | collective-permute-start | bytes 172040 | tf_op jit(solution)/shard_map/ppermute | solution.py:183
  23.8 0.2 collective-permute-done.10
  24.0 2.5 %collective-permute-start.11 = (bf16[8,3584]{1,0:T(8,128)(2,1)S(1)}, bf16[8,3584]{1,0:T(8,128)(2,1)S(1)}, u32[]{:S(2)}, u32[]{:S(2)}) collective-permute-start(bf16[8,3584]{1,0:T(8,128)(2,1)S(1)} %add.63.high), channel_id=1, source_target_pairs={{0,3},{1,2},{2,1},{3,0},{4,7},{5,6},{6,5},{7,4},{8,11},{9,10},{10,... | collective-permute-start | bytes 172040 | tf_op jit(solution)/shard_map/ppermute | solution.py:183
  26.5 0.4 collective-permute-start.6
  26.9 1.8 %shard_map.114 = (bf16[256,3584]{1,0:T(8,128)(2,1)S(1)}, bf16[3584,256]{1,0:T(8,128)(2,1)S(1)}) custom-call(bf16[3584,128]{1,0:T(8,128)(2,1)} %encoder_far, bf16[128,3584]{1,0:T(8,128)(2,1)} %decoder_far, bf16[3584,128]{1,0:T(8,128)(2,1)S(1)} %collective-permute-done.2.encoder_other, bf16[128,3584]{1,0:T(8,128)(2,1)S(1)} %collective-permute-done.4.decoder_other), custom_call_target="tpu_custom_call" | custom-call | bytes 7340032 | tf_op jit(solution)/shard_map/pallas_call | solution.py:104
  28.7 0.0 collective-permute-done.12.high_received
  28.7 0.0 copy-start
  28.7 0.0 copy-start.2
  28.7 0.0 copy-start.3
  28.7 0.7 %shard_map.115 = (bf16[16,3584]{1,0:T(8,128)(2,1)S(1)}, f32[1,3584]{1,0:T(1,128)S(1)}) custom-call(bf16[8,3584]{1,0:T(8,128)(2,1)S(1)} %add.61.low, bf16[8,3584]{1,0:T(8,128)(2,1)S(1)} %collective-permute-done.11.low_received, bf16[8,3584]{1,0:T(8,128)(2,1)S(1)} %maximum_select_fusion.rows, f32[8,256]{1,0:T(8,128)S(1)} %get-tuple-element.94.gates, ...), custom_call_target="tpu_custom_call" | custom-call | bytes 4044800 | tf_op jit(solution)/shard_map/pallas_call | solution.py:162
  29.4 0.4 %collective-permute-start.13 = (bf16[16,3584]{1,0:T(8,128)(2,1)S(1)}, bf16[16,3584]{1,0:T(8,128)(2,1)S(1)}, u32[]{:S(2)}, u32[]{:S(2)}) collective-permute-start(bf16[16,3584]{1,0:T(8,128)(2,1)S(1)} %get-tuple-element.72.errors), channel_id=1, source_target_pairs={{0,1},{1,0},{2,3},{3,2},{4,5},{5,4},{6,7},{7,6},{8,9},{9,8},{10,11... | collective-permute-start | bytes 344072 | tf_op jit(solution)/shard_map/ppermute | solution.py:183
  29.9 0.2 collective-permute-start.14
  30.2 0.2 convolution_add_fusion
  30.4 0.4 compare_reduce_fusion
  30.8 0.4 collective-permute-done.14
  31.2 1.7 %collective-permute-start.15 = (f32[1,3584]{1,0:T(1,128)S(1)}, f32[1,3584]{1,0:T(1,128)S(1)}, u32[]{:S(2)}, u32[]{:S(2)}) collective-permute-start(f32[1,3584]{1,0:T(1,128)S(1)} %add.64), channel_id=1, source_target_pairs={{0,3},{1,2},{2,1},{3,0},{4,7},{5,6},{6,5},{7,4},{8,11},{9,10},{10,... | collective-permute-start | bytes 43016 | tf_op jit(solution)/shard_map/ppermute | solution.py:183
  32.9 0.9 %select_reduce_fusion = (f32[128]{0:T(128)}, f32[128]{0:T(128)}, bf16[32,128]{1,0:T(8,128)(2,1)S(1)}) fusion(pred[16,128]{1,0:T(8,128)(4,1)S(1)} %compare_reduce_fusion, pred[16,128]{1,0:T(8,128)(4,1)S(1)} %get-tuple-element.89, f32[128]{0:T(128)S(1)} %copy-done.3, f32[16,128]{1,0:T(8,128)S(1)} %convolution_add_fusion, f32[8,128]{1,0:T(8,128)S(1)} %get-tuple-element.78, ...), kind=kOutput, calls=%fused_computation.20 | convolution fusion | flops 29425408 | bytes 1177600 | tf_op jit(solution)/shard_map/dot_general | solution.py:27
  33.9 0.5 %collective-permute-done.15 = f32[1,3584]{1,0:T(1,128)S(1)} collective-permute-done((f32[1,3584]{1,0:T(1,128)S(1)}, f32[1,3584]{1,0:T(1,128)S(1)}, u32[]{:S(2)}, u32[]{:S(2)}) %collective-permute-start.15) | collective-permute-done | bytes 14368 | tf_op jit(solution)/shard_map/ppermute | solution.py:183
  34.4 1.4 %collective-permute-start.16 = (f32[1,3584]{1,0:T(1,128)S(1)}, f32[1,3584]{1,0:T(1,128)S(1)}, u32[]{:S(2)}, u32[]{:S(2)}) collective-permute-start(f32[1,3584]{1,0:T(1,128)S(1)} %add.67), channel_id=1, source_target_pairs={{0,5},{1,4},{2,7},{3,6},{4,1},{5,0},{6,3},{7,2},{8,13},{9,12},{10,... | collective-permute-start | bytes 43016 | tf_op jit(solution)/shard_map/ppermute | solution.py:183
  35.8 1.3 %convolution_convert_fusion = bf16[128,3584]{1,0:T(8,128)(2,1)} fusion(bf16[32,3584]{1,0:T(8,128)(2,1)S(1)} %constant_dynamic-update-slice_fusion.2, f32[16,128]{1,0:T(8,128)S(1)} %convolution_add_fusion, f32[8,128]{1,0:T(8,128)S(1)} %get-tuple-element.78, f32[8,128]{1,0:T(8,128)S(1)} %get-tuple-element.77, pred[16,128]{1,0:T(8,128)(4,1)S(1)} %compare_reduce_fusion, ...), kind=kOutput, calls=%fused_computation | convolution fusion | flops 29851648 | bytes 1167360 | tf_op jit(solution)/shard_map/dot_general | solution.py:31
  37.2 0.1 shard_map.116
  37.3 0.3 collective-permute-done.16
  37.6 2.6 %collective-permute-start.17 = (f32[1,3584]{1,0:T(1,128)S(1)}, f32[1,3584]{1,0:T(1,128)S(1)}, u32[]{:S(2)}, u32[]{:S(2)}) collective-permute-start(f32[1,3584]{1,0:T(1,128)S(1)} %add.68), channel_id=1, source_target_pairs={{0,9},{1,8},{2,11},{3,10},{4,13},{5,12},{6,15},{7,14},{8,1},{9,0},... | collective-permute-start | bytes 43016 | tf_op jit(solution)/shard_map/ppermute | solution.py:183
  40.2 1.4 %convolution_convert_fusion.1 = bf16[3584,128]{1,0:T(8,128)(2,1)} fusion(bf16[32,128]{1,0:T(8,128)(2,1)S(1)} %select_convert_fusion.1, bf16[16,3584]{1,0:T(8,128)(2,1)S(1)} %get-tuple-element.92, bf16[16,3584]{1,0:T(8,128)(2,1)S(1)} %get-tuple-element.91), kind=kOutput, calls=%fused_computation.1 | convolution fusion | flops 30277632 | bytes 1155072 | tf_op jit(solution)/shard_map/dot_general | solution.py:31
  41.6 0.1 collective-permute-done.17
  41.7 0.7 %subtract_reduce_fusion.1 = f32[3584]{0:T(1024)} fusion(f32[1,3584]{1,0:T(1,128)S(1)} %shard_map.116, f32[1,3584]{1,0:T(1,128)S(1)} %add.68, f32[1,3584]{1,0:T(1,128)S(1)} %collective-permute-done.17), kind=kLoop, calls=%fused_computation.18 | loop fusion | flops 7168 | bytes 57344 | tf_op jit(solution)/shard_map/sub | solution.py:310
  (38 shorter events, 0.4 us)
Async XLA Ops:
  0.6 5.2 %collective-permute-start = (bf16[2,3584]{1,0:T(2,128)(2,1)}, bf16[2,3584]{1,0:T(2,128)(2,1)S(1)}, u32[]{:S(2)}, u32[]{:S(2)}) collective-permute-start(bf16[2,3584]{1,0:T(2,128)(2,1)} %refs_0_.1), channel_id=1, source_target_pairs={{0,9},{1,8},{2,11},{3,10},{4,13},{5,12},{6,15},{7,14},{8,1},{9,0},... | collective-permute-start | bytes 43016 | tf_op jit(solution)/shard_map/ppermute | solution.py:183
  4.2 7.6 %collective-permute-start.2 = (bf16[3584,128]{1,0:T(8,128)(2,1)}, bf16[3584,128]{1,0:T(8,128)(2,1)S(1)}, u32[]{:S(2)}, u32[]{:S(2)}) collective-permute-start(bf16[3584,128]{1,0:T(8,128)(2,1)} %encoder_far), channel_id=1, source_target_pairs={{0,1},{1,0},{2,3},{3,2},{4,5},{5,4},{6,7},{7,6},{8,9},{9,8},{10,11... | collective-permute-start | bytes 2752520 | tf_op jit(solution)/shard_map/ppermute | solution.py:183
  4.8 6.9 %collective-permute-start.3 = (f32[1,128]{1,0:T(1,128)}, f32[1,128]{1,0:T(1,128)S(1)}, u32[]{:S(2)}, u32[]{:S(2)}) collective-permute-start(f32[1,128]{1,0:T(1,128)} %bitcast.7), channel_id=1, source_target_pairs={{0,1},{1,0},{2,3},{3,2},{4,5},{5,4},{6,7},{7,6},{8,9},{9,8},{10,11... | collective-permute-start | bytes 1544 | tf_op jit(solution)/shard_map/ppermute | solution.py:183
  5.9 3.9 %collective-permute-start.1 = (bf16[4,3584]{1,0:T(4,128)(2,1)S(1)}, bf16[4,3584]{1,0:T(4,128)(2,1)S(1)}, u32[]{:S(2)}, u32[]{:S(2)}) collective-permute-start(bf16[4,3584]{1,0:T(4,128)(2,1)S(1)} %maximum_select_fusion.1), channel_id=1, source_target_pairs={{0,5},{1,4},{2,7},{3,6},{4,1},{5,0},{6,3},{7,2},{8,13},{9,12},{10,... | collective-permute-start | bytes 86024 | tf_op jit(solution)/shard_map/ppermute | solution.py:183
  7.9 3.9 %collective-permute-start.4 = (bf16[128,3584]{1,0:T(8,128)(2,1)}, bf16[128,3584]{1,0:T(8,128)(2,1)S(1)}, u32[]{:S(2)}, u32[]{:S(2)}) collective-permute-start(bf16[128,3584]{1,0:T(8,128)(2,1)} %decoder_far), channel_id=1, source_target_pairs={{0,1},{1,0},{2,3},{3,2},{4,5},{5,4},{6,7},{7,6},{8,9},{9,8},{10,11... | collective-permute-start | bytes 2752520 | tf_op jit(solution)/shard_map/ppermute | solution.py:183
  10.0 4.1 %collective-permute-start.5 = (bf16[8,3584]{1,0:T(8,128)(2,1)S(1)}, bf16[8,3584]{1,0:T(8,128)(2,1)S(1)}, u32[]{:S(2)}, u32[]{:S(2)}) collective-permute-start(bf16[8,3584]{1,0:T(8,128)(2,1)S(1)} %maximum_select_fusion.rows), channel_id=1, source_target_pairs={{0,3},{1,2},{2,1},{3,0},{4,7},{5,6},{6,5},{7,4},{8,11},{9,10},{10,... | collective-permute-start | bytes 172040 | tf_op jit(solution)/shard_map/ppermute | solution.py:183
  12.4 3.8 %collective-permute-start.7 = (bf16[8,3584]{1,0:T(8,128)(2,1)S(1)}, bf16[8,3584]{1,0:T(8,128)(2,1)S(1)}, u32[]{:S(2)}, u32[]{:S(2)}) collective-permute-start(bf16[8,3584]{1,0:T(8,128)(2,1)S(1)} %get-tuple-element.61), channel_id=1, source_target_pairs={{0,5},{1,4},{2,7},{3,6},{4,1},{5,0},{6,3},{7,2},{8,13},{9,12},{10,... | collective-permute-start | bytes 172040 | tf_op jit(solution)/shard_map/ppermute | solution.py:183
  14.7 4.4 %collective-permute-start.9 = (bf16[8,3584]{1,0:T(8,128)(2,1)S(1)}, bf16[8,3584]{1,0:T(8,128)(2,1)S(1)}, u32[]{:S(2)}, u32[]{:S(2)}) collective-permute-start(bf16[8,3584]{1,0:T(8,128)(2,1)S(1)} %get-tuple-element.63), channel_id=1, source_target_pairs={{0,5},{1,4},{2,7},{3,6},{4,1},{5,0},{6,3},{7,2},{8,13},{9,12},{10,... | collective-permute-start | bytes 172040 | tf_op jit(solution)/shard_map/ppermute | solution.py:183
  16.3 5.3 %collective-permute-start.8 = (bf16[8,3584]{1,0:T(8,128)(2,1)S(1)}, bf16[8,3584]{1,0:T(8,128)(2,1)S(1)}, u32[]{:S(2)}, u32[]{:S(2)}) collective-permute-start(bf16[8,3584]{1,0:T(8,128)(2,1)S(1)} %add.60), channel_id=1, source_target_pairs={{0,9},{1,8},{2,11},{3,10},{4,13},{5,12},{6,15},{7,14},{8,1},{9,0},... | collective-permute-start | bytes 172040 | tf_op jit(solution)/shard_map/ppermute | solution.py:183
  19.2 4.8 %collective-permute-start.10 = (bf16[8,3584]{1,0:T(8,128)(2,1)S(1)}, bf16[8,3584]{1,0:T(8,128)(2,1)S(1)}, u32[]{:S(2)}, u32[]{:S(2)}) collective-permute-start(bf16[8,3584]{1,0:T(8,128)(2,1)S(1)} %add.62), channel_id=1, source_target_pairs={{0,9},{1,8},{2,11},{3,10},{4,13},{5,12},{6,15},{7,14},{8,1},{9,0},... | collective-permute-start | bytes 172040 | tf_op jit(solution)/shard_map/ppermute | solution.py:183
  21.5 7.1 %collective-permute-start.12 = (bf16[8,3584]{1,0:T(8,128)(2,1)S(1)}, bf16[8,3584]{1,0:T(8,128)(2,1)S(1)}, u32[]{:S(2)}, u32[]{:S(2)}) collective-permute-start(bf16[8,3584]{1,0:T(8,128)(2,1)S(1)} %add.61.low), channel_id=1, source_target_pairs={{0,3},{1,2},{2,1},{3,0},{4,7},{5,6},{6,5},{7,4},{8,11},{9,10},{10,... | collective-permute-start | bytes 172040 | tf_op jit(solution)/shard_map/ppermute | solution.py:183
  24.0 4.6 %collective-permute-start.11 = (bf16[8,3584]{1,0:T(8,128)(2,1)S(1)}, bf16[8,3584]{1,0:T(8,128)(2,1)S(1)}, u32[]{:S(2)}, u32[]{:S(2)}) collective-permute-start(bf16[8,3584]{1,0:T(8,128)(2,1)S(1)} %add.63.high), channel_id=1, source_target_pairs={{0,3},{1,2},{2,1},{3,0},{4,7},{5,6},{6,5},{7,4},{8,11},{9,10},{10,... | collective-permute-start | bytes 172040 | tf_op jit(solution)/shard_map/ppermute | solution.py:183
  26.5 3.6 %collective-permute-start.6 = (bf16[16,3584]{1,0:T(8,128)(2,1)S(1)}, bf16[16,3584]{1,0:T(8,128)(2,1)S(1)}, u32[]{:S(2)}, u32[]{:S(2)}) collective-permute-start(bf16[16,3584]{1,0:T(8,128)(2,1)S(1)} %constant_dynamic-update-slice_fusion), channel_id=1, source_target_pairs={{0,1},{1,0},{2,3},{3,2},{4,5},{5,4},{6,7},{7,6},{8,9},{9,8},{10,11... | collective-permute-start | bytes 344072 | tf_op jit(solution)/shard_map/ppermute | solution.py:183
  28.7 1.5 %copy-start = (bf16[3584,128]{1,0:T(8,128)(2,1)S(1)}, bf16[3584,128]{1,0:T(8,128)(2,1)}, u32[]{:S(2)}) copy-start(bf16[3584,128]{1,0:T(8,128)(2,1)} %encoder_far) | copy-start | bytes 2752516
  28.7 1.5 %copy-start.2 = (f32[128]{0:T(128)S(1)}, f32[128]{0:T(128)}, u32[]{:S(2)}) copy-start(f32[128]{0:T(128)} %refs_2_.2) | copy-start | bytes 1540
  28.7 2.0 %copy-start.3 = (f32[128]{0:T(128)S(1)}, f32[128]{0:T(128)}, u32[]{:S(2)}) copy-start(f32[128]{0:T(128)} %param.11) | copy-start | bytes 1540
  29.4 3.5 %copy-start.1 = (bf16[128,3584]{1,0:T(8,128)(2,1)S(1)}, bf16[128,3584]{1,0:T(8,128)(2,1)}, u32[]{:S(2)}) copy-start(bf16[128,3584]{1,0:T(8,128)(2,1)} %decoder_far) | copy-start | bytes 2752516
  29.4 1.7 %collective-permute-start.13 = (bf16[16,3584]{1,0:T(8,128)(2,1)S(1)}, bf16[16,3584]{1,0:T(8,128)(2,1)S(1)}, u32[]{:S(2)}, u32[]{:S(2)}) collective-permute-start(bf16[16,3584]{1,0:T(8,128)(2,1)S(1)} %get-tuple-element.72.errors), channel_id=1, source_target_pairs={{0,1},{1,0},{2,3},{3,2},{4,5},{5,4},{6,7},{7,6},{8,9},{9,8},{10,11... | collective-permute-start | bytes 344072 | tf_op jit(solution)/shard_map/ppermute | solution.py:183
  29.9 1.2 %collective-permute-start.14 = (f32[1,3584]{1,0:T(1,128)S(1)}, f32[1,3584]{1,0:T(1,128)S(1)}, u32[]{:S(2)}, u32[]{:S(2)}) collective-permute-start(f32[1,3584]{1,0:T(1,128)S(1)} %get-tuple-element.75), channel_id=1, source_target_pairs={{0,1},{1,0},{2,3},{3,2},{4,5},{5,4},{6,7},{7,6},{8,9},{9,8},{10,11... | collective-permute-start | bytes 43016 | tf_op jit(solution)/shard_map/ppermute | solution.py:183
  31.2 3.2 %collective-permute-start.15 = (f32[1,3584]{1,0:T(1,128)S(1)}, f32[1,3584]{1,0:T(1,128)S(1)}, u32[]{:S(2)}, u32[]{:S(2)}) collective-permute-start(f32[1,3584]{1,0:T(1,128)S(1)} %add.64), channel_id=1, source_target_pairs={{0,3},{1,2},{2,1},{3,0},{4,7},{5,6},{6,5},{7,4},{8,11},{9,10},{10,... | collective-permute-start | bytes 43016 | tf_op jit(solution)/shard_map/ppermute | solution.py:183
  34.4 3.2 %collective-permute-start.16 = (f32[1,3584]{1,0:T(1,128)S(1)}, f32[1,3584]{1,0:T(1,128)S(1)}, u32[]{:S(2)}, u32[]{:S(2)}) collective-permute-start(f32[1,3584]{1,0:T(1,128)S(1)} %add.67), channel_id=1, source_target_pairs={{0,5},{1,4},{2,7},{3,6},{4,1},{5,0},{6,3},{7,2},{8,13},{9,12},{10,... | collective-permute-start | bytes 43016 | tf_op jit(solution)/shard_map/ppermute | solution.py:183
  37.6 4.1 %collective-permute-start.17 = (f32[1,3584]{1,0:T(1,128)S(1)}, f32[1,3584]{1,0:T(1,128)S(1)}, u32[]{:S(2)}, u32[]{:S(2)}) collective-permute-start(f32[1,3584]{1,0:T(1,128)S(1)} %add.68), channel_id=1, source_target_pairs={{0,9},{1,8},{2,11},{3,10},{4,13},{5,12},{6,15},{7,14},{8,1},{9,0},... | collective-permute-start | bytes 43016 | tf_op jit(solution)/shard_map/ppermute | solution.py:183
